TPU v7x, 256 devices: a whole 4x4x8 slice. The times are simulated.
256 devices in a mesh: gx: 8 (over z_lo, core), gy: 32 (over z_hi, x, y).
Axes of the slice: x: 4, y: 4, z: 8 (z_hi: 2, z_lo: 4; z = z_hi * 4 + z_lo), core: 2. Of those that a mesh axis runs over, the one named last changes fastest.
Arguments:
- positions: float32 [3, 131072], P(None, ('gx', 'gy')), may hold values from 0 to 1
- species: int32 [131072], P(('gx', 'gy')), may hold values from 0 to 7, as said below
- neighbours: int32 [131072, 32], P(('gx', 'gy')), may hold values from -1 to 2815, as said below
- ghost_index: int32 [65536], P(('gx', 'gy')), may hold values from 0 to 511, as said below
- wave_index: int32 [3, 4096], replicated, may hold values from -32 to 31, as said below
- embedding: float32 [8, 128], replicated, may hold values from -6 to 6
- radial_weight: float32 [8, 256], replicated, may hold values from -2 to 2
- message_weight: float32 [128, 128], replicated, may hold values from -0.5 to 0.5
- scalar_weight: float32 [128, 128], replicated, may hold values from -0.5 to 0.5
- vector_weight: float32 [128, 128], replicated, may hold values from -0.25 to 0.25
- readout_hidden: float32 [128, 128], replicated, may hold values from -0.5 to 0.5
- readout_vector: float32 [128], replicated, may hold values from -0.5 to 0.5
- charge_weight: float32 [128, 32], replicated, may hold values from -0.5 to 0.5
Outputs:
- forces: float32 [3, 131072], P(None, ('gx', 'gy'))
- atom_energy: float32 [131072], P(('gx', 'gy'))
Inputs may be any that keep to these rules, and one draw needn't show every extreme that they name: Each atom's species. Within each domain, atoms are more often of the lower half of the species the higher the domain number d is. `ghost_index`: within each domain's block, 256 different local atom indices. `neighbours`: entries below 512 are the domain's own atoms, never the atom itself; an entry 512 + 256 b + g is entry g of the b-th received boundary block, b = 3 i + j, never b = 4; -1 pads the slots after the live ones; each row has 16 to 32 live slots, the first atom of every domain 32. `wave_index`: the 4096 columns are distinct integer vectors; row 0 lies in -8 to 8, row 1 in -32 to 31, row 2 in 1 to 4.
All inputs are finite; a program needn't handle non-finite values.
Results may differ from a plain program's by a relative error of at most 0.0003.
Values sent between devices are 32-bit elements; how exact they have to be, the bound alone decides.
No kernel may reach another device: no remote copies, remote signals or barrier semaphores. Data moves between devices by JAX's collectives and lax.ppermute only.
A program may use at most 128 MiB of HBM per device.

v0:
```python
import jax
import jax.numpy as jnp
from jax import lax
from jax.sharding import PartitionSpec as P

NB = 8
NS = 8


HIGHEST = lax.Precision.HIGHEST
TWO_PI = 6.283185307179586
BOX_HEIGHT = 4.0
SPLITTING = 2.5
SOFTENING = 0.01
CENTRE_STEP = 0.3


def shifted(array, axis, by):
    devices = lax.axis_size(axis)
    return lax.ppermute(array, axis, [(i, (i + by) % devices) for i in range(devices)])


def extended(cells, sides, width):
    for axis, dim in sides:
        count = lax.axis_size(axis)
        head = lax.slice_in_dim(cells, 0, width, axis=dim)
        tail = lax.slice_in_dim(cells, cells.shape[dim] - width, cells.shape[dim], axis=dim)
        cells = jnp.concatenate(
            [
                lax.ppermute(tail, axis, [(i, (i + 1) % count) for i in range(count)]),
                cells,
                lax.ppermute(head, axis, [((i + 1) % count, i) for i in range(count)]),
            ],
            axis=dim,
        )
    return cells


def short_range(
    own_pos,
    table_pos,
    one_hot,
    neighbours,
    embedding,
    radial_weight,
    message_weight,
    scalar_weight,
    vector_weight,
    readout_hidden,
    readout_vector,
    charge_weight,
):
    atom_count = own_pos.shape[1]
    channels = embedding.shape[1]
    feature_table = jnp.dot(one_hot, embedding, precision=HIGHEST)
    own_features = feature_table[:atom_count]
    message_table = jnp.dot(feature_table, message_weight, precision=HIGHEST)
    live_mask = (neighbours >= 0).astype(jnp.float32)
    safe_index = jnp.maximum(neighbours, 0)
    neighbour_message = message_table[safe_index] * live_mask[:, :, None]
    offsets = table_pos[:, safe_index] - own_pos[:, :, None]
    distance_sq = jnp.sum(offsets * offsets, axis=0)
    distance = jnp.sqrt(distance_sq + SOFTENING)
    direction = offsets / distance
    centres = CENTRE_STEP * jnp.arange(NB, dtype=jnp.float32)
    radial_basis = (
        jnp.exp(-((distance[:, :, None] - centres) ** 2) / (2.0 * CENTRE_STEP**2))
        * jnp.exp(-0.25 * distance_sq)[:, :, None]
    )
    filters = jnp.einsum("akn,nf->akf", radial_basis, radial_weight, precision=HIGHEST)
    scalar_sum = jnp.sum(filters[:, :, :channels] * neighbour_message, axis=1)
    vector_sum = jnp.einsum(
        "xak,akc->xac", direction, filters[:, :, channels:] * neighbour_message, precision=HIGHEST
    )
    vector_norm = jnp.sum(vector_sum * vector_sum, axis=0)
    update = jnp.dot(scalar_sum, scalar_weight, precision=HIGHEST) + jnp.dot(
        vector_norm, vector_weight, precision=HIGHEST
    )
    hidden = own_features + jax.nn.silu(update)
    energy = jnp.dot(
        jax.nn.silu(jnp.dot(hidden, readout_hidden, precision=HIGHEST)),
        readout_vector,
        precision=HIGHEST,
    )
    charges = jnp.dot(hidden, charge_weight, precision=HIGHEST)
    return (energy, charges)


def wave_vectors(wave_index, box_first, box_second):
    extent = jnp.array([box_first, box_second, BOX_HEIGHT], dtype=jnp.float32)
    vectors = TWO_PI * wave_index.astype(jnp.float32) / extent[:, None]
    squared = jnp.sum(vectors * vectors, axis=0)
    green_weight = jnp.exp(-squared / (4.0 * SPLITTING**2)) / squared
    return (vectors, green_weight)


def phases(global_pos, vectors):
    angles = (
        global_pos[0][:, None] * vectors[0]
        + global_pos[1][:, None] * vectors[1]
        + global_pos[2][:, None] * vectors[2]
    )
    return (jnp.cos(angles), jnp.sin(angles))


def send_back_columns_first(blocks):
    column_sum = blocks[:, 1]
    for column_step in (-1, 1):
        column_sum = column_sum + shifted(blocks[:, 1 + column_step], "gy", column_step)
    total_sum = column_sum[1]
    for row_step in (-1, 1):
        total_sum = total_sum + shifted(column_sum[1 + row_step], "gx", row_step)
    return total_sum


def shards(
    positions,
    species,
    neighbours,
    ghost_index,
    wave_index,
    embedding,
    radial_weight,
    message_weight,
    scalar_weight,
    vector_weight,
    readout_hidden,
    readout_vector,
    charge_weight,
):
    atom_count = positions.shape[1]
    border_count = ghost_index.shape[0]
    grid_first = lax.axis_size("gx")
    grid_second = lax.axis_size("gy")
    atoms_all = atom_count * grid_first * grid_second
    border = jnp.concatenate(
        [positions[:, ghost_index], species[ghost_index].astype(jnp.float32)[None]], axis=0
    )
    received = extended(border[None, None], (("gx", 0), ("gy", 1)), 1)
    steps_row = jnp.arange(3, dtype=jnp.float32) - 1.0
    shift_grid = jnp.stack(
        [
            jnp.broadcast_to(steps_row[:, None], (3, 3)),
            jnp.broadcast_to(steps_row[None, :], (3, 3)),
            jnp.zeros((3, 3), jnp.float32),
        ],
        axis=2,
    )
    ghost_pos = (
        (received[:, :, :3, :] + shift_grid[:, :, :, None])
        .transpose(2, 0, 1, 3)
        .reshape(3, 9 * border_count)
    )
    ghost_species = received[:, :, 3, :].reshape(9 * border_count)
    species_kinds = jnp.arange(NS, dtype=jnp.int32)
    one_hot = jnp.concatenate(
        [
            (species[:, None] == species_kinds).astype(jnp.float32),
            (ghost_species[:, None] == species_kinds.astype(jnp.float32)).astype(jnp.float32),
        ],
        axis=0,
    )

    def local_model(own_pos, far_pos):
        table_pos = jnp.concatenate([own_pos, far_pos], axis=1)
        return short_range(
            own_pos,
            table_pos,
            one_hot,
            neighbours,
            embedding,
            radial_weight,
            message_weight,
            scalar_weight,
            vector_weight,
            readout_hidden,
            readout_vector,
            charge_weight,
        )

    (energy, charges), pullback = jax.vjp(local_model, positions, ghost_pos)
    vectors, green_weight = wave_vectors(wave_index, grid_first, grid_second)
    anchor = jnp.stack(
        [
            lax.axis_index("gx").astype(jnp.float32),
            lax.axis_index("gy").astype(jnp.float32),
            jnp.zeros((), jnp.float32),
        ]
    )
    global_pos = positions + anchor[:, None]
    cosines, sine_terms = phases(global_pos, vectors)
    unit_cos_part = jnp.sum(cosines, axis=0)
    unit_sin_part = jnp.sum(sine_terms, axis=0)
    totals = lax.psum(jnp.sum(charges, axis=0), ("gx", "gy"))
    mean_charge = totals / atoms_all
    neutral = charges - mean_charge
    cos_part = jnp.einsum("aq,ak->qk", neutral, cosines, precision=HIGHEST)
    sin_part = jnp.einsum("aq,ak->qk", neutral, sine_terms, precision=HIGHEST)
    structure_cos, structure_sin, unit_cos, unit_sin = lax.psum(
        (cos_part, sin_part, unit_cos_part, unit_sin_part), ("gx", "gy")
    )
    weighted_cos = green_weight * structure_cos
    weighted_sin = green_weight * structure_sin
    potential = (
        jnp.dot(cosines, weighted_cos.T, precision=HIGHEST)
        + jnp.dot(sine_terms, weighted_sin.T, precision=HIGHEST)
    ) / atoms_all
    site_energy = energy + jnp.sum(neutral * potential, axis=1)
    potential_mean = (
        (
            jnp.dot(weighted_cos, unit_cos, precision=HIGHEST)
            + jnp.dot(weighted_sin, unit_sin, precision=HIGHEST)
        )
        / atoms_all
        / atoms_all
    )
    charge_cotangent = 2.0 * (potential - potential_mean)
    angle_cotangent = (
        2.0
        / atoms_all
        * (
            cosines * jnp.dot(neutral, weighted_sin, precision=HIGHEST)
            - sine_terms * jnp.dot(neutral, weighted_cos, precision=HIGHEST)
        )
    )
    ewald_gradient = jnp.einsum("xk,ak->xa", vectors, angle_cotangent, precision=HIGHEST)
    own_gradient, ghost_gradient = pullback((jnp.ones_like(energy), charge_cotangent))
    blocks = ghost_gradient.reshape(3, 3, 3, border_count).transpose(1, 2, 0, 3)
    returned = send_back_columns_first(blocks)
    gradient = (own_gradient + ewald_gradient).at[:, ghost_index].add(returned)
    return (-gradient, site_energy)


def solution(mesh):
    return jax.shard_map(
        shards,
        mesh=mesh,
        in_specs=(
            P(None, ("gx", "gy")),
            P(("gx", "gy")),
            P(("gx", "gy"), None),
            P(("gx", "gy")),
            P(),
            P(),
            P(),
            P(),
            P(),
            P(),
            P(),
            P(),
            P(),
        ),
        out_specs=(P(None, ("gx", "gy")), P(("gx", "gy"))),
        check_vma=False,
    )
```

profile of v0, /device:TPU:0, one launch (start us, length us, event | category | flops | bytes accessed | tf_op | source)
XLA Modules:
  0.0 971.5 jit_solution(6807633248202084861)
XLA Ops:
  11.6 2.4 collective-permute-start.1
  19.9 33.6 %fusion.19 = (f32[4096]{0:T(1024)}, f32[4096]{0:T(1024)}) fusion(f32[4096]{0:T(1024)S(1)} %bitcast.135, f32[512]{0:T(512)S(1)} %bitcast.155, f32[4096]{0:T(1024)S(1)} %bitcast.141, f32[512]{0:T(512)S(1)} %bitcast.161, f32[4096]{0:T(1024)S(1)} %bitcast.129, f32[512]{0:T(512)S(1)} %bitcast.149), kind=kLoop, calls=%fused_computation.26 | loop fusion | flops 14671872 | bytes 88064 | tf_op jit(solution)/shard_map/reduce_sum | solution.py:193
  54.2 9.2 collective-permute-start.3
  63.4 11.7 %collective-permute-start.2 = (f32[3,1,4,256]{3,2,1,0:T(4,128)S(1)}, f32[3,1,4,256]{3,2,1,0:T(4,128)S(1)}, u32[]{:S(2)}, u32[]{:S(2)}) collective-permute-start(f32[3,1,4,256]{3,2,1,0:T(4,128)S(1)} %pad_maximum_fusion.2), channel_id=1, source_target_pairs={{0,1},{1,2},{2,3},{3,4},{4,5},{5,6},{6,7},{7,8},{8,9},{9,10},{10,1... | collective-permute-start | bytes 36872 | tf_op jit(solution)/shard_map/ppermute | solution.py:30
  75.1 11.8 %collective-permute-done.2 = f32[3,1,4,256]{3,2,1,0:T(4,128)S(1)} collective-permute-done((f32[3,1,4,256]{3,2,1,0:T(4,128)S(1)}, f32[3,1,4,256]{3,2,1,0:T(4,128)S(1)}, u32[]{:S(2)}, u32[]{:S(2)}) %collective-permute-start.2) | collective-permute-done | bytes 12320 | tf_op jit(solution)/shard_map/ppermute | solution.py:30
  91.4 54.8 %gather_fusion.3 = f32[16384,128]{1,0:T(8,128)} fusion(f32[2816,128]{1,0:T(8,128)S(1)} %fusion.163, s32[16384]{0:T(1024)S(1)} %broadcast_clamp_fusion), kind=kCustom, calls=%fused_computation.3 | custom fusion | bytes 16842752 | tf_op jit(solution)/shard_map/jvp()/gather | solution.py:60
  146.2 54.8 %gather_fusion.2 = f32[16384,3]{1,0:T(8,128)} fusion(f32[3,2816]{0,1:T(8,128)S(1)} %copy.92, s32[16384]{0:T(1024)S(1)} %broadcast_clamp_fusion), kind=kCustom, calls=%fused_computation.2 | custom fusion | bytes 458752 | tf_op jit(solution)/shard_map/jvp()/gather | solution.py:61
  201.0 5.9 copy.94
  206.9 2.8 multiply_reduce_fusion.1
  210.0 14.4 %fusion.82 = f32[512,32,256]{2,0,1:T(8,128)S(1)} fusion(f32[512,32]{0,1:T(8,128)S(1)} %get-tuple-element.34, f32[8]{0:T(128)S(1)} %copy-done.47, f32[512,32]{0,1:T(8,128)S(1)} %get-tuple-element.35, f32[8,256]{1,0:T(8,128)S(1)} %copy-done.27), kind=kOutput, calls=%fused_computation.94 | convolution fusion | flops 403308544 | bytes 16916512 | tf_op jit(solution)/shard_map/jvp(akn,nf->akf)/dot_general | solution.py:70
  224.4 8.6 slice_multiply_fusion.1
  233.5 2.8 copy-done.2
  236.3 14.0 %multiply_reduce_fusion = (f32[512,128]{1,0:T(8,128)S(1)}, f32[512,128,3]{1,2,0:T(4,128)}) fusion(f32[512,32,3]{1,2,0:T(4,128)S(1)} %copy.94, f32[512,32]{1,0:T(8,128)S(1)} %copy.99, f32[3,512]{0,1:T(8,128)S(1)} %copy.89, f32[512,32,128]{2,0,1:T(8,128)S(1)} %get-tuple-element.25), kind=kOutput, calls=%fused_computation.80 | convolution fusion | flops 75923456 | bytes 9705472 | tf_op jit(solution)/shard_map/jvp(xak,akc->xac)/dot_general | solution.py:72
  252.8 73.1 %all-reduce.2 = (f32[32]{0:T(128)S(1)}, f32[4096]{0:T(1024)}, f32[4096]{0:T(1024)}) all-reduce(f32[32]{0:T(128)S(1)} %get-tuple-element.46, f32[4096]{0:T(1024)S(1)} %copy-done.31, f32[4096]{0:T(1024)S(1)} %copy-done.30), channel_id=1, replica_groups=mesh['gx'=8,'gy'=32] {'gx','gy'}, use_global_device_ids=true, to_apply=%region_5.6 | all-reduce | flops 8224 | bytes 65792 | tf_op jit(solution)/shard_map/psum | solution.py:194
  325.9 34.4 %fusion.22 = f32[32,4096]{1,0:T(8,128)} fusion(f32[4096]{0:T(1024)S(1)} %bitcast.136, f32[512]{0:T(512)S(1)} %bitcast.157, f32[4096]{0:T(1024)S(1)} %bitcast.142, f32[512]{0:T(512)S(1)} %bitcast.163, f32[4096]{0:T(1024)S(1)} %bitcast.130, f32[512]{0:T(512)S(1)} %bitcast.151, f32[512,32]{0,1:T(8,128)S(1)} %get-tuple-element.47, f32[32]{0:T(128)S(1)} %broadcast_multiply_fusion), kind=kOutput, calls=%fused_computation.28 | convolution fusion | flops 815808512 | bytes 645248 | tf_op jit(solution)/shard_map/aq,ak->qk/dot_general | solution.py:198
  360.4 33.6 %fusion.16 = f32[32,4096]{1,0:T(8,128)} fusion(f32[4096]{0:T(1024)S(1)} %bitcast.137, f32[512]{0:T(512)S(1)} %bitcast.158, f32[4096]{0:T(1024)S(1)} %bitcast.143, f32[512]{0:T(512)S(1)} %bitcast.164, f32[4096]{0:T(1024)S(1)} %bitcast.131, f32[512]{0:T(512)S(1)} %bitcast.152, f32[512,32]{0,1:T(8,128)S(1)} %get-tuple-element.47, f32[32]{0:T(128)S(1)} %broadcast_multiply_fusion), kind=kOutput, calls=%fused_computation.25 | convolution fusion | flops 815808512 | bytes 645248 | tf_op jit(solution)/shard_map/aq,ak->qk/dot_general | solution.py:197
  396.4 250.7 %all-reduce.6.cloned.1.call-done = (f32[32,4096]{1,0:T(8,128)}, f32[32,4096]{1,0:T(8,128)}) async-done(((f32[32,4096]{1,0:T(8,128)}, f32[32,4096]{1,0:T(8,128)}), (f32[32,4096]{1,0:T(8,128)}, f32[32,4096]{1,0:T(8,128)})) %all-reduce.6.cloned.1.call-update) | async-done | bytes 1048592 | tf_op jit(solution)/shard_map/psum | solution.py:199
  649.8 35.7 %fusion.14 = f32[512,32]{0,1:T(8,128)S(1)} fusion(f32[4096]{0:T(1024)} %bitcast.138, f32[512]{0:T(512)} %bitcast.156, f32[4096]{0:T(1024)} %bitcast.144, f32[512]{0:T(512)} %bitcast.162, f32[4096]{0:T(1024)S(1)} %bitcast.132, f32[512]{0:T(512)} %bitcast.150, f32[32,4096]{1,0:T(8,128)S(1)} %fusion.197), kind=kOutput, calls=%fused_computation.24 | convolution fusion | flops 815792128 | bytes 645120 | tf_op jit(solution)/shard_map/dot_general | solution.py:205
  686.2 36.0 %multiply_reduce_fusion.2 = (f32[512]{0:T(512)}, f32[512,32]{0,1:T(8,128)S(1)}) fusion(f32[512,32]{0,1:T(8,128)S(1)} %get-tuple-element.47, f32[32]{0:T(128)S(1)} %copy-done.45, f32[512,32]{0,1:T(8,128)S(1)} %fusion.14, f32[4096]{0:T(1024)S(1)} %bitcast.139, f32[512]{0:T(512)S(1)} %bitcast.159, f32[4096]{0:T(1024)S(1)} %bitcast.145, f32[512]{0:T(512)S(1)} %bitcast.165, ...), kind=kOutput, calls=%fused_computation.152 | convolution fusion | flops 815873536 | bytes 778368 | tf_op jit(solution)/shard_map/dot_general | solution.py:206
  724.2 9.1 fusion.91
  733.3 9.1 fusion.95
  742.4 16.4 %fusion.72 = f32[512,32,128]{2,1,0:T(8,128)} fusion(f32[512,128,3]{1,2,0:T(4,128)S(1)} %copy-done.6, f32[512,128]{1,0:T(8,128)S(1)} %fusion.166, f32[512,32,3]{1,2,0:T(4,128)S(1)} %copy.94, f32[512,32]{1,0:T(8,128)S(1)} %copy.99, f32[3,512]{0,1:T(8,128)S(1)} %copy.89), kind=kOutput, calls=%fused_computation.82 | convolution fusion | flops 75988992 | bytes 9705472 | tf_op jit(solution)/shard_map/transpose(jvp(xak,akc->xac))/dot_general | solution.py:72
  758.9 17.7 %fusion.71 = (f32[512,32]{1,0:T(8,128)}, f32[512,3,32]{2,1,0:T(4,128)S(1)}) fusion(f32[512,32,3]{1,2,0:T(4,128)S(1)} %copy.94, f32[512,32]{1,0:T(8,128)S(1)} %copy-done.7, f32[3,512]{0,1:T(8,128)S(1)} %copy.89, f32[512,32,128]{2,0,1:T(8,128)S(1)} %bitcast.120, f32[512,128,3]{1,2,0:T(4,128)S(1)} %copy-done.6, f32[512,128]{1,0:T(8,128)S(1)} %fusion.166), kind=kOutput, calls=%fused_computation.77 | convolution fusion | flops 76070912 | bytes 9967616 | tf_op jit(solution)/shard_map/transpose(jvp(xak,akc->xac))/dot_general | solution.py:72
  777.6 15.7 %copy_multiply_fusion = (f32[512,32,128]{2,0,1:T(8,128)S(1)}, f32[512,32,128]{2,0,1:T(8,128)S(1)}) fusion(f32[512,32,128]{2,1,0:T(8,128)} %fusion.72, f32[512,32,128]{2,1,0:T(8,128)} %bitcast.118, f32[512,32]{0,1:T(8,128)S(1)} %compare_convert_fusion, f32[512,128]{1,0:T(8,128)S(1)} %fusion.167), kind=kLoop, calls=%fused_computation.13 | loop fusion | flops 6291456 | bytes 33882112 | tf_op jit(solution)/shard_map/transpose(jvp())/mul | solution.py:73
  793.3 14.2 %fusion.84 = (f32[512,32]{0,1:T(8,128)S(1)}, f32[512,32]{0,1:T(8,128)S(1)}) fusion(f32[8]{0:T(128)S(1)} %copy-done.48, f32[512,32]{0,1:T(8,128)S(1)} %get-tuple-element.35, f32[512,32]{0,1:T(8,128)S(1)} %get-tuple-element.34, f32[8,256]{1,0:T(8,128)S(1)} %copy-done.28, f32[512,32,128]{2,0,1:T(8,128)S(1)} %get-tuple-element.28, ...), kind=kOutput, calls=%fused_computation.95 | convolution fusion | flops 408518656 | bytes 17047584 | tf_op jit(solution)/shard_map/transpose(jvp(akn,nf->akf))/dot_general | solution.py:70
  807.7 2.7 fusion.159
  810.4 6.5 copy.116
  817.0 88.3 %scatter_custom_fusion = f32[3,2816]{0,1:T(8,128)S(1)} fusion(s32[16384]{0:T(1024)} %copy-done.12, f32[16384,3]{1,0:T(8,128)} %bitcast.122, f32[]{:T(128)} %constant.24.clone.1), kind=kCustom, calls=%fused_computation.85 | custom fusion | flops 49152 | bytes 34304 | tf_op jit(solution)/shard_map/transpose(jvp())/scatter-add | solution.py:61
  906.4 7.3 collective-permute-start.4
  913.8 34.7 %fusion.199 = f32[512,4096]{1,0:T(8,128)} fusion(f32[512,4096]{1,0:T(8,128)} %fusion.95, f32[512,4096]{1,0:T(8,128)} %fusion.91, f32[4096]{0:T(1024)S(1)} %bitcast.140, f32[512]{0:T(512)S(1)} %bitcast.160, f32[4096]{0:T(1024)S(1)} %bitcast.146, f32[512]{0:T(512)S(1)} %bitcast.166, f32[4096]{0:T(1024)S(1)} %bitcast.134, f32[512]{0:T(512)S(1)} %bitcast.154), kind=kLoop, calls=%fused_computation.16.clone.clone.clone.1 | loop fusion | flops 18874368 | bytes 25221120 | tf_op jit(solution)/shard_map/xk,ak->xa/dot_general | solution.py:226
  951.1 9.4 fusion.66
  961.3 2.2 scatter_custom_fusion.1
  (197 shorter events, 32.3 us)
Async XLA Ops:
  7.2 83.0 %copy-start = (f32[128,128]{1,0:T(8,128)S(1)}, f32[128,128]{1,0:T(8,128)}, u32[]{:S(2)}) copy-start(f32[128,128]{1,0:T(8,128)} %param.21) | copy-start | bytes 196612
  7.2 79.9 %copy-start.16 = (f32[3,512]{1,0:T(4,128)S(1)}, f32[3,512]{1,0:T(4,128)}, u32[]{:S(2)}) copy-start(f32[3,512]{1,0:T(4,128)} %param.14) | copy-start | bytes 18436
  7.2 80.5 %copy-start.49 = (f32[8,128]{1,0:T(8,128)S(1)}, f32[8,128]{1,0:T(8,128)}, u32[]{:S(2)}) copy-start(f32[8,128]{1,0:T(8,128)} %param.19) | copy-start | bytes 12292
  7.2 639.9 %all-reduce.6.cloned.1.call-start = ((), (), s32[]{:S(2)}) async-start(), calls=%async_computation | async-start | bytes 2097152 | tf_op jit(solution)/shard_map/psum | solution.py:199
  11.6 42.5 %collective-permute-start.1 = (f32[1,1,4,256]{3,2,1,0:T(4,128)S(1)}, f32[1,1,4,256]{3,2,1,0:T(4,128)S(1)}, u32[]{:S(2)}, u32[]{:S(2)}) collective-permute-start(f32[1,1,4,256]{3,2,1,0:T(4,128)S(1)} %maximum_bitcast_fusion), channel_id=1, source_target_pairs={{32,0},{64,32},{96,64},{128,96},{160,128},{192,160},{224,192},{0,2... | collective-permute-start | bytes 12296 | tf_op jit(solution)/shard_map/ppermute | solution.py:32
  14.0 40.1 %collective-permute-start = (f32[1,1,4,256]{3,2,1,0:T(4,128)S(1)}, f32[1,1,4,256]{3,2,1,0:T(4,128)S(1)}, u32[]{:S(2)}, u32[]{:S(2)}) collective-permute-start(f32[1,1,4,256]{3,2,1,0:T(4,128)S(1)} %maximum_bitcast_fusion), channel_id=1, source_target_pairs={{0,32},{32,64},{64,96},{96,128},{128,160},{160,192},{192,224},{224... | collective-permute-start | bytes 12296 | tf_op jit(solution)/shard_map/ppermute | solution.py:30
  17.3 69.7 %copy-start.36 = (f32[1,512]{1,0:T(1,128)}, f32[1,512]{1,0:T(1,128)S(1)}, u32[]{:S(2)}) copy-start(f32[1,512]{1,0:T(1,128)S(1)} %get-tuple-element.40) | copy-start | bytes 6148
  17.3 69.7 %copy-start.32 = (f32[1,512]{1,0:T(1,128)}, f32[1,512]{1,0:T(1,128)S(1)}, u32[]{:S(2)}) copy-start(f32[1,512]{1,0:T(1,128)S(1)} %get-tuple-element.39) | copy-start | bytes 6148
  18.9 341.5 %copy-start.17 = (f32[1,4096]{1,0:T(1,128)}, f32[1,4096]{1,0:T(1,128)S(1)}, u32[]{:S(2)}) copy-start(f32[1,4096]{1,0:T(1,128)S(1)} %get-tuple-element.37) | copy-start | bytes 49156
  18.9 341.5 %copy-start.20 = (f32[1,4096]{1,0:T(1,128)}, f32[1,4096]{1,0:T(1,128)S(1)}, u32[]{:S(2)}) copy-start(f32[1,4096]{1,0:T(1,128)S(1)} %get-tuple-element.38) | copy-start | bytes 49156
  19.6 126.6 %copy-start.12 = (s32[16384]{0:T(1024)}, s32[16384]{0:T(1024)S(1)}, u32[]{:S(2)}) copy-start(s32[16384]{0:T(1024)S(1)} %reshape.95) | copy-start | bytes 196612
  54.2 20.9 %collective-permute-start.3 = (f32[3,1,4,256]{3,2,1,0:T(4,128)S(1)}, f32[3,1,4,256]{3,2,1,0:T(4,128)S(1)}, u32[]{:S(2)}, u32[]{:S(2)}) collective-permute-start(f32[3,1,4,256]{3,2,1,0:T(4,128)S(1)} %pad_maximum_fusion.2), channel_id=1, source_target_pairs={{1,0},{2,1},{3,2},{4,3},{5,4},{6,5},{7,6},{8,7},{9,8},{10,9},{11,1... | collective-permute-start | bytes 36872 | tf_op jit(solution)/shard_map/ppermute | solution.py:32
  63.4 23.5 %collective-permute-start.2 = (f32[3,1,4,256]{3,2,1,0:T(4,128)S(1)}, f32[3,1,4,256]{3,2,1,0:T(4,128)S(1)}, u32[]{:S(2)}, u32[]{:S(2)}) collective-permute-start(f32[3,1,4,256]{3,2,1,0:T(4,128)S(1)} %pad_maximum_fusion.2), channel_id=1, source_target_pairs={{0,1},{1,2},{2,3},{3,4},{4,5},{5,6},{6,7},{7,8},{8,9},{9,10},{10,1... | collective-permute-start | bytes 36872 | tf_op jit(solution)/shard_map/ppermute | solution.py:30
  233.1 92.8 %copy-start.33 = (f32[1,512]{1,0:T(1,128)S(1)}, f32[1,512]{1,0:T(1,128)}, u32[]{:S(2)}) copy-start(f32[1,512]{1,0:T(1,128)} %copy-done.32) | copy-start | bytes 6148
  233.1 92.8 %copy-start.37 = (f32[1,512]{1,0:T(1,128)S(1)}, f32[1,512]{1,0:T(1,128)}, u32[]{:S(2)}) copy-start(f32[1,512]{1,0:T(1,128)} %copy-done.36) | copy-start | bytes 6148
  233.1 92.8 %copy-start.41 = (f32[1,512]{1,0:T(1,128)S(1)}, f32[1,512]{1,0:T(1,128)}, u32[]{:S(2)}) copy-start(f32[1,512]{1,0:T(1,128)} %copy-done.40) | copy-start | bytes 6148
  395.3 290.3 %copy-start.29 = (f32[4096]{0:T(1024)S(1)}, f32[4096]{0:T(1024)}, u32[]{:S(2)}) copy-start(f32[4096]{0:T(1024)} %get-tuple-element.18) | copy-start | bytes 49156
  395.3 290.8 %copy-start.18 = (f32[1,4096]{1,0:T(1,128)S(1)}, f32[1,4096]{1,0:T(1,128)}, u32[]{:S(2)}) copy-start(f32[1,4096]{1,0:T(1,128)} %copy-done.17) | copy-start | bytes 49156
  395.3 290.8 %copy-start.21 = (f32[1,4096]{1,0:T(1,128)S(1)}, f32[1,4096]{1,0:T(1,128)}, u32[]{:S(2)}) copy-start(f32[1,4096]{1,0:T(1,128)} %copy-done.20) | copy-start | bytes 49156
  395.3 290.8 %copy-start.34 = (f32[1,512]{1,0:T(1,128)S(1)}, f32[1,512]{1,0:T(1,128)}, u32[]{:S(2)}) copy-start(f32[1,512]{1,0:T(1,128)} %copy-done.32) | copy-start | bytes 6148
  395.3 290.8 %copy-start.38 = (f32[1,512]{1,0:T(1,128)S(1)}, f32[1,512]{1,0:T(1,128)}, u32[]{:S(2)}) copy-start(f32[1,512]{1,0:T(1,128)} %copy-done.36) | copy-start | bytes 6148
  395.4 290.8 %copy-start.42 = (f32[1,512]{1,0:T(1,128)S(1)}, f32[1,512]{1,0:T(1,128)}, u32[]{:S(2)}) copy-start(f32[1,512]{1,0:T(1,128)} %copy-done.40) | copy-start | bytes 6148
  395.4 290.8 %copy-start.45 = (f32[32]{0:T(128)S(1)}, f32[32]{0:T(128)}, u32[]{:S(2)}) copy-start(f32[32]{0:T(128)} %copy-done.44) | copy-start | bytes 388
  810.4 103.4 %copy-start.19 = (f32[1,4096]{1,0:T(1,128)S(1)}, f32[1,4096]{1,0:T(1,128)}, u32[]{:S(2)}) copy-start(f32[1,4096]{1,0:T(1,128)} %copy-done.17) | copy-start | bytes 49156
  810.4 103.4 %copy-start.22 = (f32[1,4096]{1,0:T(1,128)S(1)}, f32[1,4096]{1,0:T(1,128)}, u32[]{:S(2)}) copy-start(f32[1,4096]{1,0:T(1,128)} %copy-done.20) | copy-start | bytes 49156
  810.4 103.4 %copy-start.35 = (f32[1,512]{1,0:T(1,128)S(1)}, f32[1,512]{1,0:T(1,128)}, u32[]{:S(2)}) copy-start(f32[1,512]{1,0:T(1,128)} %copy-done.32) | copy-start | bytes 6148
  810.4 103.4 %copy-start.39 = (f32[1,512]{1,0:T(1,128)S(1)}, f32[1,512]{1,0:T(1,128)}, u32[]{:S(2)}) copy-start(f32[1,512]{1,0:T(1,128)} %copy-done.36) | copy-start | bytes 6148
  810.4 103.4 %copy-start.43 = (f32[1,512]{1,0:T(1,128)S(1)}, f32[1,512]{1,0:T(1,128)}, u32[]{:S(2)}) copy-start(f32[1,512]{1,0:T(1,128)} %copy-done.40) | copy-start | bytes 6148
  906.4 42.4 %collective-permute-start.4 = (f32[3,3,256]{1,2,0:T(8,128)}, f32[3,3,256]{1,2,0:T(8,128)}, u32[]{:S(2)}, u32[]{:S(2)}) collective-permute-start(f32[3,3,256]{1,2,0:T(8,128)} %get-tuple-element.29), channel_id=1, source_target_pairs={{0,31},{1,0},{2,1},{3,2},{4,3},{5,4},{6,5},{7,6},{8,7},{9,8},{10,9... | collective-permute-start | bytes 27656 | tf_op jit(solution)/shard_map/ppermute | solution.py:20
  913.8 35.0 %collective-permute-start.5 = (f32[3,3,256]{1,2,0:T(8,128)}, f32[3,3,256]{1,2,0:T(8,128)}, u32[]{:S(2)}, u32[]{:S(2)}) collective-permute-start(f32[3,3,256]{1,2,0:T(8,128)} %get-tuple-element.30), channel_id=1, source_target_pairs={{0,1},{1,2},{2,3},{3,4},{4,5},{5,6},{6,7},{7,8},{8,9},{9,10},{10,1... | collective-permute-start | bytes 27656 | tf_op jit(solution)/shard_map/ppermute | solution.py:20
  950.0 11.3 %collective-permute-start.6 = (f32[3,256]{0,1:T(8,128)S(1)}, f32[3,256]{0,1:T(8,128)S(1)}, u32[]{:S(2)}, u32[]{:S(2)}) collective-permute-start(f32[3,256]{0,1:T(8,128)S(1)} %get-tuple-element.31), channel_id=1, source_target_pairs={{0,224},{32,0},{64,32},{96,64},{128,96},{160,128},{192,160},{224,1... | collective-permute-start | bytes 9224 | tf_op jit(solution)/shard_map/ppermute | solution.py:20
  951.1 10.2 %collective-permute-start.7 = (f32[3,256]{0,1:T(8,128)S(1)}, f32[3,256]{0,1:T(8,128)S(1)}, u32[]{:S(2)}, u32[]{:S(2)}) collective-permute-start(f32[3,256]{0,1:T(8,128)S(1)} %get-tuple-element.32), channel_id=1, source_target_pairs={{0,32},{32,64},{64,96},{96,128},{128,160},{160,192},{192,224},{224... | collective-permute-start | bytes 9224 | tf_op jit(solution)/shard_map/ppermute | solution.py:20
  (34 other events, 971.9 us)
Sparse Core Ops, SparseCore 0:
  394.2 252.8 all-reduce.5
where the time goes:
time: 983 us; the launch traced here: 972 us
  waiting for transfers between devices  263 us (27%)
  matrix products  255 us (26%)
  other arithmetic  198 us (20%)
  local copies, waits for them, and re-layouts  136 us (14%)
  blocking collectives  73.1 us (7%)
  starting transfers between devices  31.8 us (3%)
  between operations  15.5 us (2%)
    psum x1, waiting for transfers between devices, shards(): lax.psum((cos_part, sin_part, unit_cos_part, unit_sin_part), ('gx', 'gy'))  251 us
    scatter-add x1, other arithmetic, short_range(): offsets = table_pos[:, safe_index] - own_pos[:, :, None]  88.3 us
    psum x1, blocking collectives, shards(): totals = lax.psum(jnp.sum(charges, axis=0), ('gx', 'gy'))  73.1 us
    gather x2, local copies, waits for them, and re-layouts, short_range(): offsets = table_pos[:, safe_index] - own_pos[:, :, None]  60.7 us
    gather x1, local copies, waits for them, and re-layouts, short_range(): neighbour_message = message_table[safe_index] * live_mask[:, :, None]  54.8 us
    dot_general x3, matrix products, short_range(): jnp.einsum('xak,akc->xac', direction, filters[:, :, channels:] * neighbou...  48.1 us
    dot_general x1, matrix products, shards(): jnp.dot(sine_terms, weighted_sin.T, precision=HIGHEST)  36 us
    dot_general x1, matrix products, shards(): jnp.dot(cosines, weighted_cos.T, precision=HIGHEST)  35.7 us
  transfers between devices with their start and end apart: 9, of which 2 were waited for; matrix products, arithmetic and copies ran while one was open for 9% of the time, Pallas kernels for 0%

commit v1 on v0

v1 whole, which is shorter than its diff:
```python
import functools

import jax
import jax.numpy as jnp
from jax import lax
from jax.experimental import pallas as pl
from jax.experimental.pallas import tpu as pltpu
from jax.sharding import PartitionSpec as P

NB = 8
NS = 8
HIGHEST = lax.Precision.HIGHEST
TWO_PI = 6.283185307179586
BOX_HEIGHT = 4.0
SPLITTING = 2.5
SOFTENING = 0.01
CENTRE_STEP = 0.3
AXES = ("gx", "gy")

HX = 9
LZ = 4
NY = 32
XF = 2 * HX - 1
PAIRS = XF * LZ
PROWS = 72
ROWS = 2304
UNIT_ROW = PAIRS * 32
TOTAL_ROW = UNIT_ROW + PROWS
CHUNK = 72

F32 = jnp.float32
BF16 = jnp.bfloat16
NT = (((1,), (1,)), ((), ()))
NN = (((1,), (0,)), ((), ()))


def mm(a, b, dims=NN, precision=None):
    return lax.dot_general(a, b, dims, precision=precision, preferred_element_type=F32)


def parts(x):
    high = x.astype(BF16)
    return high, (x - high.astype(F32)).astype(BF16)


def mm3(a, b, dims=NN):
    a_high, a_low = parts(a)
    b_high, b_low = parts(b)
    return mm(a_high, b_high, dims) + (mm(a_low, b_high, dims) + mm(a_high, b_low, dims))


def cos_turns(t):
    r = t - jnp.floor(t + 0.5)
    s = (0.25 - jnp.abs(r)) * TWO_PI
    q = s * s
    p = -2.5052108e-08 + q * 1.6059044e-10
    p = 2.7557319e-06 + q * p
    p = -1.9841270e-04 + q * p
    p = 8.3333333e-03 + q * p
    p = -1.6666667e-01 + q * p
    return s + s * (q * p)


def silu_parts(x):
    gate = 1.0 / (1.0 + jnp.exp(-x))
    return x * gate, gate * (1.0 + x * (1.0 - gate))


def iota(shape, dim):
    return lax.broadcasted_iota(jnp.int32, shape, dim)


def call(kernel, outs, scratch=(), flops=0, nbytes=0, smem=0, vmem=56, inputs=0):
    specs = None
    if smem:
        specs = [pl.BlockSpec(memory_space=pltpu.SMEM)] * smem + [
            pl.BlockSpec(memory_space=pltpu.VMEM)
        ] * (inputs - smem)
    options = {} if specs is None else {"in_specs": specs}
    return pl.pallas_call(
        kernel,
        out_shape=[jax.ShapeDtypeStruct(s, d) for s, d in outs],
        scratch_shapes=list(scratch),
        compiler_params=pltpu.CompilerParams(vmem_limit_bytes=vmem * 2**20),
        cost_estimate=pl.CostEstimate(flops=flops, bytes_accessed=nbytes, transcendentals=0),
        **options,
    )


def border_kernel(pos_ref, species_ref, ghost_ref, out_ref, tab_ref):
    atoms = pos_ref.shape[1]
    tab_ref[0:3, :] = pos_ref[...]
    tab_ref[3:4, :] = species_ref[...].astype(F32)
    for part in range(ghost_ref.shape[1] // 128):
        lanes = pl.ds(128 * part, 128)
        index = jnp.broadcast_to(ghost_ref[:, lanes], (8, 128))
        high, low = index >> 7, index & 127
        value = jnp.zeros((8, 128), F32)
        for block in range(atoms // 128):
            source = tab_ref[:, pl.ds(128 * block, 128)]
            value = jnp.where(high == block, jnp.take_along_axis(source, low, axis=1), value)
        out_ref[:, lanes] = value[0:4]


def prepare_kernel(
    grid,
    where_ref,
    pos_ref,
    wave_ref,
    nbr_ref,
    radial_ref,
    message_ref,
    scalar_ref,
    vector_ref,
    hidden_ref,
    charge_ref,
    nbr_out,
    xz_out,
    dx_out,
    dz_out,
    y_out,
    ycat_out,
    dycat_out,
    unit_out,
    table_out,
    wide_out,
    narrow_out,
    back_out,
):
    extent_x, extent_y, atoms_all = grid
    atoms = pos_ref.shape[1]
    u, v = where_ref[0], where_ref[1]
    x, y, z = pos_ref[0:1, :], pos_ref[1:2, :], pos_ref[2:3, :]

    row = iota((PROWS, atoms), 0)
    xf, order_z = row >> 2, (row & 3) + 1
    order_x = jnp.where(xf < HX, xf, xf - (HX - 1))
    valid = row < PAIRS
    shift_x = jnp.where(xf < HX, 0.0, 0.25)
    whole_x = lax.rem(order_x * u, extent_x).astype(F32)
    turn_x = (order_x.astype(F32) * x + whole_x) / extent_x - shift_x
    fx = jnp.where(valid, cos_turns(turn_x), 0.0)
    gx = jnp.where(valid, cos_turns(turn_x + 0.25) * order_x.astype(F32) * (TWO_PI / extent_x), 0.0)
    whole_y = lax.rem(v, 2 * extent_y).astype(F32)
    turn_z = order_z.astype(F32) * z * (1.0 / BOX_HEIGHT) - (y + whole_y) * (0.5 / extent_y)
    for half in range(2):
        fz = cos_turns(turn_z - 0.25 * half)
        gz = cos_turns(turn_z - 0.25 * half + 0.25)
        xz_out[half] = fx * fz
        dx_out[half] = gx * fz
        dz_out[half] = fx * gz

    row = iota((2 * NY, atoms), 0)
    twice = 2 * (row & (NY - 1)) + 1
    shift_y = jnp.where(row < NY, 0.0, 0.25)
    whole = lax.rem(twice * v, 2 * extent_y).astype(F32)
    turn_y = (twice.astype(F32) * y + whole) * (0.5 / extent_y) - shift_y
    fy = cos_turns(turn_y)
    gy = cos_turns(turn_y + 0.25) * twice.astype(F32) * (0.5 * TWO_PI / extent_y)
    y_out[...] = fy
    high, low = parts(fy)
    ycat_out[0 : 2 * NY, :] = high
    ycat_out[2 * NY :, :] = low
    high, low = parts(gy)
    dycat_out[0 : 2 * NY, :] = high
    dycat_out[2 * NY :, :] = low

    both = jnp.concatenate([fy, fy], axis=0)
    first = mm(xz_out[0], both, NT, HIGHEST)
    second = mm(xz_out[1], both, NT, HIGHEST)
    lane = iota((PROWS, 128), 1)
    unit_out[...] = jnp.where(lane < 64, first, second)

    step = wave_ref.shape[1]
    order = iota((40, step), 0)
    along_x, along_y, along_z = wave_ref[0:1, :], wave_ref[1:2, :], wave_ref[2:3, :]
    matches_z = ((order & 3) + 1 == along_z) & (order < HX * LZ)
    plus = matches_z & ((order >> 2) == along_x)
    minus = matches_z & ((order >> 2) == -along_x) & (order >= LZ)
    lanes = iota((128, step), 0) & (NY - 1)
    up = (lanes == along_y).astype(F32).astype(BF16)
    down = (-lanes - 1 == along_y).astype(F32).astype(BF16)
    plus = plus.astype(F32).astype(BF16)
    minus = minus.astype(F32).astype(BF16)
    order = iota((40, 128), 0)
    lanes = iota((40, 128), 1)
    wave_b = (lanes & (NY - 1)).astype(F32)
    kx = (order >> 2).astype(F32) * (TWO_PI / extent_x)
    kz = ((order & 3) + 1).astype(F32) * (TWO_PI / BOX_HEIGHT)

    def weights(ky):
        squared = kx * kx + ky * ky + kz * kz
        return jnp.exp(-squared / (4.0 * SPLITTING**2)) / squared / atoms_all

    green_up = weights(wave_b * (TWO_PI / extent_y))
    green_down = weights((wave_b + 1.0) * (TWO_PI / extent_y))
    pp = green_up * mm(plus, up, NT)
    pm = green_down * mm(plus, down, NT)
    mp = green_up * mm(minus, up, NT)
    mn = green_down * mm(minus, down, NT)
    quarter = lanes >> 5
    sign_t = jnp.where((quarter == 1) | (quarter == 2), 1.0, -1.0)
    sign_st = jnp.where((quarter & 1) == 1, 1.0, -1.0)
    sign_s = jnp.where(quarter >= 2, 1.0, -1.0)
    table_out[0] = (pp + pm) + (mp + mn)
    table_out[1] = sign_t * ((pp - pm) + (mp - mn))
    table_out[2] = sign_st * ((pp - pm) - (mp - mn))
    table_out[3] = sign_s * ((pp + pm) - (mp + mn))

    col = iota((NB, 512), 1)
    sub = iota((NB, 512), 0)
    pick_b = ((col >> 6) == sub).astype(F32)
    pick_s = (((col >> 3) & 7) == sub).astype(F32)
    message = message_ref[...]
    spread = mm(message, pick_s, NN, HIGHEST)
    channels = message.shape[0]
    for which in range(2):
        wide = mm(radial_ref[which * channels : (which + 1) * channels, :], pick_b, NN, HIGHEST) * spread
        high, low = parts(wide)
        wide_out[which, 0:channels] = high
        wide_out[which, channels:] = low
    col = iota((NB, 64), 1)
    sub = iota((NB, 64), 0)
    pick_b = ((col >> 3) == sub).astype(F32)
    pick_s = ((col & 7) == sub).astype(F32)
    spread = mm(message, pick_s, NN, HIGHEST)
    for which in range(2):
        narrow = mm(radial_ref[which * channels : (which + 1) * channels, :], pick_b, NN, HIGHEST) * spread
        narrow_out[which] = narrow.T
    back_out[0] = scalar_ref[...].T
    back_out[1] = vector_ref[...].T
    back_out[2] = hidden_ref[...].T
    back_out[3, 0:32] = charge_ref[...].T
    nbr_out[...] = nbr_ref[...].T


def basis_terms(dist, rho, live):
    envelope = jnp.exp(-0.25 * rho) * live
    out = []
    for b in range(NB):
        off = dist - CENTRE_STEP * b
        out.append((jnp.exp(off * off * (-0.5 / CENTRE_STEP**2)) * envelope, off))
    return out


def forward_kernel(
    where_ref,
    pos_ref,
    species_ref,
    mid_ref,
    prev_ref,
    next_ref,
    nbr_ref,
    embed_ref,
    wide_ref,
    back_ref,
    hidden_ref,
    readout_ref,
    xz_ref,
    ycat_ref,
    unit_ref,
    energy_out,
    charge_out,
    hbar_out,
    slope_out,
    vsum_out,
    geo_out,
    keep_out,
    send_out,
    tab_ref,
    moment_ref,
    qh_ref,
    ql_ref,
    pay_ref,
):
    atoms = pos_ref.shape[1]
    tiles = atoms // 128
    for c in range(3):
        for j in range(tiles):
            tab_ref[c, j : j + 1, :] = pos_ref[c : c + 1, pl.ds(128 * j, 128)]
    for j in range(tiles):
        tab_ref[3, j : j + 1, :] = species_ref[:, pl.ds(128 * j, 128)].astype(F32)
    for i in range(3):
        for j, block_ref in enumerate((prev_ref, mid_ref, next_ref)):
            block = block_ref[i]
            shifts = (i - 1.0, j - 1.0, 0.0, 0.0)
            for c in range(4):
                for h in range(2):
                    at = tiles + 2 * (3 * i + j) + h
                    tab_ref[c, at : at + 1, :] = block[c : c + 1, 128 * h : 128 * h + 128] + shifts[c]

    def lane_tile(t, carry):
        lanes = pl.ds(pl.multiple_of(t * 128, 128), 128)
        for tile in range(4):
            index = nbr_ref[pl.ds(8 * tile, 8), lanes]
            live = (index >= 0).astype(F32)
            index = jnp.maximum(index, 0)
            high, low = index >> 7, index & 127
            value = [jnp.zeros((8, 128), F32) for _ in range(4)]
            for block in range(tiles + 18):
                if block // 2 == tiles // 2 + 4:
                    continue
                here = high == block
                for c in range(4):
                    source = jnp.broadcast_to(tab_ref[c, block : block + 1, :], (8, 128))
                    value[c] = jnp.where(here, jnp.take_along_axis(source, low, axis=1), value[c])
            rx, ry, rz = (value[c] - pos_ref[c : c + 1, lanes] for c in range(3))
            rho = rx * rx + ry * ry + rz * rz
            dist = jnp.sqrt(rho + SOFTENING)
            inv = 1.0 / dist
            rows = pl.ds(8 * tile, 8)
            geo_out[0, rows, lanes] = rx * inv
            geo_out[1, rows, lanes] = ry * inv
            geo_out[2, rows, lanes] = rz * inv
            geo_out[3, rows, lanes] = dist
            geo_out[4, rows, lanes] = rho
            geo_out[5, rows, lanes] = value[3]
            geo_out[6, rows, lanes] = live
        dist = geo_out[3, :, lanes]
        terms = basis_terms(dist, geo_out[4, :, lanes], geo_out[6, :, lanes])
        kind = geo_out[5, :, lanes]
        for f in range(4):
            for b in range(NB):
                value = terms[b][0] if f == 0 else terms[b][0] * geo_out[f - 1, :, lanes]
                for s in range(NS):
                    chosen = jnp.where(kind == float(s), value, 0.0)
                    total = (chosen[0:8] + chosen[8:16]) + (chosen[16:24] + chosen[24:32])
                    moment_ref[f, pl.ds(8 * (8 * b + s), 8), lanes] = total
        return carry

    lax.fori_loop(0, tiles, lane_tile, 0)

    def gathered(f):
        wide = wide_ref[0 if f == 0 else 1]
        high, low = parts(moment_ref[f])
        both = mm(wide, high)
        return both[0:128] + both[128:256] + mm(wide[0:128], low)

    scalar_sum = gathered(0)
    norm = None
    for c in range(3):
        vector = gathered(c + 1)
        vsum_out[c] = vector
        norm = vector * vector if norm is None else norm + vector * vector
    update = mm3(back_ref[0], scalar_sum) + mm3(back_ref[1], norm)
    feature = jnp.zeros_like(update)
    kinds = species_ref[...]
    for s in range(NS):
        feature = jnp.where(kinds == s, embed_ref[:, s : s + 1], feature)
    act, slope = silu_parts(update)
    slope_out[...] = slope
    hidden = feature + act
    act, slope = silu_parts(mm3(back_ref[2], hidden))
    readout = readout_ref[...]
    energy_out[...] = jnp.sum(act * readout, axis=0, keepdims=True)
    hbar_out[...] = mm3(hidden_ref[...], slope * readout)
    charges = mm3(back_ref[3, 0:32], hidden)
    charge_out[...] = charges

    total = jnp.sum(charges, axis=1, keepdims=True)
    local = total * (1.0 / atoms)
    centred = charges - local
    lane = iota((32, 128), 1)
    group = 17

    def sums(k, carry):
        for half in range(2):
            for i in range(group):
                row = xz_ref[half, pl.ds(k * group + i, 1), :]
                high, low = parts(centred * row)
                qh_ref[half, 32 * i : 32 * i + 32, :] = high
                ql_ref[half, 32 * i : 32 * i + 32, :] = low
        ycat = ycat_ref[...]
        first = mm(qh_ref[0], ycat, NT) + mm(ql_ref[0], ycat, NT)
        second = mm(qh_ref[1], ycat, NT) + mm(ql_ref[1], ycat, NT)
        first = first + pltpu.roll(first, 64, 1)
        second = second + pltpu.roll(second, 64, 1)
        for i in range(group):
            rows = slice(32 * i, 32 * i + 32)
            packed = jnp.where(lane < 64, first[rows], second[rows])
            packed = packed + local * unit_ref[pl.ds(k * group + i, 1), :]
            at = pl.multiple_of((k * group + i) * 32, 32)
            pay_ref[pl.ds(at, 32), :] = packed
        return carry

    lax.fori_loop(0, PAIRS // group, sums, 0)
    pay_ref[UNIT_ROW:TOTAL_ROW, :] = unit_ref[...]
    pay_ref[TOTAL_ROW : TOTAL_ROW + 32, :] = jnp.broadcast_to(total, (32, 128))
    pay_ref[TOTAL_ROW + 32 :, :] = jnp.zeros((ROWS - TOTAL_ROW - 32, 128), F32)
    place(where_ref, pay_ref, keep_out, send_out, False)


def place(where_ref, whole_ref, near_ref, far_ref, inward):
    for c in range(2):
        for y in range(4):
            for x in range(4):
                absolute = ((where_ref[2] + c) & 1) * 16 + ((where_ref[3] + y) & 3) * 4 + ((where_ref[4] + x) & 3)
                there = pl.ds(pl.multiple_of(absolute * CHUNK, 8), CHUNK)
                here = pl.ds((4 * y + x) * CHUNK, CHUNK)
                part = near_ref if c == 0 else far_ref
                if inward:
                    whole_ref[there, :] = part[here, :]
                else:
                    part[here, :] = whole_ref[there, :]


def quarters(x, which):
    lane = iota(x.shape, 1)
    if which == 2:
        return pltpu.roll(x, 64, 1)
    even = ((lane >> 5) & 1) == 0
    if which == 1:
        return jnp.where(even, pltpu.roll(x, 96, 1), pltpu.roll(x, 32, 1))
    return jnp.where(even, pltpu.roll(x, 32, 1), pltpu.roll(x, 96, 1))


def backward_kernel(
    atoms_all,
    where_ref,
    near_ref,
    far_ref,
    table_ref,
    xz_ref,
    ycat_ref,
    energy_ref,
    charge_ref,
    hbar_ref,
    slope_ref,
    vsum_ref,
    geo_ref,
    nbr_ref,
    scalar_ref,
    vector_ref,
    weight_ref,
    narrow_ref,
    site_out,
    neutral_out,
    va_out,
    vb_out,
    own_out,
    prev_out,
    mid_out,
    next_out,
    sum_ref,
    ta_ref,
    tb_ref,
    g_ref,
    rbar_ref,
):
    atoms = nbr_ref.shape[1]
    tiles = atoms // 128
    place(where_ref, sum_ref, near_ref, far_ref, True)
    mean = sum_ref[TOTAL_ROW : TOTAL_ROW + 32, :] * (1.0 / atoms_all)
    lane = iota((32, 128), 1)

    def put(p, value):
        high = value.astype(BF16).astype(F32)
        low = value - high
        rows = pl.ds(pl.multiple_of(p * 32, 32), 32)
        va_out[rows, :] = jnp.where(lane < 64, high, pltpu.roll(low, 64, 1)).astype(BF16)
        vb_out[rows, :] = jnp.where(lane < 64, pltpu.roll(high, 64, 1), low).astype(BF16)

    def tile_of(p):
        unit = sum_ref[pl.ds(UNIT_ROW + p, 1), :]
        return sum_ref[pl.ds(pl.multiple_of(p * 32, 32), 32), :] - mean * unit, unit

    overlap = jnp.zeros((32, 128), F32)
    for l in range(LZ):
        cos_tile, unit = tile_of(l)
        g0 = table_ref[0, l : l + 1, :]
        gt = table_ref[1, l : l + 1, :]
        value = g0 * cos_tile + gt * quarters(cos_tile, 3)
        overlap = overlap + value * unit
        put(l, value)

    def mix(a, overlap):
        for l in range(LZ):
            at = a * LZ + l
            sat = (a + HX - 1) * LZ + l
            cos_tile, cos_unit = tile_of(at)
            sin_tile, sin_unit = tile_of(sat)
            g0 = table_ref[0, pl.ds(at, 1), :]
            gt = table_ref[1, pl.ds(at, 1), :]
            gst = table_ref[2, pl.ds(at, 1), :]
            gs = table_ref[3, pl.ds(at, 1), :]
            value = (g0 * cos_tile + gt * quarters(cos_tile, 3)) + (
                gst * quarters(sin_tile, 1) + gs * quarters(sin_tile, 2)
            )
            overlap = overlap + value * cos_unit
            put(at, value)
            value = (g0 * sin_tile + gt * quarters(sin_tile, 3)) - (
                gst * quarters(cos_tile, 1) + gs * quarters(cos_tile, 2)
            )
            overlap = overlap + value * sin_unit
            put(sat, value)
        return overlap

    overlap = lax.fori_loop(1, HX, mix, overlap)
    potential_mean = jnp.sum(overlap, axis=1, keepdims=True) * (1.0 / atoms_all)

    high, low = ycat_ref[0:64, :], ycat_ref[64:128, :]
    right = jnp.concatenate([high, high, low, low], axis=0)
    group = 17

    def evaluate(k, potential):
        rows = pl.ds(pl.multiple_of(k * group * 32, 32), group * 32)
        left = va_out[rows, :]
        ta_ref[...] = mm(jnp.concatenate([left, left], axis=1), right)
        left = vb_out[rows, :]
        tb_ref[...] = mm(jnp.concatenate([left, left], axis=1), right)
        for i in range(group):
            first = xz_ref[0, pl.ds(k * group + i, 1), :]
            second = xz_ref[1, pl.ds(k * group + i, 1), :]
            here = slice(32 * i, 32 * i + 32)
            potential = potential + (first * ta_ref[here, :] + second * tb_ref[here, :])
        return potential

    potential = lax.fori_loop(0, PAIRS // group, evaluate, jnp.zeros((32, atoms), F32))
    neutral = charge_ref[...] - mean[:, 0:1]
    neutral_out[...] = neutral
    site_out[...] = energy_ref[...] + jnp.sum(neutral * potential, axis=0, keepdims=True)
    charge_bar = 2.0 * (potential - potential_mean)
    update_bar = (hbar_ref[...] + mm3(weight_ref[...], charge_bar)) * slope_ref[...]
    scalar_bar = mm3(scalar_ref[...], update_bar)
    norm_bar = 2.0 * mm3(vector_ref[...], update_bar)
    g_ref[0] = mm3(narrow_ref[0], scalar_bar)
    for c in range(3):
        g_ref[c + 1] = mm3(narrow_ref[1], vsum_ref[c] * norm_bar)

    def slots(t, carry):
        lanes = pl.ds(pl.multiple_of(t * 128, 128), 128)
        own = [jnp.zeros((8, 128), F32) for _ in range(3)]
        for tile in range(4):
            rows = pl.ds(8 * tile, 8)
            unit = [geo_ref[c, rows, lanes] for c in range(3)]
            dist = geo_ref[3, rows, lanes]
            kind = geo_ref[5, rows, lanes].astype(jnp.int32)
            terms = basis_terms(dist, geo_ref[4, rows, lanes], geo_ref[6, rows, lanes])
            inv = 1.0 / dist
            ubar = [jnp.zeros((8, 128), F32) for _ in range(3)]
            plain = jnp.zeros((8, 128), F32)
            tilted = jnp.zeros((8, 128), F32)
            for b in range(NB):
                value, off = terms[b]
                picked = [
                    jnp.take_along_axis(g_ref[f, 8 * b : 8 * b + 8, lanes], kind, axis=0) for f in range(4)
                ]
                bar = picked[0]
                for c in range(3):
                    bar = bar + unit[c] * picked[c + 1]
                    ubar[c] = ubar[c] + value * picked[c + 1]
                bar = bar * value
                plain = plain + bar
                tilted = tilted + bar * off
            along = ubar[0] * unit[0] + ubar[1] * unit[1] + ubar[2] * unit[2]
            dist_bar = tilted * (-1.0 / CENTRE_STEP**2) - along * inv
            radial = dist * (2.0 * (-0.25 * plain) + dist_bar * inv)
            for c in range(3):
                bar = ubar[c] * inv + unit[c] * radial
                rbar_ref[c, rows, lanes] = bar
                own[c] = own[c] + bar
        for c in range(3):
            own_out[c : c + 1, lanes] = -jnp.sum(own[c], axis=0, keepdims=True)
        return carry

    lax.fori_loop(0, tiles, slots, 0)

    block_rows = 24
    rows_high = iota((block_rows, atoms), 0)
    rows_low = iota((128, atoms), 0)

    def scatter(s, total):
        index = jnp.maximum(nbr_ref[pl.ds(s, 1), :], 0)
        at_high = rows_high == (index >> 7)
        at_low = jnp.where(rows_low == (index & 127), 1.0, 0.0).astype(BF16)
        pieces = []
        for c in range(3):
            value = rbar_ref[c, pl.ds(s, 1), :]
            high = value.astype(BF16).astype(F32)
            pieces.append(jnp.where(at_high, high, 0.0))
            pieces.append(jnp.where(at_high, value - high, 0.0))
        left = jnp.concatenate(pieces, axis=0).astype(BF16)
        return total + mm(left, at_low, NT)

    total = lax.fori_loop(0, nbr_ref.shape[0], scatter, jnp.zeros((6 * block_rows, 128), F32))
    for c in range(3):
        at = 2 * block_rows * c
        table = total[at : at + block_rows] + total[at + block_rows : at + 2 * block_rows]
        for j in range(tiles):
            lanes = pl.ds(128 * j, 128)
            own_out[c : c + 1, lanes] = own_out[c : c + 1, lanes] + table[j : j + 1]
        for i in range(3):
            for j, out in enumerate((prev_out, mid_out, next_out)):
                for h in range(2):
                    row = tiles + 2 * (3 * i + j) + h
                    out[i, c : c + 1, 128 * h : 128 * h + 128] = table[row : row + 1]


def ewald_kernel(
    grid,
    va_ref,
    vb_ref,
    xz_ref,
    dx_ref,
    dz_ref,
    ycat_ref,
    dycat_ref,
    neutral_ref,
    own_ref,
    out_ref,
    ta_ref,
    tb_ref,
    da_ref,
    db_ref,
):
    extent_y = grid
    atoms = neutral_ref.shape[1]
    right = [
        jnp.concatenate([ref[0:64, :], ref[0:64, :], ref[64:128, :], ref[64:128, :]], axis=0)
        for ref in (ycat_ref, dycat_ref)
    ]
    neutral = neutral_ref[...]
    group = 17

    def step(k, sums):
        rows = pl.ds(pl.multiple_of(k * group * 32, 32), group * 32)
        for ref, even, odd in ((va_ref, ta_ref, da_ref), (vb_ref, tb_ref, db_ref)):
            left = ref[rows, :]
            left = jnp.concatenate([left, left], axis=1)
            even[...] = mm(left, right[0])
            odd[...] = mm(left, right[1])
        sum_x, sum_y, sum_z = sums
        for i in range(group):
            at = k * group + i
            order = (lax.rem(at, LZ) + 1).astype(F32) * (TWO_PI / BOX_HEIGHT)
            here = slice(32 * i, 32 * i + 32)
            for half, even, odd in ((0, ta_ref, da_ref), (1, tb_ref, db_ref)):
                value = even[here, :]
                sum_x = sum_x + dx_ref[half, pl.ds(at, 1), :] * value
                turned = dz_ref[half, pl.ds(at, 1), :]
                sum_z = sum_z + (order * turned) * value
                sum_y = sum_y + (
                    xz_ref[half, pl.ds(at, 1), :] * odd[here, :]
                    - ((0.5 * TWO_PI / extent_y) * turned) * value
                )
        return sum_x, sum_y, sum_z

    zero = jnp.zeros((32, atoms), F32)
    sums = lax.fori_loop(0, PAIRS // group, step, (zero, zero, zero))
    for c in range(3):
        out_ref[c : c + 1, :] = own_ref[c : c + 1, :] + 2.0 * jnp.sum(neutral * sums[c], axis=0, keepdims=True)


def finish_kernel(base_ref, mid_ref, first_ref, second_ref, ghost_ref, out_ref):
    atoms = base_ref.shape[1]
    returned = mid_ref[...] + first_ref[...] + second_ref[...]
    high = returned.astype(BF16).astype(F32)
    rest = returned - high
    middle = rest.astype(BF16).astype(F32)
    split = jnp.concatenate([high, middle, rest - middle, jnp.zeros((7, 256), F32)], axis=0).astype(BF16)
    at = jnp.where(iota((atoms, 256), 0) == ghost_ref[...], 1.0, 0.0).astype(BF16)
    spread = mm(split, at, NT)
    out_ref[...] = -(base_ref[...] + ((spread[0:3] + spread[3:6]) + spread[6:9]))


def add_kernel(count, *refs):
    ins, outs = refs[:count], refs[count:]
    rows = outs[0].shape[0]
    for k, out in enumerate(outs):
        here = pl.ds(k * rows, rows)
        total = ins[0][here, :]
        for ref in ins[1:]:
            total = total + ref[here, :]
        out[...] = total


def add_up(arrays, pieces):
    rows = arrays[0].shape[0] // pieces
    return call(functools.partial(add_kernel, len(arrays)), [((rows, 128), F32)] * pieces)(*arrays)


def shifted(array, axis, by):
    devices = lax.axis_size(axis)
    return lax.ppermute(array, axis, [(i, (i + by) % devices) for i in range(devices)])


class Ring:
    def __init__(self):
        self.first, self.second = lax.axis_size("gx"), lax.axis_size("gy")
        u, v = lax.axis_index("gx"), lax.axis_index("gy")
        self.index = [u, v, u % 2, v % 4, v // 4 % 4]

    def move(self, array, axis, by):
        pairs = []
        for device in range(self.first * self.second):
            u, v = divmod(device, self.second)
            core, z, y, x, top = u % 2, u // 2, v % 4, v // 4 % 4, v // 16
            if axis == "core":
                core = (core + by) % 2
            elif axis == "y":
                y = (y + by) % 4
            elif axis == "x":
                x = (x + by) % 4
            elif axis == "z":
                z = (z + by) % 4
            elif axis == "top":
                top = (top + by) % 2
            pairs.append((device, (z * 2 + core) * self.second + top * 16 + x * 4 + y))
        return lax.ppermute(array, AXES, pairs)


def total_over_devices(ring, keep, send):
    got = ring.move(send, "core", 1)
    for axis in ("y", "x"):
        parts_ = add_up([keep, got] if axis == "y" else [keep] + got, 4)
        keep = parts_[0]
        got = [ring.move(parts_[d], axis, d) for d in range(1, 4)]
    (keep,) = add_up([keep] + got, 1)
    got = [ring.move(keep, "z", d) for d in range(1, 4)]
    (keep,) = add_up([keep] + got, 1)
    (keep,) = add_up([keep, ring.move(keep, "top", 1)], 1)
    for axis in ("x", "y"):
        keep = jnp.concatenate([keep] + [ring.move(keep, axis, -d) for d in range(1, 4)], axis=0)
    return keep, ring.move(keep, "core", 1)


def shards(
    positions,
    species,
    neighbours,
    ghost_index,
    wave_index,
    embedding,
    radial_weight,
    message_weight,
    scalar_weight,
    vector_weight,
    readout_hidden,
    readout_vector,
    charge_weight,
):
    atoms = positions.shape[1]
    ring = Ring()
    atoms_all = atoms * ring.first * ring.second
    where = jnp.stack(ring.index).astype(jnp.int32)
    kinds = species[None]
    ghosts = ghost_index[None]

    (border,) = call(border_kernel, [((4, 256), F32)], [pltpu.VMEM((8, atoms), F32)])(positions, kinds, ghosts)
    mid = jnp.stack([shifted(border, "gx", 1), border, shifted(border, "gx", -1)])
    prev, after = shifted(mid, "gy", 1), shifted(mid, "gy", -1)

    embed_t = embedding.T
    message_t = lax.dot_general(message_weight, embedding, (((0,), (1,)), ((), ())), precision=HIGHEST)
    nbr, xz, dx, dz, _, ycat, dycat, unit, table, wide, narrow, back = call(
        functools.partial(prepare_kernel, (ring.first, ring.second, atoms_all)),
        [
            ((32, atoms), jnp.int32),
            ((2, PROWS, atoms), F32),
            ((2, PROWS, atoms), F32),
            ((2, PROWS, atoms), F32),
            ((64, atoms), F32),
            ((128, atoms), BF16),
            ((128, atoms), BF16),
            ((PROWS, 128), F32),
            ((4, 40, 128), F32),
            ((2, 256, 512), BF16),
            ((2, 64, 128), F32),
            ((4, 128, 128), F32),
        ],
        smem=1,
        inputs=10,
        flops=10**9,
        nbytes=4 * 10**6,
    )(
        where,
        positions,
        wave_index,
        neighbours,
        radial_weight.T,
        message_t,
        scalar_weight,
        vector_weight,
        readout_hidden,
        charge_weight,
    )

    energy, charge, hbar, slope, vsum, geo, keep, send = call(
        forward_kernel,
        [
            ((1, atoms), F32),
            ((32, atoms), F32),
            ((128, atoms), F32),
            ((128, atoms), F32),
            ((3, 128, atoms), F32),
            ((7, 32, atoms), F32),
            ((ROWS // 2, 128), F32),
            ((ROWS // 2, 128), F32),
        ],
        [
            pltpu.VMEM((4, 24, 128), F32),
            pltpu.VMEM((4, 512, atoms), F32),
            pltpu.VMEM((2, 544, atoms), BF16),
            pltpu.VMEM((2, 544, atoms), BF16),
            pltpu.VMEM((ROWS, 128), F32),
        ],
        smem=1,
        inputs=15,
        flops=5 * 10**9,
        nbytes=4 * 10**6,
    )(
        where,
        positions,
        kinds,
        mid,
        prev,
        after,
        nbr,
        embed_t,
        wide,
        back,
        readout_hidden,
        readout_vector[:, None],
        xz,
        ycat,
        unit,
    )

    near, far = total_over_devices(ring, keep, send)

    site, neutral, va, vb, own, g_prev, g_mid, g_next = call(
        functools.partial(backward_kernel, atoms_all),
        [
            ((1, atoms), F32),
            ((32, atoms), F32),
            ((UNIT_ROW, 128), BF16),
            ((UNIT_ROW, 128), BF16),
            ((3, atoms), F32),
            ((3, 3, 256), F32),
            ((3, 3, 256), F32),
            ((3, 3, 256), F32),
        ],
        [
            pltpu.VMEM((ROWS, 128), F32),
            pltpu.VMEM((544, atoms), F32),
            pltpu.VMEM((544, atoms), F32),
            pltpu.VMEM((4, 64, atoms), F32),
            pltpu.VMEM((3, 32, atoms), F32),
        ],
        smem=1,
        inputs=17,
        flops=5 * 10**9,
        nbytes=4 * 10**6,
    )(
        where,
        near,
        far,
        table,
        xz,
        ycat,
        energy,
        charge,
        hbar,
        slope,
        vsum,
        geo,
        nbr,
        scalar_weight,
        vector_weight,
        charge_weight,
        narrow,
    )

    column = g_mid + shifted(g_prev, "gy", -1) + shifted(g_next, "gy", 1)
    first, second = shifted(column[0], "gx", -1), shifted(column[2], "gx", 1)
    (base,) = call(
        functools.partial(ewald_kernel, ring.second),
        [((3, atoms), F32)],
        [pltpu.VMEM((544, atoms), F32)] * 4,
        flops=5 * 10**9,
        nbytes=4 * 10**6,
    )(va, vb, xz, dx, dz, ycat, dycat, neutral, own)
    (forces,) = call(finish_kernel, [((3, atoms), F32)])(base, column[1], first, second, ghosts)
    return forces, site[0]


def solution(mesh):
    return jax.shard_map(
        shards,
        mesh=mesh,
        in_specs=(
            P(None, ("gx", "gy")),
            P(("gx", "gy")),
            P(("gx", "gy"), None),
            P(("gx", "gy")),
            P(),
            P(),
            P(),
            P(),
            P(),
            P(),
            P(),
            P(),
            P(),
        ),
        out_specs=(P(None, ("gx", "gy")), P(("gx", "gy"))),
        check_vma=False,
    )
```

time: 983 us -> 160 us (0.16); the launches traced: 972 us -> 159 us
  matrix products: 255 us -> 0.92 us
  waiting for transfers between devices: 263 us -> 48.8 us
  other arithmetic: 198 us -> 0.73 us
  local copies, waits for them, and re-layouts: 136 us -> 12.7 us
  blocking collectives: 73.1 us -> 0 us
  Pallas kernels: 0 us -> 50 us
  between operations: 15.5 us -> 0.82 us
  starting transfers between devices: 31.8 us -> 45 us
    dot_general x25 -> x1, matrix products: 255 us -> 0.92 us  [shards(): lax.dot_general(message_weight, embedding, (((0,), (1,)), ((), ())), prec...]
    psum x1 -> x0, waiting for transfers between devices: 251 us -> none  [shards(): lax.psum((cos_part, sin_part, unit_cos_part, unit_sin_part), ('gx', 'gy'))]
    gather x6 -> x0, local copies, waits for them, and re-layouts: 118 us -> none  [the longest x2 60.7 us: short_range(): offsets = table_pos[:, safe_index] - own_pos[:, :, None]]
    scatter-add x2 -> x0, other arithmetic: 90.5 us -> none  [the longest x1 88.3 us: short_range(): offsets = table_pos[:, safe_index] - own_pos[:, :, None]]
    psum x1 -> x0, blocking collectives: 73.1 us -> none  [shards(): totals = lax.psum(jnp.sum(charges, axis=0), ('gx', 'gy'))]
    pallas_call x0 -> x11, Pallas kernels: none -> 50 us  [the longest x1 15.7 us: shards(): call(functools.partial(backward_kernel, atoms_all), [((1, atoms), F32), (...]
    reduce_sum x5 -> x0, other arithmetic: 40.8 us -> none  [the longest x1 33.6 us: shards(): unit_sin_part = jnp.sum(sine_terms, axis=0)]
    dot_general x2 -> x0, other arithmetic: 35.9 us -> none  [the longest x1 34.7 us: shards(): jnp.einsum('xk,ak->xa', vectors, angle_cotangent, precision=HIGHEST)]
  transfers between devices with their start and end apart: 9 -> 26, of which waited for: 2 -> 19; matrix products, arithmetic and copies ran while one was open for 9% -> 4% of each run, Pallas kernels for 0% -> 8%
where the time goes in v1:
time: 160 us; the launch traced here: 159 us
  Pallas kernels  50 us (31%)
  waiting for transfers between devices  48.8 us (30%)
  starting transfers between devices  45 us (28%)
  local copies, waits for them, and re-layouts  12.7 us (8%)
    ppermute x18, waiting for transfers between devices, move(): return lax.ppermute(array, AXES, pairs)  32.4 us
    ppermute x8, starting transfers between devices, shifted(): lax.ppermute(array, axis, [(i, (i + by) % devices) for i in range(devices)])  23 us
    ppermute x18, starting transfers between devices, move(): return lax.ppermute(array, AXES, pairs)  21.9 us
    ppermute x8, waiting for transfers between devices, shifted(): lax.ppermute(array, axis, [(i, (i + by) % devices) for i in range(devices)])  16.5 us
    pallas_call x1, Pallas kernels, shards(): call(functools.partial(backward_kernel, atoms_all), [((1, atoms), F32), (...  15.7 us
    pallas_call x1, Pallas kernels, shards(): call(forward_kernel, [((1, atoms), F32), ((32, atoms), F32), ((128, atoms...  11 us
    unnamed x62, local copies, waits for them, and re-layouts  10.7 us
    pallas_call x5, Pallas kernels, add_up(): call(functools.partial(add_kernel, len(arrays)), [((rows, 128), F32)] * p...  8.17 us
  transfers between devices with their start and end apart: 26, of which 19 were waited for; matrix products, arithmetic and copies ran while one was open for 4% of the time, Pallas kernels for 8%

profile of v1, /device:TPU:0, one launch (start us, length us, event | category | flops | bytes accessed | tf_op | source)
XLA Modules:
  0.0 158.9 jit_solution(14369156849436586842)
XLA Ops:
  0.7 1.4 shard_map.140
  2.1 2.3 %collective-permute-start.1 = (f32[4,256]{1,0:T(4,128)}, f32[4,256]{1,0:T(4,128)S(1)}, u32[]{:S(2)}, u32[]{:S(2)}) collective-permute-start(f32[4,256]{1,0:T(4,128)} %shard_map.140), channel_id=1, source_target_pairs={{0,224},{32,0},{64,32},{96,64},{128,96},{160,128},{192,160},{224,1... | collective-permute-start | bytes 12296 | tf_op jit(solution)/shard_map/ppermute | solution.py:684
  9.5 9.2 %collective-permute-start.3 = (f32[3,4,256]{2,1,0:T(4,128)S(1)}, f32[3,4,256]{2,1,0:T(4,128)S(1)}, u32[]{:S(2)}, u32[]{:S(2)}) collective-permute-start(f32[3,4,256]{2,1,0:T(4,128)S(1)} %pad_maximum_fusion.1.mid_ref), channel_id=1, source_target_pairs={{0,31},{1,0},{2,1},{3,2},{4,3},{5,4},{6,5},{7,6},{8,7},{9,8},{10,9... | collective-permute-start | bytes 36872 | tf_op jit(solution)/shard_map/ppermute | solution.py:684
  18.7 5.6 %shard_map.141 = (s32[32,512]{1,0:T(8,128)}, f32[2,72,512]{2,1,0:T(8,128)}, f32[2,72,512]{2,1,0:T(8,128)}, f32[2,72,512]{2,1,0:T(8,128)}, f32[64,512]{1,0:T(8,12...) custom-call(s32[5]{0:T(128)} %stack.35.where_ref, ...), custom_call_target="tpu_custom_call" | custom-call | flops 1000000000 | bytes 4000000 | tf_op jit(solution)/shard_map/pallas_call | solution.py:755
  26.4 4.1 %collective-permute-done.2.prev_ref = f32[3,4,256]{2,1,0:T(4,128)S(1)} collective-permute-done((f32[3,4,256]{2,1,0:T(4,128)S(1)}, f32[3,4,256]{2,1,0:T(4,128)S(1)}, u32[]{:S(2)}, u32[]{:S(2)}) %collective-permute-start.2) | collective-permute-done | bytes 12320 | tf_op jit(solution)/shard_map/ppermute | solution.py:684
  31.1 11.0 %shard_map.142 = (f32[1,512]{1,0:T(1,128)}, f32[32,512]{1,0:T(8,128)}, f32[128,512]{1,0:T(8,128)}, f32[128,512]{1,0:T(8,128)}, f32[3,128,512]{2,1,0:T(8,128)}, /...) custom-call(s32[5]{0:T(128)} %stack.35.where_ref, f32[3,512]{1,0:T(4,128)} %pos_ref.5, ...), custom_call_target="tpu_custom_call" | custom-call | flops 5000000000 | bytes 4000000 | tf_op jit(solution)/shard_map/pallas_call | solution.py:788
  42.1 2.2 %collective-permute-done.4.refs_1_ = f32[1152,128]{1,0:T(8,128)S(1)} collective-permute-done((f32[1152,128]{1,0:T(8,128)}, f32[1152,128]{1,0:T(8,128)S(1)}, u32[]{:S(2)}, u32[]{:S(2)}) %collective-permute-start.4) | collective-permute-done | bytes 589856 | tf_op jit(solution)/shard_map/ppermute | solution.py:709
  45.1 2.1 %shard_map.143 = (f32[288,128]{1,0:T(8,128)}, f32[288,128]{1,0:T(8,128)}, f32[288,128]{1,0:T(8,128)}, f32[288,128]{1,0:T(8,128)}) custom-call(f32[1152,128]{1,0:T(8,128)} %get-tuple-element.43.refs_0_, f32[1152,128]{1,0:T(8,128)} %copy-done.1), custom_call_target="tpu_custom_call" | custom-call | tf_op jit(solution)/shard_map/pallas_call | solution.py:679
  47.2 3.2 %collective-permute-start.7 = (f32[288,128]{1,0:T(8,128)}, f32[288,128]{1,0:T(8,128)S(1)}, u32[]{:S(2)}, u32[]{:S(2)}) collective-permute-start(f32[288,128]{1,0:T(8,128)} %get-tuple-element.48), channel_id=1, source_target_pairs={{0,3},{1,0},{2,1},{3,2},{4,7},{5,4},{6,5},{7,6},{8,11},{9,8},{10,9... | collective-permute-start | bytes 442376 | tf_op jit(solution)/shard_map/ppermute | solution.py:709
  50.4 7.2 %collective-permute-done.5.refs_1_ = f32[288,128]{1,0:T(8,128)S(1)} collective-permute-done((f32[288,128]{1,0:T(8,128)}, f32[288,128]{1,0:T(8,128)S(1)}, u32[]{:S(2)}, u32[]{:S(2)}) %collective-permute-start.5) | collective-permute-done | bytes 147488 | tf_op jit(solution)/shard_map/ppermute | solution.py:709
  59.0 1.8 %shard_map.144 = (f32[72,128]{1,0:T(8,128)}, f32[72,128]{1,0:T(8,128)}, f32[72,128]{1,0:T(8,128)}, f32[72,128]{1,0:T(8,128)}) custom-call(f32[288,128]{1,0:T(8,128)} %get-tuple-element.45.refs_0_, f32[288,128]{1,0:T(8,128)} %copy-done.3, f32[288,128]{1,0:T(8,128)} %copy-done.4, f32[288,128]{1,0:T(8,128)} %copy-done.5), custom_call_target="tpu_custom_call" | custom-call | tf_op jit(solution)/shard_map/pallas_call | solution.py:679
  60.8 1.8 %collective-permute-start.9 = (f32[72,128]{1,0:T(8,128)}, f32[72,128]{1,0:T(8,128)S(1)}, u32[]{:S(2)}, u32[]{:S(2)}) collective-permute-start(f32[72,128]{1,0:T(8,128)} %get-tuple-element.51), channel_id=1, source_target_pairs={{0,8},{1,9},{2,10},{3,11},{4,12},{5,13},{6,14},{7,15},{8,0},{9,1},... | collective-permute-start | bytes 110600 | tf_op jit(solution)/shard_map/ppermute | solution.py:709
  64.0 2.1 %collective-permute-done.8.refs_1_ = f32[72,128]{1,0:T(8,128)S(1)} collective-permute-done((f32[72,128]{1,0:T(8,128)}, f32[72,128]{1,0:T(8,128)S(1)}, u32[]{:S(2)}, u32[]{:S(2)}) %collective-permute-start.8) | collective-permute-done | bytes 36896 | tf_op jit(solution)/shard_map/ppermute | solution.py:709
  68.0 1.4 shard_map.145.refs_0_
  69.4 2.3 %collective-permute-start.13 = (f32[72,128]{1,0:T(8,128)}, f32[72,128]{1,0:T(8,128)S(1)}, u32[]{:S(2)}, u32[]{:S(2)}) collective-permute-start(f32[72,128]{1,0:T(8,128)} %shard_map.145.refs_0_), channel_id=1, source_target_pairs={{0,192},{1,193},{2,194},{3,195},{4,196},{5,197},{6,198},{7,199},{8... | collective-permute-start | bytes 110600 | tf_op jit(solution)/shard_map/ppermute | solution.py:709
  72.3 1.7 %collective-permute-done.13.refs_3_ = f32[72,128]{1,0:T(8,128)S(1)} collective-permute-done((f32[72,128]{1,0:T(8,128)}, f32[72,128]{1,0:T(8,128)S(1)}, u32[]{:S(2)}, u32[]{:S(2)}) %collective-permute-start.13) | collective-permute-done | bytes 36896 | tf_op jit(solution)/shard_map/ppermute | solution.py:709
  74.0 2.8 %collective-permute-done.12.refs_2_ = f32[72,128]{1,0:T(8,128)S(1)} collective-permute-done((f32[72,128]{1,0:T(8,128)}, f32[72,128]{1,0:T(8,128)S(1)}, u32[]{:S(2)}, u32[]{:S(2)}) %collective-permute-start.12) | collective-permute-done | bytes 36896 | tf_op jit(solution)/shard_map/ppermute | solution.py:709
  78.3 1.4 shard_map.146.refs_0_
  79.7 4.5 %collective-permute-start.14 = (f32[72,128]{1,0:T(8,128)}, f32[72,128]{1,0:T(8,128)S(1)}, u32[]{:S(2)}, u32[]{:S(2)}) collective-permute-start(f32[72,128]{1,0:T(8,128)} %shard_map.146.refs_0_), channel_id=1, source_target_pairs={{0,16},{1,17},{2,18},{3,19},{4,20},{5,21},{6,22},{7,23},{8,24},{9,... | collective-permute-start | bytes 110600 | tf_op jit(solution)/shard_map/ppermute | solution.py:709
  84.2 3.6 %collective-permute-done.14.refs_1_ = f32[72,128]{1,0:T(8,128)S(1)} collective-permute-done((f32[72,128]{1,0:T(8,128)}, f32[72,128]{1,0:T(8,128)S(1)}, u32[]{:S(2)}, u32[]{:S(2)}) %collective-permute-start.14) | collective-permute-done | bytes 36896 | tf_op jit(solution)/shard_map/ppermute | solution.py:709
  91.2 2.2 %collective-permute-start.16 = (f32[72,128]{1,0:T(8,128)}, f32[72,128]{1,0:T(8,128)S(1)}, u32[]{:S(2)}, u32[]{:S(2)}) collective-permute-start(f32[72,128]{1,0:T(8,128)} %shard_map.147), channel_id=1, source_target_pairs={{0,8},{1,9},{2,10},{3,11},{4,12},{5,13},{6,14},{7,15},{8,0},{9,1},... | collective-permute-start | bytes 110600 | tf_op jit(solution)/shard_map/ppermute | solution.py:709
  95.2 1.7 %collective-permute-done.16 = f32[72,128]{1,0:T(8,128)S(1)} collective-permute-done((f32[72,128]{1,0:T(8,128)}, f32[72,128]{1,0:T(8,128)S(1)}, u32[]{:S(2)}, u32[]{:S(2)}) %collective-permute-start.16) | collective-permute-done | bytes 36896 | tf_op jit(solution)/shard_map/ppermute | solution.py:709
  98.0 3.6 %collective-permute-start.19 = (f32[288,128]{1,0:T(8,128)S(1)}, f32[288,128]{1,0:T(8,128)S(1)}, u32[]{:S(2)}, u32[]{:S(2)}) collective-permute-start(f32[288,128]{1,0:T(8,128)S(1)} %pad_maximum_fusion), channel_id=1, source_target_pairs={{0,2},{1,3},{2,0},{3,1},{4,6},{5,7},{6,4},{7,5},{8,10},{9,11},{10,... | collective-permute-start | bytes 442376 | tf_op jit(solution)/shard_map/ppermute | solution.py:709
  101.5 5.1 %collective-permute-done.18 = f32[288,128]{1,0:T(8,128)S(1)} collective-permute-done((f32[288,128]{1,0:T(8,128)S(1)}, f32[288,128]{1,0:T(8,128)S(1)}, u32[]{:S(2)}, u32[]{:S(2)}) %collective-permute-start.18) | collective-permute-done | bytes 147488 | tf_op jit(solution)/shard_map/ppermute | solution.py:709
  106.8 2.0 %collective-permute-done.21.far_ref = f32[1152,128]{1,0:T(8,128)S(1)} collective-permute-done((f32[1152,128]{1,0:T(8,128)S(1)}, f32[1152,128]{1,0:T(8,128)S(1)}, u32[]{:S(2)}, u32[]{:S(2)}) %collective-permute-start.21) | collective-permute-done | bytes 589856 | tf_op jit(solution)/shard_map/ppermute | solution.py:709
  109.7 15.7 %shard_map.148 = (f32[1,512]{1,0:T(1,128)}, f32[32,512]{1,0:T(8,128)}, bf16[2176,128]{1,0:T(8,128)(2,1)}, bf16[2176,128]{1,0:T(8,128)(2,1)}, f32[3,512]{1,0:T(4,...) custom-call(s32[5]{0:T(128)} %stack.35.where_ref, f32[1152,128]{1,0:T(8,128)} %copy-done.21, ...), custom_call_target="tpu_custom_call" | custom-call | flops 5000000000 | bytes 4000000 | tf_op jit(solution)/shard_map/pallas_call | solution.py:831
  125.4 7.9 %collective-permute-start.22 = (f32[3,3,256]{2,1,0:T(4,128)}, f32[3,3,256]{2,1,0:T(4,128)S(1)}, u32[]{:S(2)}, u32[]{:S(2)}) collective-permute-start(f32[3,3,256]{2,1,0:T(4,128)} %get-tuple-element.69), channel_id=1, source_target_pairs={{0,31},{1,0},{2,1},{3,2},{4,3},{5,4},{6,5},{7,6},{8,7},{9,8},{10,9... | collective-permute-start | bytes 27656 | tf_op jit(solution)/shard_map/ppermute | solution.py:684
  133.4 1.6 %collective-permute-done.22 = f32[3,3,256]{2,1,0:T(4,128)S(1)} collective-permute-done((f32[3,3,256]{2,1,0:T(4,128)}, f32[3,3,256]{2,1,0:T(4,128)S(1)}, u32[]{:S(2)}, u32[]{:S(2)}) %collective-permute-start.22) | collective-permute-done | bytes 9248 | tf_op jit(solution)/shard_map/ppermute | solution.py:684
  135.0 10.4 %collective-permute-done.23 = f32[3,3,256]{2,1,0:T(4,128)S(1)} collective-permute-done((f32[3,3,256]{2,1,0:T(4,128)}, f32[3,3,256]{2,1,0:T(4,128)S(1)}, u32[]{:S(2)}, u32[]{:S(2)}) %collective-permute-start.23) | collective-permute-done | bytes 9248 | tf_op jit(solution)/shard_map/ppermute | solution.py:684
  146.7 3.5 %collective-permute-start.24 = (f32[3,256]{1,0:T(4,128)S(1)}, f32[3,256]{1,0:T(4,128)S(1)}, u32[]{:S(2)}, u32[]{:S(2)}) collective-permute-start(f32[3,256]{1,0:T(4,128)S(1)} %get-tuple-element.73), channel_id=1, source_target_pairs={{0,224},{32,0},{64,32},{96,64},{128,96},{160,128},{192,160},{224,1... | collective-permute-start | bytes 9224 | tf_op jit(solution)/shard_map/ppermute | solution.py:684
  150.2 6.5 %shard_map.149.base_ref = f32[3,512]{1,0:T(4,128)} custom-call(bf16[2176,128]{1,0:T(8,128)(2,1)} %get-tuple-element.61.va_ref, bf16[2176,128]{1,0:T(8,128)(2,1)} %get-tuple-element.62.vb_ref, f32[2,72,512]{2,1,0:T(8,128)} %get-tuple-element.40.xz_ref, f32[2,72,512]{2,1,0:T(8,128)} %get-tuple-element.63.dx_ref, f32[2,72,512]{2,1,0:T(8,128)} %get-tuple-element.64.dz_ref, ...), custom_call_target="tpu_custom_call" | custom-call | flops 5000000000 | bytes 4000000 | tf_op jit(solution)/shard_map/pallas_call | solution.py:876
  157.4 1.5 shard_map.150
  (101 shorter events, 24.3 us)
Async XLA Ops:
  0.6 3.8 %copy-start = (f32[128,128]{1,0:T(8,128)S(1)}, f32[128,128]{1,0:T(8,128)}, u32[]{:S(2)}) copy-start(f32[128,128]{1,0:T(8,128)} %param.20) | copy-start | bytes 196612
  0.6 3.8 %copy-start.15 = (f32[8,128]{1,0:T(8,128)S(1)}, f32[8,128]{1,0:T(8,128)}, u32[]{:S(2)}) copy-start(f32[8,128]{1,0:T(8,128)} %param.18) | copy-start | bytes 12292
  2.1 7.0 %collective-permute-start.1 = (f32[4,256]{1,0:T(4,128)}, f32[4,256]{1,0:T(4,128)S(1)}, u32[]{:S(2)}, u32[]{:S(2)}) collective-permute-start(f32[4,256]{1,0:T(4,128)} %shard_map.140), channel_id=1, source_target_pairs={{0,224},{32,0},{64,32},{96,64},{128,96},{160,128},{192,160},{224,1... | collective-permute-start | bytes 12296 | tf_op jit(solution)/shard_map/ppermute | solution.py:684
  4.4 5.0 %collective-permute-start = (f32[4,256]{1,0:T(4,128)}, f32[4,256]{1,0:T(4,128)S(1)}, u32[]{:S(2)}, u32[]{:S(2)}) collective-permute-start(f32[4,256]{1,0:T(4,128)} %shard_map.140), channel_id=1, source_target_pairs={{0,32},{32,64},{64,96},{96,128},{128,160},{160,192},{192,224},{224... | collective-permute-start | bytes 12296 | tf_op jit(solution)/shard_map/ppermute | solution.py:684
  9.5 14.8 %copy-start.17 = (f32[3,4,256]{2,1,0:T(4,128)}, f32[3,4,256]{2,1,0:T(4,128)S(1)}, u32[]{:S(2)}) copy-start(f32[3,4,256]{2,1,0:T(4,128)S(1)} %pad_maximum_fusion.1.mid_ref) | copy-start | bytes 36868
  9.5 16.9 %collective-permute-start.3 = (f32[3,4,256]{2,1,0:T(4,128)S(1)}, f32[3,4,256]{2,1,0:T(4,128)S(1)}, u32[]{:S(2)}, u32[]{:S(2)}) collective-permute-start(f32[3,4,256]{2,1,0:T(4,128)S(1)} %pad_maximum_fusion.1.mid_ref), channel_id=1, source_target_pairs={{0,31},{1,0},{2,1},{3,2},{4,3},{5,4},{6,5},{7,6},{8,7},{9,8},{10,9... | collective-permute-start | bytes 36872 | tf_op jit(solution)/shard_map/ppermute | solution.py:684
  18.7 11.8 %collective-permute-start.2 = (f32[3,4,256]{2,1,0:T(4,128)S(1)}, f32[3,4,256]{2,1,0:T(4,128)S(1)}, u32[]{:S(2)}, u32[]{:S(2)}) collective-permute-start(f32[3,4,256]{2,1,0:T(4,128)S(1)} %pad_maximum_fusion.1.mid_ref), channel_id=1, source_target_pairs={{0,1},{1,2},{2,3},{3,4},{4,5},{5,6},{6,7},{7,8},{8,9},{9,10},{10,1... | collective-permute-start | bytes 36872 | tf_op jit(solution)/shard_map/ppermute | solution.py:684
  26.4 4.1 %copy-start.24 = (f32[3,4,256]{2,1,0:T(4,128)}, f32[3,4,256]{2,1,0:T(4,128)S(1)}, u32[]{:S(2)}) copy-start(f32[3,4,256]{2,1,0:T(4,128)S(1)} %collective-permute-done.3.next_ref) | copy-start | bytes 36868
  42.1 2.2 %collective-permute-start.4 = (f32[1152,128]{1,0:T(8,128)}, f32[1152,128]{1,0:T(8,128)S(1)}, u32[]{:S(2)}, u32[]{:S(2)}) collective-permute-start(f32[1152,128]{1,0:T(8,128)} %get-tuple-element.44), channel_id=1, source_target_pairs={{0,32},{1,33},{2,34},{3,35},{4,36},{5,37},{6,38},{7,39},{8,40},{9,... | collective-permute-start | bytes 1769480 | tf_op jit(solution)/shard_map/ppermute | solution.py:709
  47.2 10.5 %collective-permute-start.5 = (f32[288,128]{1,0:T(8,128)}, f32[288,128]{1,0:T(8,128)S(1)}, u32[]{:S(2)}, u32[]{:S(2)}) collective-permute-start(f32[288,128]{1,0:T(8,128)} %get-tuple-element.46), channel_id=1, source_target_pairs={{0,1},{1,2},{2,3},{3,0},{4,5},{5,6},{6,7},{7,4},{8,9},{9,10},{10,1... | collective-permute-start | bytes 442376 | tf_op jit(solution)/shard_map/ppermute | solution.py:709
  47.2 10.5 %collective-permute-start.6 = (f32[288,128]{1,0:T(8,128)}, f32[288,128]{1,0:T(8,128)S(1)}, u32[]{:S(2)}, u32[]{:S(2)}) collective-permute-start(f32[288,128]{1,0:T(8,128)} %get-tuple-element.47), channel_id=1, source_target_pairs={{0,2},{1,3},{2,0},{3,1},{4,6},{5,7},{6,4},{7,5},{8,10},{9,11},{10,... | collective-permute-start | bytes 442376 | tf_op jit(solution)/shard_map/ppermute | solution.py:709
  47.2 11.1 %collective-permute-start.7 = (f32[288,128]{1,0:T(8,128)}, f32[288,128]{1,0:T(8,128)S(1)}, u32[]{:S(2)}, u32[]{:S(2)}) collective-permute-start(f32[288,128]{1,0:T(8,128)} %get-tuple-element.48), channel_id=1, source_target_pairs={{0,3},{1,0},{2,1},{3,2},{4,7},{5,4},{6,5},{7,6},{8,11},{9,8},{10,9... | collective-permute-start | bytes 442376 | tf_op jit(solution)/shard_map/ppermute | solution.py:709
  60.8 5.4 %collective-permute-start.8 = (f32[72,128]{1,0:T(8,128)}, f32[72,128]{1,0:T(8,128)S(1)}, u32[]{:S(2)}, u32[]{:S(2)}) collective-permute-start(f32[72,128]{1,0:T(8,128)} %get-tuple-element.50), channel_id=1, source_target_pairs={{0,4},{1,5},{2,6},{3,7},{4,8},{5,9},{6,10},{7,11},{8,12},{9,13},{1... | collective-permute-start | bytes 110600 | tf_op jit(solution)/shard_map/ppermute | solution.py:709
  60.8 5.8 %collective-permute-start.9 = (f32[72,128]{1,0:T(8,128)}, f32[72,128]{1,0:T(8,128)S(1)}, u32[]{:S(2)}, u32[]{:S(2)}) collective-permute-start(f32[72,128]{1,0:T(8,128)} %get-tuple-element.51), channel_id=1, source_target_pairs={{0,8},{1,9},{2,10},{3,11},{4,12},{5,13},{6,14},{7,15},{8,0},{9,1},... | collective-permute-start | bytes 110600 | tf_op jit(solution)/shard_map/ppermute | solution.py:709
  62.6 4.8 %collective-permute-start.10 = (f32[72,128]{1,0:T(8,128)}, f32[72,128]{1,0:T(8,128)S(1)}, u32[]{:S(2)}, u32[]{:S(2)}) collective-permute-start(f32[72,128]{1,0:T(8,128)} %get-tuple-element.52), channel_id=1, source_target_pairs={{0,12},{1,13},{2,14},{3,15},{4,0},{5,1},{6,2},{7,3},{8,4},{9,5},{1... | collective-permute-start | bytes 110600 | tf_op jit(solution)/shard_map/ppermute | solution.py:709
  69.4 4.6 %collective-permute-start.13 = (f32[72,128]{1,0:T(8,128)}, f32[72,128]{1,0:T(8,128)S(1)}, u32[]{:S(2)}, u32[]{:S(2)}) collective-permute-start(f32[72,128]{1,0:T(8,128)} %shard_map.145.refs_0_), channel_id=1, source_target_pairs={{0,192},{1,193},{2,194},{3,195},{4,196},{5,197},{6,198},{7,199},{8... | collective-permute-start | bytes 110600 | tf_op jit(solution)/shard_map/ppermute | solution.py:709
  71.7 5.1 %collective-permute-start.12 = (f32[72,128]{1,0:T(8,128)}, f32[72,128]{1,0:T(8,128)S(1)}, u32[]{:S(2)}, u32[]{:S(2)}) collective-permute-start(f32[72,128]{1,0:T(8,128)} %shard_map.145.refs_0_), channel_id=1, source_target_pairs={{0,128},{1,129},{2,130},{3,131},{4,132},{5,133},{6,134},{7,135},{8... | collective-permute-start | bytes 110600 | tf_op jit(solution)/shard_map/ppermute | solution.py:709
  71.7 6.0 %collective-permute-start.11 = (f32[72,128]{1,0:T(8,128)}, f32[72,128]{1,0:T(8,128)S(1)}, u32[]{:S(2)}, u32[]{:S(2)}) collective-permute-start(f32[72,128]{1,0:T(8,128)} %shard_map.145.refs_0_), channel_id=1, source_target_pairs={{0,64},{1,65},{2,66},{3,67},{4,68},{5,69},{6,70},{7,71},{8,72},{9,... | collective-permute-start | bytes 110600 | tf_op jit(solution)/shard_map/ppermute | solution.py:709
  74.0 3.7 %copy-start.10 = (f32[72,128]{1,0:T(8,128)}, f32[72,128]{1,0:T(8,128)S(1)}, u32[]{:S(2)}) copy-start(f32[72,128]{1,0:T(8,128)S(1)} %collective-permute-done.13.refs_3_) | copy-start | bytes 110596
  79.7 8.1 %collective-permute-start.14 = (f32[72,128]{1,0:T(8,128)}, f32[72,128]{1,0:T(8,128)S(1)}, u32[]{:S(2)}, u32[]{:S(2)}) collective-permute-start(f32[72,128]{1,0:T(8,128)} %shard_map.146.refs_0_), channel_id=1, source_target_pairs={{0,16},{1,17},{2,18},{3,19},{4,20},{5,21},{6,22},{7,23},{8,24},{9,... | collective-permute-start | bytes 110600 | tf_op jit(solution)/shard_map/ppermute | solution.py:709
  89.8 7.8 %copy-start.2 = (f32[72,128]{1,0:T(8,128)S(1)}, f32[72,128]{1,0:T(8,128)}, u32[]{:S(2)}) copy-start(f32[72,128]{1,0:T(8,128)} %shard_map.147) | copy-start | bytes 110596
  89.8 5.4 %collective-permute-start.17 = (f32[72,128]{1,0:T(8,128)}, f32[72,128]{1,0:T(8,128)S(1)}, u32[]{:S(2)}, u32[]{:S(2)}) collective-permute-start(f32[72,128]{1,0:T(8,128)} %shard_map.147), channel_id=1, source_target_pairs={{0,4},{1,5},{2,6},{3,7},{4,8},{5,9},{6,10},{7,11},{8,12},{9,13},{1... | collective-permute-start | bytes 110600 | tf_op jit(solution)/shard_map/ppermute | solution.py:709
  91.2 5.7 %collective-permute-start.16 = (f32[72,128]{1,0:T(8,128)}, f32[72,128]{1,0:T(8,128)S(1)}, u32[]{:S(2)}, u32[]{:S(2)}) collective-permute-start(f32[72,128]{1,0:T(8,128)} %shard_map.147), channel_id=1, source_target_pairs={{0,8},{1,9},{2,10},{3,11},{4,12},{5,13},{6,14},{7,15},{8,0},{9,1},... | collective-permute-start | bytes 110600 | tf_op jit(solution)/shard_map/ppermute | solution.py:709
  93.5 4.2 %collective-permute-start.15 = (f32[72,128]{1,0:T(8,128)}, f32[72,128]{1,0:T(8,128)S(1)}, u32[]{:S(2)}, u32[]{:S(2)}) collective-permute-start(f32[72,128]{1,0:T(8,128)} %shard_map.147), channel_id=1, source_target_pairs={{0,12},{1,13},{2,14},{3,15},{4,0},{5,1},{6,2},{7,3},{8,4},{9,5},{1... | collective-permute-start | bytes 110600 | tf_op jit(solution)/shard_map/ppermute | solution.py:709
  97.7 9.1 %collective-permute-start.20 = (f32[288,128]{1,0:T(8,128)S(1)}, f32[288,128]{1,0:T(8,128)S(1)}, u32[]{:S(2)}, u32[]{:S(2)}) collective-permute-start(f32[288,128]{1,0:T(8,128)S(1)} %pad_maximum_fusion), channel_id=1, source_target_pairs={{0,1},{1,2},{2,3},{3,0},{4,5},{5,6},{6,7},{7,4},{8,9},{9,10},{10,1... | collective-permute-start | bytes 442376 | tf_op jit(solution)/shard_map/ppermute | solution.py:709
  98.0 8.7 %collective-permute-start.19 = (f32[288,128]{1,0:T(8,128)S(1)}, f32[288,128]{1,0:T(8,128)S(1)}, u32[]{:S(2)}, u32[]{:S(2)}) collective-permute-start(f32[288,128]{1,0:T(8,128)S(1)} %pad_maximum_fusion), channel_id=1, source_target_pairs={{0,2},{1,3},{2,0},{3,1},{4,6},{5,7},{6,4},{7,5},{8,10},{9,11},{10,... | collective-permute-start | bytes 442376 | tf_op jit(solution)/shard_map/ppermute | solution.py:709
  101.5 5.1 %collective-permute-start.18 = (f32[288,128]{1,0:T(8,128)S(1)}, f32[288,128]{1,0:T(8,128)S(1)}, u32[]{:S(2)}, u32[]{:S(2)}) collective-permute-start(f32[288,128]{1,0:T(8,128)S(1)} %pad_maximum_fusion), channel_id=1, source_target_pairs={{0,3},{1,0},{2,1},{3,2},{4,7},{5,4},{6,5},{7,6},{8,11},{9,8},{10,9... | collective-permute-start | bytes 442376 | tf_op jit(solution)/shard_map/ppermute | solution.py:709
  106.7 2.1 %collective-permute-start.21 = (f32[1152,128]{1,0:T(8,128)S(1)}, f32[1152,128]{1,0:T(8,128)S(1)}, u32[]{:S(2)}, u32[]{:S(2)}) collective-permute-start(f32[1152,128]{1,0:T(8,128)S(1)} %constant_dynamic-update-slice_fusion.near_ref), channel_id=1, source_target_pairs={{0,32},{1,33},{2,34},{3,35},{4,36},{5,37},{6,38},{7,39},{8,40},{9,... | collective-permute-start | bytes 1769480 | tf_op jit(solution)/shard_map/ppermute | solution.py:709
  125.4 9.6 %collective-permute-start.22 = (f32[3,3,256]{2,1,0:T(4,128)}, f32[3,3,256]{2,1,0:T(4,128)S(1)}, u32[]{:S(2)}, u32[]{:S(2)}) collective-permute-start(f32[3,3,256]{2,1,0:T(4,128)} %get-tuple-element.69), channel_id=1, source_target_pairs={{0,31},{1,0},{2,1},{3,2},{4,3},{5,4},{6,5},{7,6},{8,7},{9,8},{10,9... | collective-permute-start | bytes 27656 | tf_op jit(solution)/shard_map/ppermute | solution.py:684
  133.4 12.0 %collective-permute-start.23 = (f32[3,3,256]{2,1,0:T(4,128)}, f32[3,3,256]{2,1,0:T(4,128)S(1)}, u32[]{:S(2)}, u32[]{:S(2)}) collective-permute-start(f32[3,3,256]{2,1,0:T(4,128)} %get-tuple-element.70), channel_id=1, source_target_pairs={{0,1},{1,2},{2,3},{3,4},{4,5},{5,6},{6,7},{7,8},{8,9},{9,10},{10,1... | collective-permute-start | bytes 27656 | tf_op jit(solution)/shard_map/ppermute | solution.py:684
  146.7 10.1 %collective-permute-start.25 = (f32[3,256]{1,0:T(4,128)S(1)}, f32[3,256]{1,0:T(4,128)S(1)}, u32[]{:S(2)}, u32[]{:S(2)}) collective-permute-start(f32[3,256]{1,0:T(4,128)S(1)} %get-tuple-element.72), channel_id=1, source_target_pairs={{0,32},{32,64},{64,96},{96,128},{128,160},{160,192},{192,224},{224... | collective-permute-start | bytes 9224 | tf_op jit(solution)/shard_map/ppermute | solution.py:684
  146.7 10.1 %collective-permute-start.24 = (f32[3,256]{1,0:T(4,128)S(1)}, f32[3,256]{1,0:T(4,128)S(1)}, u32[]{:S(2)}, u32[]{:S(2)}) collective-permute-start(f32[3,256]{1,0:T(4,128)S(1)} %get-tuple-element.73), channel_id=1, source_target_pairs={{0,224},{32,0},{64,32},{96,64},{128,96},{160,128},{192,160},{224,1... | collective-permute-start | bytes 9224 | tf_op jit(solution)/shard_map/ppermute | solution.py:684
  (20 other events, 16.4 us)

commit v2 on v1

v2 whole, which is shorter than its diff:
```python
import functools

import jax
import jax.numpy as jnp
from jax import lax
from jax.experimental import pallas as pl
from jax.experimental.pallas import tpu as pltpu
from jax.sharding import PartitionSpec as P

NB = 8
NS = 8
HIGHEST = lax.Precision.HIGHEST
TWO_PI = 6.283185307179586
BOX_HEIGHT = 4.0
SPLITTING = 2.5
SOFTENING = 0.01
CENTRE_STEP = 0.3
AXES = ("gx", "gy")

HX = 9
LZ = 4
NY = 32
XF = 2 * HX - 1
XROWS = 24
SLAB = XF * 32
UNIT_ROW = LZ * SLAB
TOTAL_ROW = UNIT_ROW + LZ * XROWS
ROWS = TOTAL_ROW + 32

F32 = jnp.float32
BF16 = jnp.bfloat16
NT = (((1,), (1,)), ((), ()))
NN = (((1,), (0,)), ((), ()))


def mm(a, b, dims=NN, precision=None):
    return lax.dot_general(a, b, dims, precision=precision, preferred_element_type=F32)


def parts(x):
    high = x.astype(BF16)
    return high, (x - high.astype(F32)).astype(BF16)


def mm3(a, b, dims=NN):
    a_high, a_low = parts(a)
    b_high, b_low = parts(b)
    return mm(a_high, b_high, dims) + (mm(a_low, b_high, dims) + mm(a_high, b_low, dims))


def cos_turns(t):
    r = t - jnp.floor(t + 0.5)
    s = (0.25 - jnp.abs(r)) * TWO_PI
    q = s * s
    p = -2.5052108e-08 + q * 1.6059044e-10
    p = 2.7557319e-06 + q * p
    p = -1.9841270e-04 + q * p
    p = 8.3333333e-03 + q * p
    p = -1.6666667e-01 + q * p
    return s + s * (q * p)


def silu_parts(x):
    gate = 1.0 / (1.0 + jnp.exp(-x))
    return x * gate, gate * (1.0 + x * (1.0 - gate))


def iota(shape, dim):
    return lax.broadcasted_iota(jnp.int32, shape, dim)


def call(kernel, outs, scratch=(), spaces="", flops=0, nbytes=0, vmem=56):
    known = {"s": pltpu.SMEM, "v": pltpu.VMEM, "a": pl.ANY, "h": pltpu.HBM}
    return pl.pallas_call(
        kernel,
        in_specs=[pl.BlockSpec(memory_space=known[letter]) for letter in spaces],
        out_shape=[jax.ShapeDtypeStruct(s, d) for s, d in outs],
        scratch_shapes=list(scratch),
        compiler_params=pltpu.CompilerParams(vmem_limit_bytes=vmem * 2**20),
        cost_estimate=pl.CostEstimate(flops=flops, bytes_accessed=nbytes, transcendentals=0),
    )


def border_kernel(pos_ref, species_ref, ghost_ref, out_ref, tab_ref):
    atoms = pos_ref.shape[1]
    tab_ref[0:3, :] = pos_ref[...]
    tab_ref[3:4, :] = species_ref[...].astype(F32)
    for part in range(ghost_ref.shape[1] // 128):
        lanes = pl.ds(128 * part, 128)
        index = jnp.broadcast_to(ghost_ref[:, lanes], (8, 128))
        high, low = index >> 7, index & 127
        value = jnp.zeros((8, 128), F32)
        for block in range(atoms // 128):
            source = tab_ref[:, pl.ds(128 * block, 128)]
            value = jnp.where(high == block, jnp.take_along_axis(source, low, axis=1), value)
        out_ref[:, lanes] = value[0:4]


def waves(grid, where_ref, pos_ref):
    extent_x, extent_y = grid
    atoms = pos_ref.shape[1]
    u, v = where_ref[0], where_ref[1]
    x, y, z = pos_ref[0:1, :], pos_ref[1:2, :], pos_ref[2:3, :]

    row = iota((XROWS, atoms), 0)
    order = jnp.where(row < HX, row, row - (HX - 1))
    whole = lax.rem(order * u, extent_x).astype(F32)
    order = order.astype(F32)
    turn_x = (order * x + whole) / extent_x - jnp.where(row < HX, 0.0, 0.25)
    rate_x = jnp.where(row < XF, order * (TWO_PI / extent_x), 0.0)

    row = iota((2 * LZ, atoms), 0)
    whole = lax.rem(v, 2 * extent_y).astype(F32)
    turn_z = ((row >> 1) + 1).astype(F32) * z * (1.0 / BOX_HEIGHT) - (y + whole) * (0.5 / extent_y)
    turn_z = turn_z - 0.25 * (row & 1).astype(F32)

    row = iota((2 * NY, atoms), 0)
    twice = 2 * (row & (NY - 1)) + 1
    whole = lax.rem(twice * v, 2 * extent_y).astype(F32)
    twice = twice.astype(F32)
    turn_y = (twice * y + whole) * (0.5 / extent_y) - jnp.where(row < NY, 0.0, 0.25)
    return turn_x, rate_x, turn_z, turn_y, twice * (0.5 * TWO_PI / extent_y)


def prepare_kernel(
    grid,
    where_ref,
    pos_ref,
    embed_ref,
    radial_ref,
    message_ref,
    x_out,
    zy_out,
    unit_out,
    wide_out,
    embed_out,
    message_out,
):
    turn_x, _, turn_z, turn_y, _ = waves(grid, where_ref, pos_ref)
    fx = jnp.where(iota(turn_x.shape, 0) < XF, cos_turns(turn_x), 0.0)
    fz, fy = cos_turns(turn_z), cos_turns(turn_y)
    x_out[...] = fx

    for l in range(LZ):
        zy = jnp.concatenate([fz[2 * l : 2 * l + 1] * fy, fz[2 * l + 1 : 2 * l + 2] * fy], axis=0)
        high, low = parts(zy)
        zy_out[0, 128 * l : 128 * l + 128] = high
        zy_out[1, 128 * l : 128 * l + 128] = low
        unit_out[l] = mm(fx, zy, NT, HIGHEST)

    embed = embed_ref[...].T
    message = mm(message_ref[...].T, embed, NN, HIGHEST)
    embed_out[...] = embed
    message_out[...] = message
    col = iota((NB, 512), 1)
    sub = iota((NB, 512), 0)
    pick_b = ((col >> 6) == sub).astype(F32)
    pick_s = (((col >> 3) & 7) == sub).astype(F32)
    spread = mm(message, pick_s, NN, HIGHEST)
    radial = radial_ref[...].T
    channels = message.shape[0]
    for which in range(2):
        wide = mm(radial[which * channels : (which + 1) * channels], pick_b, NN, HIGHEST) * spread
        high, low = parts(wide)
        wide_out[which, 0:channels] = high
        wide_out[which, channels:] = low


def later_kernel(
    grid,
    atoms_all,
    where_ref,
    pos_ref,
    wave_ref,
    radial_ref,
    message_ref,
    charge_ref,
    table_out,
    narrow_out,
    charge_out,
    dx_out,
    z_out,
    dz_out,
    y_out,
    dy_out,
):
    extent_x, extent_y = grid
    turn_x, rate_x, turn_z, turn_y, rate_y = waves(grid, where_ref, pos_ref)
    dx_out[...] = cos_turns(turn_x + 0.25) * rate_x
    z_out[...] = cos_turns(turn_z)
    dz_out[...] = cos_turns(turn_z + 0.25)
    y_out[...] = cos_turns(turn_y)
    dy_out[...] = cos_turns(turn_y + 0.25) * rate_y

    step = wave_ref.shape[1]
    order = iota((40, step), 0)
    along_x, along_y, along_z = wave_ref[0:1, :], wave_ref[1:2, :], wave_ref[2:3, :]
    matches_z = ((order & 3) + 1 == along_z) & (order < HX * LZ)
    plus = matches_z & ((order >> 2) == along_x)
    minus = matches_z & ((order >> 2) == -along_x) & (order >= LZ)
    lanes = iota((NY, step), 0)
    up = (lanes == along_y).astype(F32).astype(BF16)
    down = (-lanes - 1 == along_y).astype(F32).astype(BF16)
    both = jnp.concatenate([up] * 4 + [down] * 4, axis=0)
    plus = mm(plus.astype(F32).astype(BF16), both, NT)
    minus = mm(minus.astype(F32).astype(BF16), both, NT)
    order = iota((40, 128), 0)
    lanes = iota((40, 128), 1)
    wave_b = (lanes & (NY - 1)).astype(F32)
    kx = (order >> 2).astype(F32) * (TWO_PI / extent_x)
    kz = ((order & 3) + 1).astype(F32) * (TWO_PI / BOX_HEIGHT)

    def weights(ky):
        squared = kx * kx + ky * ky + kz * kz
        return jnp.exp(-squared / (4.0 * SPLITTING**2)) / squared / atoms_all

    green_up = weights(wave_b * (TWO_PI / extent_y))
    green_down = weights((wave_b + 1.0) * (TWO_PI / extent_y))
    pp, pm = green_up * plus[:, 0:128], green_down * plus[:, 128:256]
    mp, mn = green_up * minus[:, 0:128], green_down * minus[:, 128:256]
    quarter = lanes >> 5
    sign_t = jnp.where((quarter == 1) | (quarter == 2), 1.0, -1.0)
    sign_st = jnp.where((quarter & 1) == 1, 1.0, -1.0)
    sign_s = jnp.where(quarter >= 2, 1.0, -1.0)
    table_out[0] = (pp + pm) + (mp + mn)
    table_out[1] = sign_t * ((pp - pm) + (mp - mn))
    table_out[2] = sign_st * ((pp - pm) - (mp - mn))
    table_out[3] = sign_s * ((pp + pm) - (mp + mn))

    col = iota((NB, 64), 1)
    sub = iota((NB, 64), 0)
    pick_b = ((col >> 3) == sub).astype(F32)
    pick_s = ((col & 7) == sub).astype(F32)
    message = message_ref[...]
    channels = message.shape[0]
    radial = radial_ref[...].T
    spread = mm(message, pick_s, NN, HIGHEST)
    for which in range(2):
        narrow = mm(radial[which * channels : (which + 1) * channels], pick_b, NN, HIGHEST) * spread
        narrow_out[which] = narrow.T
    charge_out[...] = charge_ref[...].T


def basis_terms(dist, rho, live):
    envelope = jnp.exp(-0.25 * rho) * live
    out = []
    for b in range(NB):
        off = dist - CENTRE_STEP * b
        out.append((jnp.exp(off * off * (-0.5 / CENTRE_STEP**2)) * envelope, off))
    return out


def forward_kernel(
    where_ref,
    pos_ref,
    species_ref,
    mid_ref,
    first_ref,
    second_ref,
    nbr_ref,
    embed_ref,
    wide_ref,
    scalar_ref,
    vector_ref,
    hidden_ref,
    readout_ref,
    weight_ref,
    x_ref,
    zy_ref,
    unit_ref,
    energy_out,
    charge_out,
    hbar_out,
    slope_out,
    vsum_out,
    geo_out,
    keep_out,
    send_out,
    tab_ref,
    moment_ref,
    qh_ref,
    ql_ref,
    pay_ref,
    halo_ref,
    sems,
):
    atoms = pos_ref.shape[1]
    tiles = atoms // 128
    copies = [
        pltpu.make_async_copy(ref, halo_ref.at[n], sems.at[n]) for n, ref in enumerate((mid_ref, first_ref, second_ref))
    ]
    for copy in copies:
        copy.start()
    for c in range(3):
        for j in range(tiles):
            tab_ref[c, j : j + 1, :] = pos_ref[c : c + 1, pl.ds(128 * j, 128)]
    for j in range(tiles):
        tab_ref[3, j : j + 1, :] = species_ref[:, pl.ds(128 * j, 128)].astype(F32)
    for copy in copies:
        copy.wait()
    even = (where_ref[1] & 1) == 0
    for i in range(3):
        first, second = halo_ref[1, i], halo_ref[2, i]
        prev, after = jnp.where(even, second, first), jnp.where(even, first, second)
        for j, block in enumerate((prev, halo_ref[0, i], after)):
            shifts = (i - 1.0, j - 1.0, 0.0, 0.0)
            for c in range(4):
                for h in range(2):
                    at = tiles + 2 * (3 * i + j) + h
                    tab_ref[c, at : at + 1, :] = block[c : c + 1, 128 * h : 128 * h + 128] + shifts[c]

    def lane_tile(t, carry):
        lanes = pl.ds(pl.multiple_of(t * 128, 128), 128)
        for tile in range(4):
            index = nbr_ref[pl.ds(8 * tile, 8), lanes]
            live = (index >= 0).astype(F32)
            index = jnp.maximum(index, 0)
            high, low = index >> 7, index & 127
            value = [jnp.zeros((8, 128), F32) for _ in range(4)]
            for block in range(tiles + 18):
                if block // 2 == tiles // 2 + 4:
                    continue
                here = high == block
                for c in range(4):
                    source = jnp.broadcast_to(tab_ref[c, block : block + 1, :], (8, 128))
                    value[c] = jnp.where(here, jnp.take_along_axis(source, low, axis=1), value[c])
            rx, ry, rz = (value[c] - pos_ref[c : c + 1, lanes] for c in range(3))
            rho = rx * rx + ry * ry + rz * rz
            dist = jnp.sqrt(rho + SOFTENING)
            inv = 1.0 / dist
            rows = pl.ds(8 * tile, 8)
            geo_out[0, rows, lanes] = rx * inv
            geo_out[1, rows, lanes] = ry * inv
            geo_out[2, rows, lanes] = rz * inv
            geo_out[3, rows, lanes] = dist
            geo_out[4, rows, lanes] = rho
            geo_out[5, rows, lanes] = value[3]
            geo_out[6, rows, lanes] = live
        dist = geo_out[3, :, lanes]
        terms = basis_terms(dist, geo_out[4, :, lanes], geo_out[6, :, lanes])
        kind = geo_out[5, :, lanes]
        for f in range(4):
            for b in range(NB):
                value = terms[b][0] if f == 0 else terms[b][0] * geo_out[f - 1, :, lanes]
                for s in range(NS):
                    chosen = jnp.where(kind == float(s), value, 0.0)
                    total = (chosen[0:8] + chosen[8:16]) + (chosen[16:24] + chosen[24:32])
                    moment_ref[f, pl.ds(8 * (8 * b + s), 8), lanes] = total
        return carry

    lax.fori_loop(0, tiles, lane_tile, 0, unroll=2)

    def gathered(f):
        wide = wide_ref[0 if f == 0 else 1]
        high, low = parts(moment_ref[f])
        both = mm(wide, high)
        return both[0:128] + both[128:256] + mm(wide[0:128], low)

    scalar_sum = gathered(0)
    norm = None
    for c in range(3):
        vector = gathered(c + 1)
        vsum_out[c] = vector
        norm = vector * vector if norm is None else norm + vector * vector
    update = mm3(scalar_ref[...].T, scalar_sum) + mm3(vector_ref[...].T, norm)
    feature = jnp.zeros_like(update)
    kinds = species_ref[...]
    for s in range(NS):
        feature = jnp.where(kinds == s, embed_ref[:, s : s + 1], feature)
    act, slope = silu_parts(update)
    slope_out[...] = slope
    hidden = feature + act
    act, slope = silu_parts(mm3(hidden_ref[...].T, hidden))
    readout = jnp.broadcast_to(readout_ref[...], (8, 128)).T[:, 0:1]
    energy_out[...] = jnp.sum(act * readout, axis=0, keepdims=True)
    hbar_out[...] = mm3(hidden_ref[...], slope * readout)
    charges = mm3(weight_ref[...], hidden)
    charge_out[...] = charges

    total = jnp.sum(charges, axis=1, keepdims=True)
    local = total * (1.0 / atoms)
    centred = charges - local
    for k in range(XF):
        high, low = parts(centred * x_ref[k : k + 1, :])
        qh_ref[32 * k : 32 * k + 32, :] = high
        ql_ref[32 * k : 32 * k + 32, :] = low
    high, low = qh_ref[...], ql_ref[...]
    for l in range(LZ):
        near, rest = (zy_ref[part, 128 * l : 128 * l + 128, :] for part in range(2))
        slab = mm(high, near, NT) + (mm(low, near, NT) + mm(high, rest, NT))
        unit = unit_ref[l]
        for k in range(XF):
            at = SLAB * l + 32 * k
            pay_ref[at : at + 32, :] = slab[32 * k : 32 * k + 32] + local * unit[k : k + 1]
        pay_ref[UNIT_ROW + XROWS * l : UNIT_ROW + XROWS * (l + 1), :] = unit
    pay_ref[TOTAL_ROW : TOTAL_ROW + 32, :] = jnp.broadcast_to(total, (32, 128))
    half = ROWS // 2
    core = where_ref[0] & 1
    keep_out[...] = pay_ref[pl.ds(pl.multiple_of(core * half, 8), half), :]
    send_out[...] = pay_ref[pl.ds(pl.multiple_of((1 - core) * half, 8), half), :]


def quarters(x, which):
    lane = iota(x.shape, 1)
    if which == 2:
        return pltpu.roll(x, 64, 1)
    even = ((lane >> 5) & 1) == 0
    if which == 1:
        return jnp.where(even, pltpu.roll(x, 96, 1), pltpu.roll(x, 32, 1))
    return jnp.where(even, pltpu.roll(x, 32, 1), pltpu.roll(x, 96, 1))


def backward_kernel(
    atoms_all,
    where_ref,
    near_ref,
    far_ref,
    table_ref,
    x_ref,
    zy_ref,
    energy_ref,
    charge_ref,
    hbar_ref,
    slope_ref,
    vsum_ref,
    geo_ref,
    nbr_ref,
    scalar_ref,
    vector_ref,
    weight_ref,
    narrow_ref,
    site_out,
    neutral_out,
    vh_out,
    vl_out,
    own_out,
    mid_out,
    first_out,
    second_out,
    sum_ref,
    g_ref,
    rbar_ref,
):
    atoms = nbr_ref.shape[1]
    tiles = atoms // 128
    half = ROWS // 2
    core = where_ref[0] & 1
    sum_ref[pl.ds(pl.multiple_of(core * half, 8), half), :] = near_ref[...]
    sum_ref[pl.ds(pl.multiple_of((1 - core) * half, 8), half), :] = far_ref[...]
    mean = sum_ref[TOTAL_ROW : TOTAL_ROW + 32, :] * (1.0 / atoms_all)

    def put(l, k, value):
        rows = pl.ds(pl.multiple_of(k * 32, 32), 32)
        high, low = parts(value)
        vh_out[rows, 128 * l : 128 * l + 128] = high
        vl_out[rows, 128 * l : 128 * l + 128] = low

    def tile_of(l, k):
        unit = sum_ref[pl.ds(UNIT_ROW + XROWS * l + k, 1), :]
        rows = pl.ds(pl.multiple_of(SLAB * l + k * 32, 32), 32)
        return sum_ref[rows, :] - mean * unit, unit

    overlap = jnp.zeros((32, 128), F32)
    for l in range(LZ):
        cos_tile, unit = tile_of(l, 0)
        g0 = table_ref[0, l : l + 1, :]
        gt = table_ref[1, l : l + 1, :]
        value = g0 * cos_tile + gt * quarters(cos_tile, 3)
        overlap = overlap + value * unit
        put(l, 0, value)

    def mix(a, overlap):
        for l in range(LZ):
            cos_tile, cos_unit = tile_of(l, a)
            sin_tile, sin_unit = tile_of(l, a + HX - 1)
            g0, gt, gst, gs = (table_ref[n, pl.ds(a * LZ + l, 1), :] for n in range(4))
            value = (g0 * cos_tile + gt * quarters(cos_tile, 3)) + (
                gst * quarters(sin_tile, 1) + gs * quarters(sin_tile, 2)
            )
            overlap = overlap + value * cos_unit
            put(l, a, value)
            value = (g0 * sin_tile + gt * quarters(sin_tile, 3)) - (
                gst * quarters(cos_tile, 1) + gs * quarters(cos_tile, 2)
            )
            overlap = overlap + value * sin_unit
            put(l, a + HX - 1, value)
        return overlap

    overlap = lax.fori_loop(1, HX, mix, overlap, unroll=4)
    potential_mean = jnp.sum(overlap, axis=1, keepdims=True) * (1.0 / atoms_all)

    spread = mm(vh_out[...], zy_ref[0]) + (mm(vl_out[...], zy_ref[0]) + mm(vh_out[...], zy_ref[1]))
    potential = jnp.zeros((32, atoms), F32)
    for k in range(XF):
        potential = potential + x_ref[k : k + 1, :] * spread[32 * k : 32 * k + 32]
    neutral = charge_ref[...] - mean[:, 0:1]
    neutral_out[...] = neutral
    site_out[...] = energy_ref[...] + jnp.sum(neutral * potential, axis=0, keepdims=True)
    charge_bar = 2.0 * (potential - potential_mean)
    update_bar = (hbar_ref[...] + mm3(weight_ref[...], charge_bar)) * slope_ref[...]
    scalar_bar = mm3(scalar_ref[...], update_bar)
    norm_bar = 2.0 * mm3(vector_ref[...], update_bar)
    g_ref[0] = mm3(narrow_ref[0], scalar_bar)
    for c in range(3):
        g_ref[c + 1] = mm3(narrow_ref[1], vsum_ref[c] * norm_bar)

    def slots(t, carry):
        lanes = pl.ds(pl.multiple_of(t * 128, 128), 128)
        own = [jnp.zeros((8, 128), F32) for _ in range(3)]
        for tile in range(4):
            rows = pl.ds(8 * tile, 8)
            unit = [geo_ref[c, rows, lanes] for c in range(3)]
            dist = geo_ref[3, rows, lanes]
            kind = geo_ref[5, rows, lanes].astype(jnp.int32)
            terms = basis_terms(dist, geo_ref[4, rows, lanes], geo_ref[6, rows, lanes])
            inv = 1.0 / dist
            ubar = [jnp.zeros((8, 128), F32) for _ in range(3)]
            plain = jnp.zeros((8, 128), F32)
            tilted = jnp.zeros((8, 128), F32)
            for b in range(NB):
                value, off = terms[b]
                picked = [
                    jnp.take_along_axis(g_ref[f, 8 * b : 8 * b + 8, lanes], kind, axis=0) for f in range(4)
                ]
                bar = picked[0]
                for c in range(3):
                    bar = bar + unit[c] * picked[c + 1]
                    ubar[c] = ubar[c] + value * picked[c + 1]
                bar = bar * value
                plain = plain + bar
                tilted = tilted + bar * off
            along = ubar[0] * unit[0] + ubar[1] * unit[1] + ubar[2] * unit[2]
            dist_bar = tilted * (-1.0 / CENTRE_STEP**2) - along * inv
            radial = dist * (2.0 * (-0.25 * plain) + dist_bar * inv)
            for c in range(3):
                bar = ubar[c] * inv + unit[c] * radial
                rbar_ref[c, rows, lanes] = bar
                own[c] = own[c] + bar
        for c in range(3):
            own_out[c : c + 1, lanes] = -jnp.sum(own[c], axis=0, keepdims=True)
        return carry

    lax.fori_loop(0, tiles, slots, 0)

    block_rows = 24
    rows_high = iota((block_rows, atoms), 0)
    rows_low = iota((128, atoms), 0)

    def scatter(s, total):
        index = jnp.maximum(nbr_ref[pl.ds(s, 1), :], 0)
        at_high = rows_high == (index >> 7)
        at_low = jnp.where(rows_low == (index & 127), 1.0, 0.0).astype(BF16)
        pieces = []
        for c in range(3):
            value = rbar_ref[c, pl.ds(s, 1), :]
            high = value.astype(BF16).astype(F32)
            pieces.append(jnp.where(at_high, high, 0.0))
            pieces.append(jnp.where(at_high, value - high, 0.0))
        left = jnp.concatenate(pieces, axis=0).astype(BF16)
        return total + mm(left, at_low, NT)

    even = (where_ref[1] & 1) == 0
    total = lax.fori_loop(0, nbr_ref.shape[0], scatter, jnp.zeros((6 * block_rows, 128), F32), unroll=16)
    for c in range(3):
        at = 2 * block_rows * c
        table = total[at : at + block_rows] + total[at + block_rows : at + 2 * block_rows]
        for j in range(tiles):
            lanes = pl.ds(128 * j, 128)
            own_out[c : c + 1, lanes] = own_out[c : c + 1, lanes] + table[j : j + 1]
        for i in range(3):
            for h in range(2):
                lanes = slice(128 * h, 128 * h + 128)
                prev, mid, after = (table[row : row + 1] for row in (tiles + 2 * (3 * i + j) + h for j in range(3)))
                mid_out[i, c : c + 1, lanes] = mid
                first_out[i, c : c + 1, lanes] = jnp.where(even, after, prev)
                second_out[i, c : c + 1, lanes] = jnp.where(even, prev, after)


def ewald_kernel(
    extent_y,
    vh_ref,
    vl_ref,
    x_ref,
    dx_ref,
    z_ref,
    dz_ref,
    y_ref,
    dy_ref,
    zy_ref,
    neutral_ref,
    own_ref,
    out_ref,
    high_ref,
    low_ref,
):
    neutral = neutral_ref[...]
    coefficient_high, coefficient_low = vh_ref[...], vl_ref[...]

    def total(c, functions, high, low):
        spread = mm(coefficient_high, high) + (mm(coefficient_low, high) + mm(coefficient_high, low))
        field = None
        for k in range(XF):
            term = functions[k : k + 1, :] * spread[32 * k : 32 * k + 32]
            field = term if field is None else field + term
        out_ref[c : c + 1, :] = own_ref[c : c + 1, :] + 2.0 * jnp.sum(neutral * field, axis=0, keepdims=True)

    total(0, dx_ref, zy_ref[0], zy_ref[1])
    for c in (2, 1):
        for l in range(LZ):
            for half in range(2):
                at = 2 * l + half
                turned = dz_ref[at : at + 1, :]
                if c == 2:
                    value = (TWO_PI / BOX_HEIGHT * (l + 1)) * turned * y_ref[...]
                else:
                    value = z_ref[at : at + 1, :] * dy_ref[...] - (0.5 * TWO_PI / extent_y) * turned * y_ref[...]
                high, low = parts(value)
                high_ref[64 * at : 64 * at + 64, :] = high
                low_ref[64 * at : 64 * at + 64, :] = low
        total(c, x_ref, high_ref[...], low_ref[...])


def finish_kernel(base_ref, mid_ref, first_ref, second_ref, ghost_ref, out_ref, back_ref, sems):
    atoms = base_ref.shape[1]
    copies = [
        pltpu.make_async_copy(ref, back_ref.at[n], sems.at[n]) for n, ref in enumerate((mid_ref, first_ref, second_ref))
    ]
    for copy in copies:
        copy.start()
    for copy in copies:
        copy.wait()
    returned = back_ref[0] + back_ref[1] + back_ref[2]
    high = returned.astype(BF16).astype(F32)
    rest = returned - high
    middle = rest.astype(BF16).astype(F32)
    split = jnp.concatenate([high, middle, rest - middle, jnp.zeros((7, 256), F32)], axis=0).astype(BF16)
    at = jnp.where(iota((atoms, 256), 0) == ghost_ref[...], 1.0, 0.0).astype(BF16)
    spread = mm(split, at, NT)
    out_ref[...] = -(base_ref[...] + ((spread[0:3] + spread[3:6]) + spread[6:9]))


def swapped(array, axis, far):
    n = lax.axis_size(axis)
    pairs = [(i, (i + (1 if i % 2 else -1)) % n if far else i ^ 1) for i in range(n)]
    return lax.ppermute(array, axis, pairs)


def along_z(array, flip):
    first, second = lax.axis_size("gx"), lax.axis_size("gy")
    pairs = []
    for device in range(first * second):
        u, v = divmod(device, second)
        z = (v // 16 * 4 + u // 2) ^ flip
        pairs.append((device, (z % 4 * 2 + u % 2) * second + z // 4 * 16 + v % 16))
    return lax.ppermute(array, AXES, pairs)


def across_plane(array):
    planes = [list(range(16 * k, 16 * k + 16)) for k in range(lax.axis_size("gy") // 16)]
    return lax.all_to_all(array, "gy", 0, 0, tiled=True, axis_index_groups=planes)


def reduced(keep, send):
    keep = keep + swapped(send, "gx", False)
    got = across_plane(keep.reshape(16, -1, 128))
    return sum((got[k] for k in range(1, 16)), got[0])


def spread_out(keep):
    for flip in (1, 2, 7):
        keep = keep + along_z(keep, flip)
    keep = across_plane(jnp.broadcast_to(keep, (16,) + keep.shape)).reshape(-1, 128)
    return keep, swapped(keep, "gx", False)


def shards(
    positions,
    species,
    neighbours,
    ghost_index,
    wave_index,
    embedding,
    radial_weight,
    message_weight,
    scalar_weight,
    vector_weight,
    readout_hidden,
    readout_vector,
    charge_weight,
):
    atoms = positions.shape[1]
    extents = lax.axis_size("gx"), lax.axis_size("gy")
    atoms_all = atoms * extents[0] * extents[1]
    where = jnp.stack([lax.axis_index("gx"), lax.axis_index("gy")])
    kinds = species[None]
    ghosts = ghost_index[None]

    (border,) = call(border_kernel, [((4, 256), F32)], [pltpu.VMEM((8, atoms), F32)], spaces="vvv", vmem=4)(positions, kinds, ghosts)
    even = (where[0] & 1) == 0
    second, first = swapped(border, "gx", True), swapped(border, "gx", False)
    mid = jnp.stack([jnp.where(even, second, first), border, jnp.where(even, first, second)])
    second, first = swapped(mid, "gy", True), swapped(mid, "gy", False)

    fx, zy, unit, wide, embed, message = call(
        functools.partial(prepare_kernel, extents),
        [
            ((XROWS, atoms), F32),
            ((2, 128 * LZ, atoms), BF16),
            ((LZ, XROWS, 128), F32),
            ((2, 256, 512), BF16),
            ((128, 8), F32),
            ((128, 8), F32),
        ],
        spaces="svvvv",
        vmem=16,
        flops=10**9,
        nbytes=2 * 10**6,
    )(where, positions, embedding, radial_weight, message_weight)

    nbr = neighbours.T
    charge_t = charge_weight.T
    energy, charge, hbar, slope, vsum, geo, keep, send = call(
        forward_kernel,
        [
            ((1, atoms), F32),
            ((32, atoms), F32),
            ((128, atoms), F32),
            ((128, atoms), F32),
            ((3, 128, atoms), F32),
            ((7, 32, atoms), F32),
            ((ROWS // 2, 128), F32),
            ((ROWS // 2, 128), F32),
        ],
        [
            pltpu.VMEM((4, 24, 128), F32),
            pltpu.VMEM((4, 512, atoms), F32),
            pltpu.VMEM((SLAB, atoms), BF16),
            pltpu.VMEM((SLAB, atoms), BF16),
            pltpu.VMEM((ROWS, 128), F32),
            pltpu.VMEM((3, 3, 4, 256), F32),
            pltpu.SemaphoreType.DMA((3,)),
        ],
        spaces="svvaaa" + "v" * 11,
        vmem=28,
        flops=5 * 10**9,
        nbytes=4 * 10**6,
    )(
        where,
        positions,
        kinds,
        mid,
        first,
        second,
        nbr,
        embed,
        wide,
        scalar_weight,
        vector_weight,
        readout_hidden,
        readout_vector[None],
        charge_t,
        fx,
        zy,
        unit,
    )

    keep = reduced(keep, send)
    keep, waves_late, message = lax.optimization_barrier((keep, wave_index, message))
    table, narrow, weight, dx, fz, dz, fy, dy = call(
        functools.partial(later_kernel, extents, atoms_all),
        [
            ((4, 40, 128), F32),
            ((2, 64, 128), F32),
            ((128, 32), F32),
            ((XROWS, atoms), F32),
            ((2 * LZ, atoms), F32),
            ((2 * LZ, atoms), F32),
            ((2 * NY, atoms), F32),
            ((2 * NY, atoms), F32),
        ],
        spaces="svvvvv",
        vmem=16,
        flops=10**9,
        nbytes=2 * 10**6,
    )(where, positions, waves_late, radial_weight, message, charge_t)
    near, far = spread_out(keep)

    site, neutral, vh, vl, own, g_mid, g_first, g_second = call(
        functools.partial(backward_kernel, atoms_all),
        [
            ((1, atoms), F32),
            ((32, atoms), F32),
            ((SLAB, 128 * LZ), BF16),
            ((SLAB, 128 * LZ), BF16),
            ((3, atoms), F32),
            ((3, 3, 256), F32),
            ((3, 3, 256), F32),
            ((3, 3, 256), F32),
        ],
        [
            pltpu.VMEM((ROWS, 128), F32),
            pltpu.VMEM((4, 64, atoms), F32),
            pltpu.VMEM((3, 32, atoms), F32),
        ],
        spaces="s" + "v" * 16,
        vmem=28,
        flops=5 * 10**9,
        nbytes=4 * 10**6,
    )(
        where,
        near,
        far,
        table,
        fx,
        zy,
        energy,
        charge,
        hbar,
        slope,
        vsum,
        geo,
        nbr,
        scalar_weight,
        vector_weight,
        weight,
        narrow,
    )

    second, first = swapped(g_second, "gy", True), swapped(g_first, "gy", False)
    (base,) = call(
        functools.partial(ewald_kernel, extents[1]),
        [((3, atoms), F32)],
        [pltpu.VMEM((128 * LZ, atoms), BF16)] * 2,
        spaces="v" * 11,
        vmem=24,
        flops=5 * 10**9,
        nbytes=4 * 10**6,
    )(vh, vl, fx, dx, fz, dz, fy, dy, zy, neutral, own)
    first, second, base = lax.optimization_barrier((first, second, base))
    column = g_mid + first + second
    second = swapped(jnp.where(even, column[0], column[2]), "gx", True)
    first = swapped(jnp.where(even, column[2], column[0]), "gx", False)
    (forces,) = call(
        finish_kernel,
        [((3, atoms), F32)],
        [pltpu.VMEM((3, 3, 256), F32), pltpu.SemaphoreType.DMA((3,))],
        spaces="vaaav",
        vmem=4,
    )(base, column[1], first, second, ghosts)
    return forces, site[0]


def solution(mesh):
    return jax.shard_map(
        shards,
        mesh=mesh,
        in_specs=(
            P(None, ("gx", "gy")),
            P(("gx", "gy")),
            P(("gx", "gy"), None),
            P(("gx", "gy")),
            P(),
            P(),
            P(),
            P(),
            P(),
            P(),
            P(),
            P(),
            P(),
        ),
        out_specs=(P(None, ("gx", "gy")), P(("gx", "gy"))),
        check_vma=False,
    )
```

time: 160 us -> 104 us (0.65)
  blocking collectives: 0 us -> 30.2 us
  waiting for transfers between devices: 48.8 us -> 20.4 us
  Pallas kernels: 50 us -> 22.2 us
  starting transfers between devices: 45 us -> 26.9 us
  local copies, waits for them, and re-layouts: 12.7 us -> 2.77 us
    all_to_all x0 -> x2, blocking collectives: none -> 30.2 us  [across_plane(): lax.all_to_all(array, 'gy', 0, 0, tiled=True, axis_index_groups=planes)]
    ppermute x26 -> x13, waiting for transfers between devices: 48.8 us -> 20.4 us  [the longest x10 10.5 us: swapped(): return lax.ppermute(array, axis, pairs)]
    ppermute x26 -> x13, starting transfers between devices: 45 us -> 26.9 us  [the longest x10 21.6 us: swapped(): return lax.ppermute(array, axis, pairs)]
    pallas_call x9 -> x5, Pallas kernels: 23.3 us -> 8.59 us  [the longest x1 2.79 us: shards(): call(functools.partial(ewald_kernel, extents[1]), [((3, atoms), F32)], [p...]
    pallas_call x1, Pallas kernels: 15.7 us -> 6.21 us  [shards(): call(functools.partial(backward_kernel, atoms_all), [((1, atoms), F32), (...]
    unnamed x62 -> x28, local copies, waits for them, and re-layouts: 10.7 us -> 2.73 us
    pallas_call x1, Pallas kernels: 11 us -> 7.43 us  [shards(): call(forward_kernel, [((1, atoms), F32), ((32, atoms), F32), ((128, atoms...]
  transfers between devices with their start and end apart: 26 -> 13, of which waited for: 19 -> 8; matrix products, arithmetic and copies ran while one was open for 4% -> 0% of each run, Pallas kernels for 8% -> 7%
where the time goes in v2:
time: 104 us
  blocking collectives  30.2 us (29%)
  starting transfers between devices  26.9 us (26%)
  Pallas kernels  22.2 us (21%)
  waiting for transfers between devices  20.4 us (20%)
  local copies, waits for them, and re-layouts  2.77 us (3%)
    all_to_all x2, blocking collectives, across_plane(): lax.all_to_all(array, 'gy', 0, 0, tiled=True, axis_index_groups=planes)  30.2 us
    ppermute x10, starting transfers between devices, swapped(): return lax.ppermute(array, axis, pairs)  21.6 us
    ppermute x10, waiting for transfers between devices, swapped(): return lax.ppermute(array, axis, pairs)  10.5 us
    ppermute x3, waiting for transfers between devices, along_z(): return lax.ppermute(array, AXES, pairs)  9.81 us
    pallas_call x1, Pallas kernels, shards(): call(forward_kernel, [((1, atoms), F32), ((32, atoms), F32), ((128, atoms...  7.43 us
    pallas_call x1, Pallas kernels, shards(): call(functools.partial(backward_kernel, atoms_all), [((1, atoms), F32), (...  6.21 us
    ppermute x3, starting transfers between devices, along_z(): return lax.ppermute(array, AXES, pairs)  5.25 us
    pallas_call x1, Pallas kernels, shards(): call(functools.partial(ewald_kernel, extents[1]), [((3, atoms), F32)], [p...  2.79 us
  transfers between devices with their start and end apart: 13, of which 8 were waited for; matrix products, arithmetic and copies ran while one was open for 0% of the time, Pallas kernels for 7%

profile of v2, /device:TPU:0, one launch (start us, length us, event | category | flops | bytes accessed | tf_op | source)
XLA Modules:
  0.0 103.6 jit_solution(15831361855781512929)
XLA Ops:
  0.7 0.7 copy-done.3
  1.3 0.7 copy-done
  2.0 0.1 shard_map.140
  2.2 3.0 %collective-permute-start = (f32[4,256]{1,0:T(4,128)S(1)}, f32[4,256]{1,0:T(4,128)S(1)}, u32[]{:S(2)}, u32[]{:S(2)}) collective-permute-start(f32[4,256]{1,0:T(4,128)S(1)} %shard_map.140), channel_id=1, source_target_pairs={{0,224},{32,64},{64,32},{96,128},{128,96},{160,192},{192,160},{224... | collective-permute-start | bytes 12296 | tf_op jit(solution)/shard_map/ppermute | solution.py:645
  5.2 1.8 %collective-permute-done = f32[4,256]{1,0:T(4,128)S(1)} collective-permute-done((f32[4,256]{1,0:T(4,128)S(1)}, f32[4,256]{1,0:T(4,128)S(1)}, u32[]{:S(2)}, u32[]{:S(2)}) %collective-permute-start) | collective-permute-done | bytes 4128 | tf_op jit(solution)/shard_map/ppermute | solution.py:645
  7.2 10.2 %collective-permute-start.3 = (f32[3,4,256]{2,1,0:T(4,128)S(1)}, f32[3,4,256]{2,1,0:T(4,128)S(1)}, u32[]{:S(2)}, u32[]{:S(2)}) collective-permute-start(f32[3,4,256]{2,1,0:T(4,128)S(1)} %pad_maximum_fusion.mid_ref), channel_id=1, source_target_pairs={{0,31},{1,2},{2,1},{3,4},{4,3},{5,6},{6,5},{7,8},{8,7},{9,10},{10,... | collective-permute-start | bytes 36872 | tf_op jit(solution)/shard_map/ppermute | solution.py:645
  17.4 0.7 copy-done.12
  18.1 2.5 %shard_map.141 = (f32[24,512]{1,0:T(8,128)S(1)}, bf16[2,512,512]{2,1,0:T(8,128)(2,1)S(1)}, f32[4,24,128]{2,1,0:T(8,128)S(1)}, bf16[2,256,512]{2,1,0:T(8,128)(2,1...) custom-call(s32[2]{0:T(128)S(1)} %pad_add_fusion.where_ref, f32[3,512]{1,0:T(4,128)S(1)} %copy-done.1, ...), custom_call_target="tpu_custom_call" | custom-call | flops 1000000000 | bytes 2000000 | tf_op jit(solution)/shard_map/pallas_call | solution.py:704
  20.5 0.5 collective-permute-done.2.first_ref
  21.1 0.6 copy-done.13
  21.7 7.4 %shard_map.142 = (f32[1,512]{1,0:T(1,128)S(1)}, f32[32,512]{1,0:T(8,128)S(1)}, f32[128,512]{1,0:T(8,128)S(1)}, f32[128,512]{1,0:T(8,128)S(1)}, f32[3,128,512]{2,...) custom-call(s32[2]{0:T(128)S(1)} %pad_add_fusion.where_ref, ...), custom_call_target="tpu_custom_call" | custom-call | flops 5000000000 | bytes 4000000 | tf_op jit(solution)/shard_map/pallas_call | solution.py:722
  29.1 0.1 collective-permute-start.4
  29.2 2.0 %collective-permute-done.4 = f32[1152,128]{1,0:T(8,128)S(1)} collective-permute-done((f32[1152,128]{1,0:T(8,128)S(1)}, f32[1152,128]{1,0:T(8,128)S(1)}, u32[]{:S(2)}, u32[]{:S(2)}) %collective-permute-start.4) | collective-permute-done | bytes 589856 | tf_op jit(solution)/shard_map/ppermute | solution.py:645
  31.2 0.1 add.69
  31.3 16.3 %all_to_all.10 = f32[16,72,128]{2,1,0:T(8,128)S(1)} all-to-all(f32[16,72,128]{2,1,0:T(8,128)S(1)} %bitcast.35), channel_id=1, replica_groups={{0,1,2,3,4,5,6,7,8,9,10,11,12,13,14,15},{16,17,18,19,20,21,22,23,24,25,..., dimensions={0} | all-to-all | bytes 1179648 | tf_op jit(solution)/shard_map/all_to_all | solution.py:660
  47.7 0.1 collective-permute-start.5
  47.8 3.9 %collective-permute-done.5 = f32[72,128]{1,0:T(8,128)S(1)} collective-permute-done((f32[72,128]{1,0:T(8,128)S(1)}, f32[72,128]{1,0:T(8,128)S(1)}, u32[]{:S(2)}, u32[]{:S(2)}) %collective-permute-start.5) | collective-permute-done | bytes 36896 | tf_op jit(solution)/shard_map/ppermute | solution.py:655
  51.7 1.2 %collective-permute-start.6 = (f32[72,128]{1,0:T(8,128)S(1)}, f32[72,128]{1,0:T(8,128)S(1)}, u32[]{:S(2)}, u32[]{:S(2)}) collective-permute-start(f32[72,128]{1,0:T(8,128)S(1)} %add.86), channel_id=1, source_target_pairs={{0,128},{1,129},{2,130},{3,131},{4,132},{5,133},{6,134},{7,135},{8... | collective-permute-start | bytes 110600 | tf_op jit(solution)/shard_map/ppermute | solution.py:655
  52.9 3.8 %collective-permute-done.6 = f32[72,128]{1,0:T(8,128)S(1)} collective-permute-done((f32[72,128]{1,0:T(8,128)S(1)}, f32[72,128]{1,0:T(8,128)S(1)}, u32[]{:S(2)}, u32[]{:S(2)}) %collective-permute-start.6) | collective-permute-done | bytes 36896 | tf_op jit(solution)/shard_map/ppermute | solution.py:655
  56.7 4.0 %collective-permute-start.7 = (f32[72,128]{1,0:T(8,128)S(1)}, f32[72,128]{1,0:T(8,128)S(1)}, u32[]{:S(2)}, u32[]{:S(2)}) collective-permute-start(f32[72,128]{1,0:T(8,128)S(1)} %add.87), channel_id=1, source_target_pairs={{0,208},{1,209},{2,210},{3,211},{4,212},{5,213},{6,214},{7,215},{8... | collective-permute-start | bytes 110600 | tf_op jit(solution)/shard_map/ppermute | solution.py:655
  60.7 2.1 %collective-permute-done.7 = f32[72,128]{1,0:T(8,128)S(1)} collective-permute-done((f32[72,128]{1,0:T(8,128)S(1)}, f32[72,128]{1,0:T(8,128)S(1)}, u32[]{:S(2)}, u32[]{:S(2)}) %collective-permute-start.7) | collective-permute-done | bytes 36896 | tf_op jit(solution)/shard_map/ppermute | solution.py:655
  62.8 13.8 %all_to_all.11 = f32[16,72,128]{2,1,0:T(8,128)S(1)} all-to-all(f32[16,72,128]{2,1,0:T(8,128)S(1)} %broadcast_in_dim.15), channel_id=1, replica_groups={{0,1,2,3,4,5,6,7,8,9,10,11,12,13,14,15},{16,17,18,19,20,21,22,23,24,25,..., dimensions={0} | all-to-all | bytes 1179648 | tf_op jit(solution)/shard_map/all_to_all | solution.py:660
  76.7 2.4 %shard_map.143 = (f32[4,40,128]{2,1,0:T(8,128)S(1)}, f32[2,64,128]{2,1,0:T(8,128)S(1)}, f32[128,32]{1,0:T(8,128)S(1)}, f32[24,512]{1,0:T(8,128)S(1)}, f32[8,512]...) custom-call(s32[2]{0:T(128)S(1)} %pad_add_fusion.where_ref, ...), custom_call_target="tpu_custom_call" | custom-call | flops 1000000000 | bytes 2000000 | tf_op jit(solution)/shard_map/pallas_call | solution.py:769
  79.1 6.2 %shard_map.144 = (f32[1,512]{1,0:T(1,128)}, f32[32,512]{1,0:T(8,128)S(1)}, bf16[544,512]{1,0:T(8,128)(2,1)S(1)}, bf16[544,512]{1,0:T(8,128)(2,1)S(1)}, f32[3,512...) custom-call(s32[2]{0:T(128)S(1)} %pad_add_fusion.where_ref, ...), custom_call_target="tpu_custom_call" | custom-call | flops 5000000000 | bytes 4000000 | tf_op jit(solution)/shard_map/pallas_call | solution.py:788
  85.3 0.6 collective-permute-start.9
  85.9 6.4 %collective-permute-start.10 = (f32[3,3,256]{2,1,0:T(4,128)S(1)}, f32[3,3,256]{2,1,0:T(4,128)S(1)}, u32[]{:S(2)}, u32[]{:S(2)}) collective-permute-start(f32[3,3,256]{2,1,0:T(4,128)S(1)} %get-tuple-element.59), channel_id=1, source_target_pairs={{0,31},{1,2},{2,1},{3,4},{4,3},{5,6},{6,5},{7,8},{8,7},{9,10},{10,... | collective-permute-start | bytes 27656 | tf_op jit(solution)/shard_map/ppermute | solution.py:645
  92.3 2.8 %shard_map.145.base_ref = f32[3,512]{1,0:T(4,128)S(1)} custom-call(bf16[544,512]{1,0:T(8,128)(2,1)S(1)} %get-tuple-element.60.vh_ref, bf16[544,512]{1,0:T(8,128)(2,1)S(1)} %get-tuple-element.61.vl_ref, f32[24,512]{1,0:T(8,128)S(1)} %get-tuple-element.40.x_ref, f32[24,512]{1,0:T(8,128)S(1)} %get-tuple-element.62.dx_ref, ...), custom_call_target="tpu_custom_call" | custom-call | flops 5000000000 | bytes 4000000 | tf_op jit(solution)/shard_map/pallas_call | solution.py:830
  95.1 2.6 %collective-permute-done.10 = f32[3,3,256]{2,1,0:T(4,128)S(1)} collective-permute-done((f32[3,3,256]{2,1,0:T(4,128)S(1)}, f32[3,3,256]{2,1,0:T(4,128)S(1)}, u32[]{:S(2)}, u32[]{:S(2)}) %collective-permute-start.10) | collective-permute-done | bytes 9248 | tf_op jit(solution)/shard_map/ppermute | solution.py:645
  97.7 1.1 %collective-permute-start.12 = (f32[3,256]{1,0:T(4,128)S(1)}, f32[3,256]{1,0:T(4,128)S(1)}, u32[]{:S(2)}, u32[]{:S(2)}) collective-permute-start(f32[3,256]{1,0:T(4,128)S(1)} %get-tuple-element.74), channel_id=1, source_target_pairs={{0,224},{32,64},{64,32},{96,128},{128,96},{160,192},{192,160},{224... | collective-permute-start | bytes 9224 | tf_op jit(solution)/shard_map/ppermute | solution.py:645
  98.8 0.2 collective-permute-start.11
  99.0 3.6 %collective-permute-done.12.second_ref = f32[3,256]{1,0:T(4,128)S(1)} collective-permute-done((f32[3,256]{1,0:T(4,128)S(1)}, f32[3,256]{1,0:T(4,128)S(1)}, u32[]{:S(2)}, u32[]{:S(2)}) %collective-permute-start.12) | collective-permute-done | bytes 3104 | tf_op jit(solution)/shard_map/ppermute | solution.py:645
  102.6 0.9 shard_map.146
  (42 shorter events, 0.3 us)
Async XLA Ops:
  0.6 0.7 copy-start.3
  0.6 0.7 copy-start.2
  1.3 0.7 copy-start
  2.0 15.3 %copy-start.4 = (f32[128,128]{1,0:T(8,128)S(1)}, f32[128,128]{1,0:T(8,128)}, u32[]{:S(2)}) copy-start(f32[128,128]{1,0:T(8,128)} %message_ref.1) | copy-start | bytes 196612
  2.1 3.1 %collective-permute-start.1 = (f32[4,256]{1,0:T(4,128)S(1)}, f32[4,256]{1,0:T(4,128)S(1)}, u32[]{:S(2)}, u32[]{:S(2)}) collective-permute-start(f32[4,256]{1,0:T(4,128)S(1)} %shard_map.140), channel_id=1, source_target_pairs={{0,32},{32,0},{64,96},{96,64},{128,160},{160,128},{192,224},{224,1... | collective-permute-start | bytes 12296 | tf_op jit(solution)/shard_map/ppermute | solution.py:645
  2.2 4.9 %collective-permute-start = (f32[4,256]{1,0:T(4,128)S(1)}, f32[4,256]{1,0:T(4,128)S(1)}, u32[]{:S(2)}, u32[]{:S(2)}) collective-permute-start(f32[4,256]{1,0:T(4,128)S(1)} %shard_map.140), channel_id=1, source_target_pairs={{0,224},{32,64},{64,32},{96,128},{128,96},{160,192},{192,160},{224... | collective-permute-start | bytes 12296 | tf_op jit(solution)/shard_map/ppermute | solution.py:645
  7.1 10.3 %copy-start.1 = (f32[3,512]{1,0:T(4,128)S(1)}, f32[3,512]{1,0:T(4,128)}, u32[]{:S(2)}) copy-start(f32[3,512]{1,0:T(4,128)} %pos_ref.7) | copy-start | bytes 18436
  7.1 10.3 %copy-start.11 = (f32[8,256]{1,0:T(8,128)S(1)}, f32[8,256]{1,0:T(8,128)}, u32[]{:S(2)}) copy-start(f32[8,256]{1,0:T(8,128)} %radial_ref.3) | copy-start | bytes 24580
  7.1 13.9 %copy-start.5 = (f32[128,128]{1,0:T(8,128)S(1)}, f32[128,128]{1,0:T(8,128)}, u32[]{:S(2)}) copy-start(f32[128,128]{1,0:T(8,128)} %hidden_ref.1) | copy-start | bytes 196612
  7.1 13.9 %copy-start.7 = (s32[512,32]{0,1:T(8,128)S(1)}, s32[512,32]{0,1:T(8,128)}, u32[]{:S(2)}) copy-start(s32[512,32]{0,1:T(8,128)} %param.15) | copy-start | bytes 196612
  7.1 13.9 %copy-start.8 = (f32[128,128]{1,0:T(8,128)S(1)}, f32[128,128]{1,0:T(8,128)}, u32[]{:S(2)}) copy-start(f32[128,128]{1,0:T(8,128)} %scalar_ref.3) | copy-start | bytes 196612
  7.1 13.9 %copy-start.9 = (f32[128,128]{1,0:T(8,128)S(1)}, f32[128,128]{1,0:T(8,128)}, u32[]{:S(2)}) copy-start(f32[128,128]{1,0:T(8,128)} %vector_ref.3) | copy-start | bytes 196612
  7.1 13.9 %copy-start.10 = (f32[128,32]{0,1:T(8,128)S(1)}, f32[128,32]{0,1:T(8,128)}, u32[]{:S(2)}) copy-start(f32[128,32]{0,1:T(8,128)} %param.25) | copy-start | bytes 49156
  7.2 13.4 %collective-permute-start.3 = (f32[3,4,256]{2,1,0:T(4,128)S(1)}, f32[3,4,256]{2,1,0:T(4,128)S(1)}, u32[]{:S(2)}, u32[]{:S(2)}) collective-permute-start(f32[3,4,256]{2,1,0:T(4,128)S(1)} %pad_maximum_fusion.mid_ref), channel_id=1, source_target_pairs={{0,31},{1,2},{2,1},{3,4},{4,3},{5,6},{6,5},{7,8},{8,7},{9,10},{10,... | collective-permute-start | bytes 36872 | tf_op jit(solution)/shard_map/ppermute | solution.py:645
  17.3 3.7 %collective-permute-start.2 = (f32[3,4,256]{2,1,0:T(4,128)S(1)}, f32[3,4,256]{2,1,0:T(4,128)S(1)}, u32[]{:S(2)}, u32[]{:S(2)}) collective-permute-start(f32[3,4,256]{2,1,0:T(4,128)S(1)} %pad_maximum_fusion.mid_ref), channel_id=1, source_target_pairs={{0,1},{1,0},{2,3},{3,2},{4,5},{5,4},{6,7},{7,6},{8,9},{9,8},{10,11... | collective-permute-start | bytes 36872 | tf_op jit(solution)/shard_map/ppermute | solution.py:645
  17.4 0.7 copy-start.12
  21.0 0.7 copy-start.13
  29.1 2.1 %collective-permute-start.4 = (f32[1152,128]{1,0:T(8,128)S(1)}, f32[1152,128]{1,0:T(8,128)S(1)}, u32[]{:S(2)}, u32[]{:S(2)}) collective-permute-start(f32[1152,128]{1,0:T(8,128)S(1)} %get-tuple-element.44), channel_id=1, source_target_pairs={{0,32},{32,0},{64,96},{96,64},{128,160},{160,128},{192,224},{224,1... | collective-permute-start | bytes 1769480 | tf_op jit(solution)/shard_map/ppermute | solution.py:645
  47.7 4.0 %collective-permute-start.5 = (f32[72,128]{1,0:T(8,128)S(1)}, f32[72,128]{1,0:T(8,128)S(1)}, u32[]{:S(2)}, u32[]{:S(2)}) collective-permute-start(f32[72,128]{1,0:T(8,128)S(1)} %fusion), channel_id=1, source_target_pairs={{0,64},{1,65},{2,66},{3,67},{4,68},{5,69},{6,70},{7,71},{8,72},{9,... | collective-permute-start | bytes 110600 | tf_op jit(solution)/shard_map/ppermute | solution.py:655
  51.7 5.0 %collective-permute-start.6 = (f32[72,128]{1,0:T(8,128)S(1)}, f32[72,128]{1,0:T(8,128)S(1)}, u32[]{:S(2)}, u32[]{:S(2)}) collective-permute-start(f32[72,128]{1,0:T(8,128)S(1)} %add.86), channel_id=1, source_target_pairs={{0,128},{1,129},{2,130},{3,131},{4,132},{5,133},{6,134},{7,135},{8... | collective-permute-start | bytes 110600 | tf_op jit(solution)/shard_map/ppermute | solution.py:655
  56.7 6.1 %collective-permute-start.7 = (f32[72,128]{1,0:T(8,128)S(1)}, f32[72,128]{1,0:T(8,128)S(1)}, u32[]{:S(2)}, u32[]{:S(2)}) collective-permute-start(f32[72,128]{1,0:T(8,128)S(1)} %add.87), channel_id=1, source_target_pairs={{0,208},{1,209},{2,210},{3,211},{4,212},{5,213},{6,214},{7,215},{8... | collective-permute-start | bytes 110600 | tf_op jit(solution)/shard_map/ppermute | solution.py:655
  62.8 13.8 %copy-start.6 = (s32[3,4096]{1,0:T(4,128)S(1)}, s32[3,4096]{1,0:T(4,128)}, u32[]{:S(2)}) copy-start(s32[3,4096]{1,0:T(4,128)} %wave_ref) | copy-start | bytes 147460
  76.7 2.4 %collective-permute-start.8 = (f32[1152,128]{1,0:T(8,128)S(1)}, f32[1152,128]{1,0:T(8,128)S(1)}, u32[]{:S(2)}, u32[]{:S(2)}) collective-permute-start(f32[1152,128]{1,0:T(8,128)S(1)} %bitcast.23), channel_id=1, source_target_pairs={{0,32},{32,0},{64,96},{96,64},{128,160},{160,128},{192,224},{224,1... | collective-permute-start | bytes 1769480 | tf_op jit(solution)/shard_map/ppermute | solution.py:645
  85.3 9.8 %collective-permute-start.9 = (f32[3,3,256]{2,1,0:T(4,128)S(1)}, f32[3,3,256]{2,1,0:T(4,128)S(1)}, u32[]{:S(2)}, u32[]{:S(2)}) collective-permute-start(f32[3,3,256]{2,1,0:T(4,128)S(1)} %get-tuple-element.58), channel_id=1, source_target_pairs={{0,1},{1,0},{2,3},{3,2},{4,5},{5,4},{6,7},{7,6},{8,9},{9,8},{10,11... | collective-permute-start | bytes 27656 | tf_op jit(solution)/shard_map/ppermute | solution.py:645
  85.9 11.8 %collective-permute-start.10 = (f32[3,3,256]{2,1,0:T(4,128)S(1)}, f32[3,3,256]{2,1,0:T(4,128)S(1)}, u32[]{:S(2)}, u32[]{:S(2)}) collective-permute-start(f32[3,3,256]{2,1,0:T(4,128)S(1)} %get-tuple-element.59), channel_id=1, source_target_pairs={{0,31},{1,2},{2,1},{3,4},{4,3},{5,6},{6,5},{7,8},{8,7},{9,10},{10,... | collective-permute-start | bytes 27656 | tf_op jit(solution)/shard_map/ppermute | solution.py:645
  97.7 4.9 %collective-permute-start.12 = (f32[3,256]{1,0:T(4,128)S(1)}, f32[3,256]{1,0:T(4,128)S(1)}, u32[]{:S(2)}, u32[]{:S(2)}) collective-permute-start(f32[3,256]{1,0:T(4,128)S(1)} %get-tuple-element.74), channel_id=1, source_target_pairs={{0,224},{32,64},{64,32},{96,128},{128,96},{160,192},{192,160},{224... | collective-permute-start | bytes 9224 | tf_op jit(solution)/shard_map/ppermute | solution.py:645
  98.8 3.8 %collective-permute-start.11 = (f32[3,256]{1,0:T(4,128)S(1)}, f32[3,256]{1,0:T(4,128)S(1)}, u32[]{:S(2)}, u32[]{:S(2)}) collective-permute-start(f32[3,256]{1,0:T(4,128)S(1)} %get-tuple-element.75), channel_id=1, source_target_pairs={{0,32},{32,0},{64,96},{96,64},{128,160},{160,128},{192,224},{224,1... | collective-permute-start | bytes 9224 | tf_op jit(solution)/shard_map/ppermute | solution.py:645

commit v3 on v2

--- a/solution.py
+++ b/solution.py
@@ -23,9 +23,9 @@
 XF = 2 * HX - 1
 XROWS = 24
 SLAB = XF * 32
-UNIT_ROW = LZ * SLAB
-TOTAL_ROW = UNIT_ROW + LZ * XROWS
-ROWS = TOTAL_ROW + 32
+UNIT_ROW = 2 * SLAB
+TOTAL_ROW = UNIT_ROW + 2 * XROWS
+HALF = TOTAL_ROW + 16
 
 F32 = jnp.float32
 BF16 = jnp.bfloat16
@@ -129,12 +129,14 @@
     embed_ref,
     radial_ref,
     message_ref,
+    readout_ref,
     x_out,
     zy_out,
     unit_out,
-    wide_out,
+    weight_out,
+    weight_t_out,
     embed_out,
-    message_out,
+    readout_out,
 ):
     turn_x, _, turn_z, turn_y, _ = waves(grid, where_ref, pos_ref)
     fx = jnp.where(iota(turn_x.shape, 0) < XF, cos_turns(turn_x), 0.0)
@@ -151,46 +153,29 @@
     embed = embed_ref[...].T
     message = mm(message_ref[...].T, embed, NN, HIGHEST)
     embed_out[...] = embed
-    message_out[...] = message
-    col = iota((NB, 512), 1)
-    sub = iota((NB, 512), 0)
-    pick_b = ((col >> 6) == sub).astype(F32)
-    pick_s = (((col >> 3) & 7) == sub).astype(F32)
+    readout_out[...] = jnp.broadcast_to(readout_ref[...], (8, 128)).T
+    col = iota((NB, 64), 1)
+    sub = iota((NB, 64), 0)
+    pick_b = ((col >> 3) == sub).astype(F32)
+    pick_s = ((col & 7) == sub).astype(F32)
     spread = mm(message, pick_s, NN, HIGHEST)
     radial = radial_ref[...].T
     channels = message.shape[0]
     for which in range(2):
-        wide = mm(radial[which * channels : (which + 1) * channels], pick_b, NN, HIGHEST) * spread
-        high, low = parts(wide)
-        wide_out[which, 0:channels] = high
-        wide_out[which, channels:] = low
+        weight = mm(radial[which * channels : (which + 1) * channels], pick_b, NN, HIGHEST) * spread
+        weight_out[which] = weight
+        weight_t_out[which] = weight.T
 
 
 def later_kernel(
     grid,
     atoms_all,
-    where_ref,
-    pos_ref,
     wave_ref,
-    radial_ref,
-    message_ref,
     charge_ref,
     table_out,
-    narrow_out,
     charge_out,
-    dx_out,
-    z_out,
-    dz_out,
-    y_out,
-    dy_out,
 ):
     extent_x, extent_y = grid
-    turn_x, rate_x, turn_z, turn_y, rate_y = waves(grid, where_ref, pos_ref)
-    dx_out[...] = cos_turns(turn_x + 0.25) * rate_x
-    z_out[...] = cos_turns(turn_z)
-    dz_out[...] = cos_turns(turn_z + 0.25)
-    y_out[...] = cos_turns(turn_y)
-    dy_out[...] = cos_turns(turn_y + 0.25) * rate_y
 
     step = wave_ref.shape[1]
     order = iota((40, step), 0)
@@ -227,17 +212,6 @@
     table_out[2] = sign_st * ((pp - pm) - (mp - mn))
     table_out[3] = sign_s * ((pp + pm) - (mp + mn))
 
-    col = iota((NB, 64), 1)
-    sub = iota((NB, 64), 0)
-    pick_b = ((col >> 3) == sub).astype(F32)
-    pick_s = ((col & 7) == sub).astype(F32)
-    message = message_ref[...]
-    channels = message.shape[0]
-    radial = radial_ref[...].T
-    spread = mm(message, pick_s, NN, HIGHEST)
-    for which in range(2):
-        narrow = mm(radial[which * channels : (which + 1) * channels], pick_b, NN, HIGHEST) * spread
-        narrow_out[which] = narrow.T
     charge_out[...] = charge_ref[...].T
 
 
@@ -259,7 +233,7 @@
     second_ref,
     nbr_ref,
     embed_ref,
-    wide_ref,
+    pair_ref,
     scalar_ref,
     vector_ref,
     hidden_ref,
@@ -268,7 +242,6 @@
     x_ref,
     zy_ref,
     unit_ref,
-    energy_out,
     charge_out,
     hbar_out,
     slope_out,
@@ -280,7 +253,6 @@
     moment_ref,
     qh_ref,
     ql_ref,
-    pay_ref,
     halo_ref,
     sems,
 ):
@@ -298,11 +270,11 @@
         tab_ref[3, j : j + 1, :] = species_ref[:, pl.ds(128 * j, 128)].astype(F32)
     for copy in copies:
         copy.wait()
-    even = (where_ref[1] & 1) == 0
-    for i in range(3):
-        first, second = halo_ref[1, i], halo_ref[2, i]
+    even = (where_ref[0] & 1) == 0
+    for j in range(3):
+        first, second = halo_ref[1, j], halo_ref[2, j]
         prev, after = jnp.where(even, second, first), jnp.where(even, first, second)
-        for j, block in enumerate((prev, halo_ref[0, i], after)):
+        for i, block in enumerate((prev, halo_ref[0, j], after)):
             shifts = (i - 1.0, j - 1.0, 0.0, 0.0)
             for c in range(4):
                 for h in range(2):
@@ -342,19 +314,23 @@
         for f in range(4):
             for b in range(NB):
                 value = terms[b][0] if f == 0 else terms[b][0] * geo_out[f - 1, :, lanes]
+                rows = []
                 for s in range(NS):
                     chosen = jnp.where(kind == float(s), value, 0.0)
-                    total = (chosen[0:8] + chosen[8:16]) + (chosen[16:24] + chosen[24:32])
-                    moment_ref[f, pl.ds(8 * (8 * b + s), 8), lanes] = total
+                    rows.append((chosen[0:8] + chosen[8:16]) + (chosen[16:24] + chosen[24:32]))
+                for step in (4, 2, 1):
+                    here = (iota((8, 128), 0) & step) == 0
+                    rows = [
+                        jnp.where(here, one + pltpu.roll(one, 8 - step, 0), two + pltpu.roll(two, step, 0))
+                        for one, two in zip(rows[: len(rows) // 2], rows[len(rows) // 2 :])
+                    ]
+                moment_ref[f, 8 * b : 8 * b + 8, lanes] = rows[0]
         return carry
 
     lax.fori_loop(0, tiles, lane_tile, 0, unroll=2)
 
     def gathered(f):
-        wide = wide_ref[0 if f == 0 else 1]
-        high, low = parts(moment_ref[f])
-        both = mm(wide, high)
-        return both[0:128] + both[128:256] + mm(wide[0:128], low)
+        return mm3(pair_ref[0 if f == 0 else 1], moment_ref[f])
 
     scalar_sum = gathered(0)
     norm = None
@@ -371,11 +347,12 @@
     slope_out[...] = slope
     hidden = feature + act
     act, slope = silu_parts(mm3(hidden_ref[...].T, hidden))
-    readout = jnp.broadcast_to(readout_ref[...], (8, 128)).T[:, 0:1]
-    energy_out[...] = jnp.sum(act * readout, axis=0, keepdims=True)
+    readout = readout_ref[:, 0:1]
+    charge_out[32:33, :] = jnp.sum(act * readout, axis=0, keepdims=True)
     hbar_out[...] = mm3(hidden_ref[...], slope * readout)
     charges = mm3(weight_ref[...], hidden)
-    charge_out[...] = charges
+    charge_out[0:32, :] = charges
+    charge_out[33:40, :] = jnp.zeros((7, atoms), F32)
 
     total = jnp.sum(charges, axis=1, keepdims=True)
     local = total * (1.0 / atoms)
@@ -385,19 +362,18 @@
         qh_ref[32 * k : 32 * k + 32, :] = high
         ql_ref[32 * k : 32 * k + 32, :] = low
     high, low = qh_ref[...], ql_ref[...]
-    for l in range(LZ):
-        near, rest = (zy_ref[part, 128 * l : 128 * l + 128, :] for part in range(2))
-        slab = mm(high, near, NT) + (mm(low, near, NT) + mm(high, rest, NT))
-        unit = unit_ref[l]
-        for k in range(XF):
-            at = SLAB * l + 32 * k
-            pay_ref[at : at + 32, :] = slab[32 * k : 32 * k + 32] + local * unit[k : k + 1]
-        pay_ref[UNIT_ROW + XROWS * l : UNIT_ROW + XROWS * (l + 1), :] = unit
-    pay_ref[TOTAL_ROW : TOTAL_ROW + 32, :] = jnp.broadcast_to(total, (32, 128))
-    half = ROWS // 2
     core = where_ref[0] & 1
-    keep_out[...] = pay_ref[pl.ds(pl.multiple_of(core * half, 8), half), :]
-    send_out[...] = pay_ref[pl.ds(pl.multiple_of((1 - core) * half, 8), half), :]
+    for out, half in ((send_out, 1 - core), (keep_out, core)):
+        for n in range(2):
+            l = 2 * half + n
+            near, rest = (zy_ref[part, pl.ds(pl.multiple_of(128 * l, 128), 128), :] for part in range(2))
+            slab = mm(high, near, NT) + (mm(low, near, NT) + mm(high, rest, NT))
+            unit = unit_ref[l]
+            for k in range(XF):
+                at = SLAB * n + 32 * k
+                out[at : at + 32, :] = slab[32 * k : 32 * k + 32] + local * unit[k : k + 1]
+            out[UNIT_ROW + XROWS * n : UNIT_ROW + XROWS * (n + 1), :] = unit
+        out[TOTAL_ROW:HALF, :] = jnp.where(iota((16, 128), 1) < 64, total[0:16], total[16:32])
 
 
 def quarters(x, which):
@@ -410,15 +386,74 @@
     return jnp.where(even, pltpu.roll(x, 32, 1), pltpu.roll(x, 96, 1))
 
 
+def contribution(half, ref, table_ref, x_ref, zy_ref, vh_out, vl_out, atoms_all):
+    ends = ref[TOTAL_ROW:HALF, :]
+    mean = jnp.concatenate([ends[:, 0:1], ends[:, 64:65]], axis=0) * (1.0 / atoms_all)
+
+    def put(n, k, value):
+        rows = pl.ds(pl.multiple_of(k * 32, 32), 32)
+        high, low = parts(value)
+        vh_out[rows, 128 * n : 128 * n + 128] = high
+        vl_out[rows, 128 * n : 128 * n + 128] = low
+
+    def tile_of(n, k):
+        unit = ref[pl.ds(UNIT_ROW + XROWS * n + k, 1), :]
+        rows = pl.ds(pl.multiple_of(SLAB * n + k * 32, 32), 32)
+        return ref[rows, :] - mean * unit, unit
+
+    overlap = jnp.zeros((32, 128), F32)
+    for n in range(2):
+        cos_tile, unit = tile_of(n, 0)
+        g0, gt = (table_ref[t, pl.ds(2 * half + n, 1), :] for t in range(2))
+        value = g0 * cos_tile + gt * quarters(cos_tile, 3)
+        overlap = overlap + value * unit
+        put(n, 0, value)
+
+    def mix(a, overlap):
+        for n in range(2):
+            cos_tile, cos_unit = tile_of(n, a)
+            sin_tile, sin_unit = tile_of(n, a + HX - 1)
+            g0, gt, gst, gs = (table_ref[t, pl.ds(a * LZ + 2 * half + n, 1), :] for t in range(4))
+            value = (g0 * cos_tile + gt * quarters(cos_tile, 3)) + (
+                gst * quarters(sin_tile, 1) + gs * quarters(sin_tile, 2)
+            )
+            overlap = overlap + value * cos_unit
+            put(n, a, value)
+            value = (g0 * sin_tile + gt * quarters(sin_tile, 3)) - (
+                gst * quarters(cos_tile, 1) + gs * quarters(cos_tile, 2)
+            )
+            overlap = overlap + value * sin_unit
+            put(n, a + HX - 1, value)
+        return overlap
+
+    overlap = lax.fori_loop(1, HX, mix, overlap, unroll=8)
+    at = pl.ds(pl.multiple_of(256 * half, 256), 256)
+    high, low = zy_ref[0, at, :], zy_ref[1, at, :]
+    spread = mm(vh_out[...], high) + (mm(vl_out[...], high) + mm(vh_out[...], low))
+    potential = jnp.zeros((32, zy_ref.shape[2]), F32)
+    for k in range(XF):
+        potential = potential + x_ref[k : k + 1, :] * spread[32 * k : 32 * k + 32]
+    return mean, potential, overlap
+
+
+def near_kernel(
+    atoms_all, where_ref, near_ref, table_ref, x_ref, zy_ref, vh_out, vl_out, potential_out, overlap_out
+):
+    half = where_ref[0] & 1
+    _, potential, overlap = contribution(half, near_ref, table_ref, x_ref, zy_ref, vh_out, vl_out, atoms_all)
+    potential_out[...] = potential
+    overlap_out[...] = overlap
+
+
 def backward_kernel(
     atoms_all,
     where_ref,
-    near_ref,
     far_ref,
     table_ref,
     x_ref,
     zy_ref,
-    energy_ref,
+    potential_ref,
+    overlap_ref,
     charge_ref,
     hbar_ref,
     slope_ref,
@@ -428,7 +463,7 @@
     scalar_ref,
     vector_ref,
     weight_ref,
-    narrow_ref,
+    pair_ref,
     site_out,
     neutral_out,
     vh_out,
@@ -437,72 +472,26 @@
     mid_out,
     first_out,
     second_out,
-    sum_ref,
     g_ref,
     rbar_ref,
 ):
     atoms = nbr_ref.shape[1]
     tiles = atoms // 128
-    half = ROWS // 2
-    core = where_ref[0] & 1
-    sum_ref[pl.ds(pl.multiple_of(core * half, 8), half), :] = near_ref[...]
-    sum_ref[pl.ds(pl.multiple_of((1 - core) * half, 8), half), :] = far_ref[...]
-    mean = sum_ref[TOTAL_ROW : TOTAL_ROW + 32, :] * (1.0 / atoms_all)
-
-    def put(l, k, value):
-        rows = pl.ds(pl.multiple_of(k * 32, 32), 32)
-        high, low = parts(value)
-        vh_out[rows, 128 * l : 128 * l + 128] = high
-        vl_out[rows, 128 * l : 128 * l + 128] = low
-
-    def tile_of(l, k):
-        unit = sum_ref[pl.ds(UNIT_ROW + XROWS * l + k, 1), :]
-        rows = pl.ds(pl.multiple_of(SLAB * l + k * 32, 32), 32)
-        return sum_ref[rows, :] - mean * unit, unit
-
-    overlap = jnp.zeros((32, 128), F32)
-    for l in range(LZ):
-        cos_tile, unit = tile_of(l, 0)
-        g0 = table_ref[0, l : l + 1, :]
-        gt = table_ref[1, l : l + 1, :]
-        value = g0 * cos_tile + gt * quarters(cos_tile, 3)
-        overlap = overlap + value * unit
-        put(l, 0, value)
-
-    def mix(a, overlap):
-        for l in range(LZ):
-            cos_tile, cos_unit = tile_of(l, a)
-            sin_tile, sin_unit = tile_of(l, a + HX - 1)
-            g0, gt, gst, gs = (table_ref[n, pl.ds(a * LZ + l, 1), :] for n in range(4))
-            value = (g0 * cos_tile + gt * quarters(cos_tile, 3)) + (
-                gst * quarters(sin_tile, 1) + gs * quarters(sin_tile, 2)
-            )
-            overlap = overlap + value * cos_unit
-            put(l, a, value)
-            value = (g0 * sin_tile + gt * quarters(sin_tile, 3)) - (
-                gst * quarters(cos_tile, 1) + gs * quarters(cos_tile, 2)
-            )
-            overlap = overlap + value * sin_unit
-            put(l, a + HX - 1, value)
-        return overlap
-
-    overlap = lax.fori_loop(1, HX, mix, overlap, unroll=4)
+    half = 1 - (where_ref[0] & 1)
+    mean, potential, overlap = contribution(half, far_ref, table_ref, x_ref, zy_ref, vh_out, vl_out, atoms_all)
+    potential = potential + potential_ref[...]
+    overlap = overlap + overlap_ref[...]
     potential_mean = jnp.sum(overlap, axis=1, keepdims=True) * (1.0 / atoms_all)
-
-    spread = mm(vh_out[...], zy_ref[0]) + (mm(vl_out[...], zy_ref[0]) + mm(vh_out[...], zy_ref[1]))
-    potential = jnp.zeros((32, atoms), F32)
-    for k in range(XF):
-        potential = potential + x_ref[k : k + 1, :] * spread[32 * k : 32 * k + 32]
-    neutral = charge_ref[...] - mean[:, 0:1]
+    neutral = charge_ref[0:32, :] - mean
     neutral_out[...] = neutral
-    site_out[...] = energy_ref[...] + jnp.sum(neutral * potential, axis=0, keepdims=True)
+    site_out[...] = charge_ref[32:33, :] + jnp.sum(neutral * potential, axis=0, keepdims=True)
     charge_bar = 2.0 * (potential - potential_mean)
     update_bar = (hbar_ref[...] + mm3(weight_ref[...], charge_bar)) * slope_ref[...]
     scalar_bar = mm3(scalar_ref[...], update_bar)
     norm_bar = 2.0 * mm3(vector_ref[...], update_bar)
-    g_ref[0] = mm3(narrow_ref[0], scalar_bar)
+    g_ref[0] = mm3(pair_ref[0], scalar_bar)
     for c in range(3):
-        g_ref[c + 1] = mm3(narrow_ref[1], vsum_ref[c] * norm_bar)
+        g_ref[c + 1] = mm3(pair_ref[1], vsum_ref[c] * norm_bar)
 
     def slots(t, carry):
         lanes = pl.ds(pl.multiple_of(t * 128, 128), 128)
@@ -577,47 +566,63 @@
 
 
 def ewald_kernel(
-    extent_y,
-    vh_ref,
-    vl_ref,
+    grid,
+    where_ref,
+    pos_ref,
+    nh_ref,
+    nl_ref,
+    fh_ref,
+    fl_ref,
     x_ref,
-    dx_ref,
-    z_ref,
-    dz_ref,
-    y_ref,
-    dy_ref,
     zy_ref,
     neutral_ref,
     own_ref,
     out_ref,
     high_ref,
     low_ref,
+    z_ref,
+    dz_ref,
+    y_ref,
+    dy_ref,
 ):
+    extent_x, extent_y = grid
+    core = where_ref[0] & 1
     neutral = neutral_ref[...]
-    coefficient_high, coefficient_low = vh_ref[...], vl_ref[...]
-
-    def total(c, functions, high, low):
-        spread = mm(coefficient_high, high) + (mm(coefficient_low, high) + mm(coefficient_high, low))
+    turn_x, rate_x, turn_z, turn_y, rate_y = waves(grid, where_ref, pos_ref)
+    first = core == 0
+    coefficients = [
+        (jnp.where(first, nh_ref[...], fh_ref[...]), jnp.where(first, nl_ref[...], fl_ref[...]), slice(0, 256)),
+        (jnp.where(first, fh_ref[...], nh_ref[...]), jnp.where(first, fl_ref[...], nl_ref[...]), slice(256, 512)),
+    ]
+
+    def total(c, functions, high_ref, low_ref):
+        spread = None
+        for high, low, at in coefficients:
+            near, rest = high_ref[at, :], low_ref[at, :]
+            term = mm(high, near) + (mm(low, near) + mm(high, rest))
+            spread = term if spread is None else spread + term
         field = None
         for k in range(XF):
             term = functions[k : k + 1, :] * spread[32 * k : 32 * k + 32]
             field = term if field is None else field + term
         out_ref[c : c + 1, :] = own_ref[c : c + 1, :] + 2.0 * jnp.sum(neutral * field, axis=0, keepdims=True)
 
-    total(0, dx_ref, zy_ref[0], zy_ref[1])
+    total(0, cos_turns(turn_x + 0.25) * rate_x, zy_ref.at[0], zy_ref.at[1])
+    z_ref[...] = cos_turns(turn_z)
+    dz_ref[...] = cos_turns(turn_z + 0.25)
+    y_ref[...] = cos_turns(turn_y)
+    dy_ref[...] = cos_turns(turn_y + 0.25) * rate_y
     for c in (2, 1):
-        for l in range(LZ):
-            for half in range(2):
-                at = 2 * l + half
-                turned = dz_ref[at : at + 1, :]
-                if c == 2:
-                    value = (TWO_PI / BOX_HEIGHT * (l + 1)) * turned * y_ref[...]
-                else:
-                    value = z_ref[at : at + 1, :] * dy_ref[...] - (0.5 * TWO_PI / extent_y) * turned * y_ref[...]
-                high, low = parts(value)
-                high_ref[64 * at : 64 * at + 64, :] = high
-                low_ref[64 * at : 64 * at + 64, :] = low
-        total(c, x_ref, high_ref[...], low_ref[...])
+        for at in range(2 * LZ):
+            turned = dz_ref[at : at + 1, :]
+            if c == 2:
+                value = (TWO_PI / BOX_HEIGHT * (at // 2 + 1)) * turned * y_ref[...]
+            else:
+                value = z_ref[at : at + 1, :] * dy_ref[...] - (0.5 * TWO_PI / extent_y) * turned * y_ref[...]
+            high, low = parts(value)
+            high_ref[64 * at : 64 * at + 64, :] = high
+            low_ref[64 * at : 64 * at + 64, :] = low
+        total(c, x_ref, high_ref, low_ref)
 
 
 def finish_kernel(base_ref, mid_ref, first_ref, second_ref, ghost_ref, out_ref, back_ref, sems):
@@ -664,13 +669,6 @@
     keep = keep + swapped(send, "gx", False)
     got = across_plane(keep.reshape(16, -1, 128))
     return sum((got[k] for k in range(1, 16)), got[0])
-
-
-def spread_out(keep):
-    for flip in (1, 2, 7):
-        keep = keep + along_z(keep, flip)
-    keep = across_plane(jnp.broadcast_to(keep, (16,) + keep.shape)).reshape(-1, 128)
-    return keep, swapped(keep, "gx", False)
 
 
 def shards(
@@ -696,52 +694,51 @@
     ghosts = ghost_index[None]
 
     (border,) = call(border_kernel, [((4, 256), F32)], [pltpu.VMEM((8, atoms), F32)], spaces="vvv", vmem=4)(positions, kinds, ghosts)
-    even = (where[0] & 1) == 0
-    second, first = swapped(border, "gx", True), swapped(border, "gx", False)
-    mid = jnp.stack([jnp.where(even, second, first), border, jnp.where(even, first, second)])
-    second, first = swapped(mid, "gy", True), swapped(mid, "gy", False)
-
-    fx, zy, unit, wide, embed, message = call(
+    even = [(where[axis] & 1) == 0 for axis in range(2)]
+    second, first = swapped(border, "gy", True), swapped(border, "gy", False)
+    fx, zy, unit, pair, pair_t, embed, readout = call(
         functools.partial(prepare_kernel, extents),
         [
             ((XROWS, atoms), F32),
             ((2, 128 * LZ, atoms), BF16),
             ((LZ, XROWS, 128), F32),
-            ((2, 256, 512), BF16),
+            ((2, 128, 64), F32),
+            ((2, 64, 128), F32),
             ((128, 8), F32),
             ((128, 8), F32),
         ],
-        spaces="svvvv",
+        spaces="svvvvv",
         vmem=16,
         flops=10**9,
         nbytes=2 * 10**6,
-    )(where, positions, embedding, radial_weight, message_weight)
+    )(where, positions, embedding, radial_weight, message_weight, readout_vector[None])
+    second, first, zy = lax.optimization_barrier((second, first, zy))
+    mid = jnp.stack([jnp.where(even[1], second, first), border, jnp.where(even[1], first, second)])
+    second, first = swapped(mid, "gx", True), swapped(mid, "gx", False)
 
     nbr = neighbours.T
     charge_t = charge_weight.T
-    energy, charge, hbar, slope, vsum, geo, keep, send = call(
+    charge, hbar, slope, vsum, geo, keep, send = call(
         forward_kernel,
         [
-            ((1, atoms), F32),
-            ((32, atoms), F32),
+            ((40, atoms), F32),
             ((128, atoms), F32),
             ((128, atoms), F32),
             ((3, 128, atoms), F32),
             ((7, 32, atoms), F32),
-            ((ROWS // 2, 128), F32),
-            ((ROWS // 2, 128), F32),
+            ((HALF, 128), F32),
+            ((HALF, 128), F32),
         ],
         [
             pltpu.VMEM((4, 24, 128), F32),
-            pltpu.VMEM((4, 512, atoms), F32),
+            pltpu.VMEM((4, 64, atoms), F32),
             pltpu.VMEM((SLAB, atoms), BF16),
             pltpu.VMEM((SLAB, atoms), BF16),
-            pltpu.VMEM((ROWS, 128), F32),
             pltpu.VMEM((3, 3, 4, 256), F32),
             pltpu.SemaphoreType.DMA((3,)),
         ],
         spaces="svvaaa" + "v" * 11,
-        vmem=28,
+        vmem=16,
         flops=5 * 10**9,
         nbytes=4 * 10**6,
     )(
@@ -753,11 +750,11 @@
         second,
         nbr,
         embed,
-        wide,
+        pair,
         scalar_weight,
         vector_weight,
         readout_hidden,
-        readout_vector[None],
+        readout,
         charge_t,
         fx,
         zy,
@@ -765,55 +762,57 @@
     )
 
     keep = reduced(keep, send)
-    keep, waves_late, message = lax.optimization_barrier((keep, wave_index, message))
-    table, narrow, weight, dx, fz, dz, fy, dy = call(
+    keep = keep + along_z(keep, 1)
+    got = along_z(keep, 2)
+    keep, waves_late, charge_late = lax.optimization_barrier((keep, wave_index, charge_t))
+    table, weight = call(
         functools.partial(later_kernel, extents, atoms_all),
-        [
-            ((4, 40, 128), F32),
-            ((2, 64, 128), F32),
-            ((128, 32), F32),
-            ((XROWS, atoms), F32),
-            ((2 * LZ, atoms), F32),
-            ((2 * LZ, atoms), F32),
-            ((2 * NY, atoms), F32),
-            ((2 * NY, atoms), F32),
-        ],
-        spaces="svvvvv",
+        [((4, 40, 128), F32), ((128, 32), F32)],
+        spaces="vv",
         vmem=16,
         flops=10**9,
         nbytes=2 * 10**6,
-    )(where, positions, waves_late, radial_weight, message, charge_t)
-    near, far = spread_out(keep)
-
-    site, neutral, vh, vl, own, g_mid, g_first, g_second = call(
+    )(waves_late, charge_late)
+    got, table, weight = lax.optimization_barrier((got, table, weight))
+    keep = keep + got
+    keep = keep + along_z(keep, 6)
+    near = across_plane(jnp.broadcast_to(keep, (16,) + keep.shape)).reshape(-1, 128)
+    far = swapped(near, "gx", False)
+    nh, nl, potential, overlap = call(
+        functools.partial(near_kernel, atoms_all),
+        [((SLAB, 256), BF16), ((SLAB, 256), BF16), ((32, atoms), F32), ((32, 128), F32)],
+        spaces="svvvv",
+        vmem=16,
+        flops=10**9,
+        nbytes=2 * 10**6,
+    )(where, near, table, fx, zy)
+    far, potential = lax.optimization_barrier((far, potential))
+
+    site, neutral, fh, fl, own, g_mid, g_first, g_second = call(
         functools.partial(backward_kernel, atoms_all),
         [
             ((1, atoms), F32),
             ((32, atoms), F32),
-            ((SLAB, 128 * LZ), BF16),
-            ((SLAB, 128 * LZ), BF16),
+            ((SLAB, 256), BF16),
+            ((SLAB, 256), BF16),
             ((3, atoms), F32),
             ((3, 3, 256), F32),
             ((3, 3, 256), F32),
             ((3, 3, 256), F32),
         ],
-        [
-            pltpu.VMEM((ROWS, 128), F32),
-            pltpu.VMEM((4, 64, atoms), F32),
-            pltpu.VMEM((3, 32, atoms), F32),
-        ],
+        [pltpu.VMEM((4, 64, atoms), F32), pltpu.VMEM((3, 32, atoms), F32)],
         spaces="s" + "v" * 16,
-        vmem=28,
+        vmem=16,
         flops=5 * 10**9,
         nbytes=4 * 10**6,
     )(
         where,
-        near,
         far,
         table,
         fx,
         zy,
-        energy,
+        potential,
+        overlap,
         charge,
         hbar,
         slope,
@@ -823,23 +822,23 @@
         scalar_weight,
         vector_weight,
         weight,
-        narrow,
+        pair_t,
     )
 
     second, first = swapped(g_second, "gy", True), swapped(g_first, "gy", False)
     (base,) = call(
-        functools.partial(ewald_kernel, extents[1]),
+        functools.partial(ewald_kernel, extents),
         [((3, atoms), F32)],
-        [pltpu.VMEM((128 * LZ, atoms), BF16)] * 2,
-        spaces="v" * 11,
-        vmem=24,
+        [pltpu.VMEM((128 * LZ, atoms), BF16)] * 2 + [pltpu.VMEM((rows, atoms), F32) for rows in (8, 8, 64, 64)],
+        spaces="s" + "v" * 9,
+        vmem=16,
         flops=5 * 10**9,
         nbytes=4 * 10**6,
-    )(vh, vl, fx, dx, fz, dz, fy, dy, zy, neutral, own)
+    )(where, positions, nh, nl, fh, fl, fx, zy, neutral, own)
     first, second, base = lax.optimization_barrier((first, second, base))
     column = g_mid + first + second
-    second = swapped(jnp.where(even, column[0], column[2]), "gx", True)
-    first = swapped(jnp.where(even, column[2], column[0]), "gx", False)
+    second = swapped(jnp.where(even[0], column[0], column[2]), "gx", True)
+    first = swapped(jnp.where(even[0], column[2], column[0]), "gx", False)
     (forces,) = call(
         finish_kernel,
         [((3, atoms), F32)],

time: 104 us -> 103 us (level); the launches traced: 104 us -> 101 us
  waiting for transfers between devices: 20.4 us -> 18.6 us
  blocking collectives: 30.2 us -> 29.1 us
    pallas_call x2 -> x3, Pallas kernels: 10.2 us -> 12.2 us  [the longest x1 7.13 us: shards(): call(forward_kernel, [((40, atoms), F32), ((128, atoms), F32), ((128, ato...]
    ppermute x3, waiting for transfers between devices: 9.81 us -> 8.18 us  [along_z(): return lax.ppermute(array, AXES, pairs)]
    all_to_all x2, blocking collectives: 30.2 us -> 29.1 us  [across_plane(): lax.all_to_all(array, 'gy', 0, 0, tiled=True, axis_index_groups=planes)]
    pallas_call x1, Pallas kernels: 2.41 us -> 1.31 us  [shards(): call(functools.partial(later_kernel, extents, atoms_all), [((4, 40, 128),...]
    pallas_call x1, Pallas kernels: 6.21 us -> 5.16 us  [shards(): call(functools.partial(backward_kernel, atoms_all), [((1, atoms), F32), (...]
    unnamed x28 -> x44, local copies, waits for them, and re-layouts: 2.73 us -> 2.93 us
  transfers between devices with their start and end apart: 13 -> 13, of which waited for: 8 -> 8; matrix products, arithmetic and copies ran while one was open for 0% -> 0% of each run, Pallas kernels for 7% -> 8%
where the time goes in v3:
time: 103 us; the launch traced here: 101 us
  blocking collectives  29.1 us (28%)
  starting transfers between devices  27.6 us (27%)
  Pallas kernels  21.8 us (21%)
  waiting for transfers between devices  18.6 us (18%)
  local copies, waits for them, and re-layouts  2.97 us (3%)
  between operations  1.09 us (1%)
    all_to_all x2, blocking collectives, across_plane(): lax.all_to_all(array, 'gy', 0, 0, tiled=True, axis_index_groups=planes)  29.1 us
    ppermute x10, starting transfers between devices, swapped(): return lax.ppermute(array, axis, pairs)  21.7 us
    ppermute x10, waiting for transfers between devices, swapped(): return lax.ppermute(array, axis, pairs)  10.4 us
    ppermute x3, waiting for transfers between devices, along_z(): return lax.ppermute(array, AXES, pairs)  8.18 us
    pallas_call x1, Pallas kernels, shards(): call(forward_kernel, [((40, atoms), F32), ((128, atoms), F32), ((128, ato...  7.13 us
    ppermute x3, starting transfers between devices, along_z(): return lax.ppermute(array, AXES, pairs)  5.88 us
    pallas_call x1, Pallas kernels, shards(): call(functools.partial(backward_kernel, atoms_all), [((1, atoms), F32), (...  5.16 us
    pallas_call x1, Pallas kernels, shards(): call(functools.partial(ewald_kernel, extents), [((3, atoms), F32)], [pltp...  3.41 us
  transfers between devices with their start and end apart: 13, of which 8 were waited for; matrix products, arithmetic and copies ran while one was open for 0% of the time, Pallas kernels for 8%

profile of v3, /device:TPU:0, one launch (start us, length us, event | category | flops | bytes accessed | tf_op | source)
XLA Modules:
  0.0 101.3 jit_solution(1878511935767787628)
XLA Ops:
  0.7 0.7 copy-done.3
  1.3 0.7 copy-done
  2.2 10.8 %collective-permute-start = (f32[4,256]{1,0:T(4,128)S(1)}, f32[4,256]{1,0:T(4,128)S(1)}, u32[]{:S(2)}, u32[]{:S(2)}) collective-permute-start(f32[4,256]{1,0:T(4,128)S(1)} %shard_map.140), channel_id=1, source_target_pairs={{0,31},{1,2},{2,1},{3,4},{4,3},{5,6},{6,5},{7,8},{8,7},{9,10},{10,... | collective-permute-start | bytes 12296 | tf_op jit(solution)/shard_map/ppermute | solution.py:650
  13.1 0.6 copy-done.11
  13.7 0.8 copy-done.4
  14.6 2.2 %shard_map.141 = (f32[24,512]{1,0:T(8,128)S(1)}, bf16[2,512,512]{2,1,0:T(8,128)(2,1)S(1)}, f32[4,24,128]{2,1,0:T(8,128)S(1)}, f32[2,128,64]{2,1,0:T(8,128)S(1)},...) custom-call(s32[2]{0:T(128)S(1)} %pad_add_fusion.where_ref, f32[3,512]{1,0:T(4,128)S(1)} %copy-done.1, ...), custom_call_target="tpu_custom_call" | custom-call | flops 1000000000 | bytes 2000000 | tf_op jit(solution)/shard_map/pallas_call | solution.py:699
  16.8 0.9 collective-permute-start.3
  17.7 0.3 collective-permute-start.2
  18.0 3.8 %collective-permute-done.3.second_ref = f32[3,4,256]{2,1,0:T(4,128)S(1)} collective-permute-done((f32[3,4,256]{2,1,0:T(4,128)S(1)}, f32[3,4,256]{2,1,0:T(4,128)S(1)}, u32[]{:S(2)}, u32[]{:S(2)}) %collective-permute-start.3) | collective-permute-done | bytes 12320 | tf_op jit(solution)/shard_map/ppermute | solution.py:650
  21.9 7.1 %shard_map.142 = (f32[40,512]{1,0:T(8,128)S(1)}, f32[128,512]{1,0:T(8,128)S(1)}, f32[128,512]{1,0:T(8,128)S(1)}, f32[3,128,512]{2,1,0:T(8,128)S(1)}, f32[7,32,51...) custom-call(s32[2]{0:T(128)S(1)} %pad_add_fusion.where_ref, f32[3,512]{1,0:T(4,128)S(1)} %copy-done.1, ...), custom_call_target="tpu_custom_call" | custom-call | flops 5000000000 | bytes 4000000 | tf_op jit(solution)/shard_map/pallas_call | solution.py:721
  29.0 0.1 collective-permute-start.4
  29.1 2.0 %collective-permute-done.4 = f32[1152,128]{1,0:T(8,128)S(1)} collective-permute-done((f32[1152,128]{1,0:T(8,128)S(1)}, f32[1152,128]{1,0:T(8,128)S(1)}, u32[]{:S(2)}, u32[]{:S(2)}) %collective-permute-start.4) | collective-permute-done | bytes 589856 | tf_op jit(solution)/shard_map/ppermute | solution.py:650
  31.2 15.4 %all_to_all.10 = f32[16,72,128]{2,1,0:T(8,128)S(1)} all-to-all(f32[16,72,128]{2,1,0:T(8,128)S(1)} %bitcast.37), channel_id=1, replica_groups={{0,1,2,3,4,5,6,7,8,9,10,11,12,13,14,15},{16,17,18,19,20,21,22,23,24,25,..., dimensions={0} | all-to-all | bytes 1179648 | tf_op jit(solution)/shard_map/all_to_all | solution.py:665
  46.7 0.1 collective-permute-start.5
  46.8 3.9 %collective-permute-done.5 = f32[72,128]{1,0:T(8,128)S(1)} collective-permute-done((f32[72,128]{1,0:T(8,128)S(1)}, f32[72,128]{1,0:T(8,128)S(1)}, u32[]{:S(2)}, u32[]{:S(2)}) %collective-permute-start.5) | collective-permute-done | bytes 36896 | tf_op jit(solution)/shard_map/ppermute | solution.py:660
  50.7 1.3 %collective-permute-start.6 = (f32[72,128]{1,0:T(8,128)S(1)}, f32[72,128]{1,0:T(8,128)S(1)}, u32[]{:S(2)}, u32[]{:S(2)}) collective-permute-start(f32[72,128]{1,0:T(8,128)S(1)} %fusion.1), channel_id=1, source_target_pairs={{0,128},{1,129},{2,130},{3,131},{4,132},{5,133},{6,134},{7,135},{8... | collective-permute-start | bytes 110600 | tf_op jit(solution)/shard_map/ppermute | solution.py:660
  52.1 1.3 %shard_map.143 = (f32[4,40,128]{2,1,0:T(8,128)S(1)}, f32[128,32]{1,0:T(8,128)S(1)}) custom-call(s32[3,4096]{1,0:T(4,128)S(1)} %copy-done.6, f32[32,128]{1,0:T(8,128)S(1)} %bitcast.35), custom_call_target="tpu_custom_call" | custom-call | flops 1000000000 | bytes 2000000 | tf_op jit(solution)/shard_map/pallas_call | solution.py:768
  53.4 2.3 %collective-permute-done.6 = f32[72,128]{1,0:T(8,128)S(1)} collective-permute-done((f32[72,128]{1,0:T(8,128)S(1)}, f32[72,128]{1,0:T(8,128)S(1)}, u32[]{:S(2)}, u32[]{:S(2)}) %collective-permute-start.6) | collective-permute-done | bytes 36896 | tf_op jit(solution)/shard_map/ppermute | solution.py:660
  55.7 4.5 %collective-permute-start.7 = (f32[72,128]{1,0:T(8,128)S(1)}, f32[72,128]{1,0:T(8,128)S(1)}, u32[]{:S(2)}, u32[]{:S(2)}) collective-permute-start(f32[72,128]{1,0:T(8,128)S(1)} %add.87), channel_id=1, source_target_pairs={{0,144},{1,145},{2,146},{3,147},{4,148},{5,149},{6,150},{7,151},{8... | collective-permute-start | bytes 110600 | tf_op jit(solution)/shard_map/ppermute | solution.py:660
  60.2 1.9 %collective-permute-done.7 = f32[72,128]{1,0:T(8,128)S(1)} collective-permute-done((f32[72,128]{1,0:T(8,128)S(1)}, f32[72,128]{1,0:T(8,128)S(1)}, u32[]{:S(2)}, u32[]{:S(2)}) %collective-permute-start.7) | collective-permute-done | bytes 36896 | tf_op jit(solution)/shard_map/ppermute | solution.py:660
  62.1 13.7 %all_to_all.11 = f32[16,72,128]{2,1,0:T(8,128)S(1)} all-to-all(f32[16,72,128]{2,1,0:T(8,128)S(1)} %broadcast_in_dim.15), channel_id=1, replica_groups={{0,1,2,3,4,5,6,7,8,9,10,11,12,13,14,15},{16,17,18,19,20,21,22,23,24,25,..., dimensions={0} | all-to-all | bytes 1179648 | tf_op jit(solution)/shard_map/all_to_all | solution.py:665
  75.9 1.7 %shard_map.144 = (bf16[544,256]{1,0:T(8,128)(2,1)S(1)}, bf16[544,256]{1,0:T(8,128)(2,1)S(1)}, f32[32,512]{1,0:T(8,128)S(1)}, f32[32,128]{1,0:T(8,128)S(1)}) custom-call(s32[2]{0:T(128)S(1)} %pad_add_fusion.where_ref, f32[1152,128]{1,0:T(8,128)S(1)} %bitcast.26, f32[4,40,128]{2,1,0:T(8,128)S(1)} %get-tuple-element.61.table_ref, ...), custom_call_target="tpu_custom_call" | custom-call | flops 1000000000 | bytes 2000000 | tf_op jit(solution)/shard_map/pallas_call | solution.py:781
  77.5 0.3 collective-permute-done.8.far_ref
  77.9 5.2 %shard_map.145 = (f32[1,512]{1,0:T(1,128)}, f32[32,512]{1,0:T(8,128)S(1)}, bf16[544,256]{1,0:T(8,128)(2,1)S(1)}, bf16[544,256]{1,0:T(8,128)(2,1)S(1)}, f32[3,512...) custom-call(s32[2]{0:T(128)S(1)} %pad_add_fusion.where_ref, ...), custom_call_target="tpu_custom_call" | custom-call | flops 5000000000 | bytes 4000000 | tf_op jit(solution)/shard_map/pallas_call | solution.py:791
  83.0 0.6 collective-permute-start.9
  83.6 7.9 %collective-permute-start.10 = (f32[3,3,256]{2,1,0:T(4,128)S(1)}, f32[3,3,256]{2,1,0:T(4,128)S(1)}, u32[]{:S(2)}, u32[]{:S(2)}) collective-permute-start(f32[3,3,256]{2,1,0:T(4,128)S(1)} %get-tuple-element.74), channel_id=1, source_target_pairs={{0,31},{1,2},{2,1},{3,4},{4,3},{5,6},{6,5},{7,8},{8,7},{9,10},{10,... | collective-permute-start | bytes 27656 | tf_op jit(solution)/shard_map/ppermute | solution.py:650
  91.5 3.4 %shard_map.146.base_ref = f32[3,512]{1,0:T(4,128)S(1)} custom-call(s32[2]{0:T(128)S(1)} %pad_add_fusion.where_ref, f32[3,512]{1,0:T(4,128)S(1)} %copy-done.1, bf16[544,256]{1,0:T(8,128)(2,1)S(1)} %get-tuple-element.75.nh_ref, bf16[544,256]{1,0:T(8,128)(2,1)S(1)} %get-tuple-element.76.nl_ref, bf16[544,256]{1,0:T(8,128)(2,1)S(1)} %get-tuple-element.77.fh_ref, ...), custom_call_target="tpu_custom_call" | custom-call | flops 5000000000 | bytes 4000000 | tf_op jit(solution)/shard_map/pallas_call | solution.py:829
  94.9 0.5 collective-permute-done.10
  95.4 0.9 collective-permute-start.12
  96.3 0.3 collective-permute-start.11
  96.5 3.8 %collective-permute-done.12.second_ref = f32[3,256]{1,0:T(4,128)S(1)} collective-permute-done((f32[3,256]{1,0:T(4,128)S(1)}, f32[3,256]{1,0:T(4,128)S(1)}, u32[]{:S(2)}, u32[]{:S(2)}) %collective-permute-start.12) | collective-permute-done | bytes 3104 | tf_op jit(solution)/shard_map/ppermute | solution.py:650
  100.3 0.9 shard_map.147
  (59 shorter events, 0.5 us)
Async XLA Ops:
  1.3 0.7 copy-start
  2.0 11.0 %copy-start.12 = (f32[8,128]{1,0:T(8,128)S(1)}, f32[8,128]{1,0:T(8,128)}, u32[]{:S(2)}) copy-start(f32[8,128]{1,0:T(8,128)} %embed_ref.1) | copy-start | bytes 12292
  2.1 14.7 %collective-permute-start.1 = (f32[4,256]{1,0:T(4,128)S(1)}, f32[4,256]{1,0:T(4,128)S(1)}, u32[]{:S(2)}, u32[]{:S(2)}) collective-permute-start(f32[4,256]{1,0:T(4,128)S(1)} %shard_map.140), channel_id=1, source_target_pairs={{0,1},{1,0},{2,3},{3,2},{4,5},{5,4},{6,7},{7,6},{8,9},{9,8},{10,11... | collective-permute-start | bytes 12296 | tf_op jit(solution)/shard_map/ppermute | solution.py:650
  2.2 14.6 %collective-permute-start = (f32[4,256]{1,0:T(4,128)S(1)}, f32[4,256]{1,0:T(4,128)S(1)}, u32[]{:S(2)}, u32[]{:S(2)}) collective-permute-start(f32[4,256]{1,0:T(4,128)S(1)} %shard_map.140), channel_id=1, source_target_pairs={{0,31},{1,2},{2,1},{3,4},{4,3},{5,6},{6,5},{7,8},{8,7},{9,10},{10,... | collective-permute-start | bytes 12296 | tf_op jit(solution)/shard_map/ppermute | solution.py:650
  13.0 0.7 copy-start.11
  13.0 0.7 copy-start.1
  13.7 0.8 copy-start.4
  14.6 7.3 %copy-start.7 = (s32[512,32]{0,1:T(8,128)S(1)}, s32[512,32]{0,1:T(8,128)}, u32[]{:S(2)}) copy-start(s32[512,32]{0,1:T(8,128)} %param.15) | copy-start | bytes 196612
  14.6 7.3 %copy-start.8 = (f32[128,128]{1,0:T(8,128)S(1)}, f32[128,128]{1,0:T(8,128)}, u32[]{:S(2)}) copy-start(f32[128,128]{1,0:T(8,128)} %scalar_ref.3) | copy-start | bytes 196612
  14.6 7.3 %copy-start.9 = (f32[128,128]{1,0:T(8,128)S(1)}, f32[128,128]{1,0:T(8,128)}, u32[]{:S(2)}) copy-start(f32[128,128]{1,0:T(8,128)} %vector_ref.3) | copy-start | bytes 196612
  14.6 7.3 %copy-start.10 = (f32[128,32]{0,1:T(8,128)S(1)}, f32[128,32]{0,1:T(8,128)}, u32[]{:S(2)}) copy-start(f32[128,32]{0,1:T(8,128)} %param.25) | copy-start | bytes 49156
  16.8 5.1 %copy-start.5 = (f32[128,128]{1,0:T(8,128)S(1)}, f32[128,128]{1,0:T(8,128)}, u32[]{:S(2)}) copy-start(f32[128,128]{1,0:T(8,128)} %hidden_ref.1) | copy-start | bytes 196612
  16.8 5.0 %collective-permute-start.3 = (f32[3,4,256]{2,1,0:T(4,128)S(1)}, f32[3,4,256]{2,1,0:T(4,128)S(1)}, u32[]{:S(2)}, u32[]{:S(2)}) collective-permute-start(f32[3,4,256]{2,1,0:T(4,128)S(1)} %pad_maximum_fusion.mid_ref), channel_id=1, source_target_pairs={{0,224},{32,64},{64,32},{96,128},{128,96},{160,192},{192,160},{224... | collective-permute-start | bytes 36872 | tf_op jit(solution)/shard_map/ppermute | solution.py:650
  17.7 4.1 %collective-permute-start.2 = (f32[3,4,256]{2,1,0:T(4,128)S(1)}, f32[3,4,256]{2,1,0:T(4,128)S(1)}, u32[]{:S(2)}, u32[]{:S(2)}) collective-permute-start(f32[3,4,256]{2,1,0:T(4,128)S(1)} %pad_maximum_fusion.mid_ref), channel_id=1, source_target_pairs={{0,32},{32,0},{64,96},{96,64},{128,160},{160,128},{192,224},{224,1... | collective-permute-start | bytes 36872 | tf_op jit(solution)/shard_map/ppermute | solution.py:650
  29.0 2.2 %copy-start.14 = (f32[7,32,512]{2,1,0:T(8,128)}, f32[7,32,512]{2,1,0:T(8,128)S(1)}, u32[]{:S(2)}) copy-start(f32[7,32,512]{2,1,0:T(8,128)S(1)} %get-tuple-element.70.geo_ref) | copy-start | bytes 1376260
  29.0 2.2 %copy-start.16 = (f32[128,512]{1,0:T(8,128)}, f32[128,512]{1,0:T(8,128)S(1)}, u32[]{:S(2)}) copy-start(f32[128,512]{1,0:T(8,128)S(1)} %get-tuple-element.67.hbar_ref) | copy-start | bytes 786436
  29.0 2.2 %copy-start.18 = (f32[128,512]{1,0:T(8,128)}, f32[128,512]{1,0:T(8,128)S(1)}, u32[]{:S(2)}) copy-start(f32[128,512]{1,0:T(8,128)S(1)} %get-tuple-element.68.slope_ref) | copy-start | bytes 786436
  29.0 2.2 %copy-start.20 = (f32[40,512]{1,0:T(8,128)}, f32[40,512]{1,0:T(8,128)S(1)}, u32[]{:S(2)}) copy-start(f32[40,512]{1,0:T(8,128)S(1)} %get-tuple-element.66.charge_ref) | copy-start | bytes 245764
  29.0 2.1 %collective-permute-start.4 = (f32[1152,128]{1,0:T(8,128)S(1)}, f32[1152,128]{1,0:T(8,128)S(1)}, u32[]{:S(2)}, u32[]{:S(2)}) collective-permute-start(f32[1152,128]{1,0:T(8,128)S(1)} %get-tuple-element.54), channel_id=1, source_target_pairs={{0,32},{32,0},{64,96},{96,64},{128,160},{160,128},{192,224},{224,1... | collective-permute-start | bytes 1769480 | tf_op jit(solution)/shard_map/ppermute | solution.py:650
  46.6 5.4 %copy-start.6 = (s32[3,4096]{1,0:T(4,128)S(1)}, s32[3,4096]{1,0:T(4,128)}, u32[]{:S(2)}) copy-start(s32[3,4096]{1,0:T(4,128)} %wave_ref) | copy-start | bytes 147460
  46.7 4.0 %collective-permute-start.5 = (f32[72,128]{1,0:T(8,128)S(1)}, f32[72,128]{1,0:T(8,128)S(1)}, u32[]{:S(2)}, u32[]{:S(2)}) collective-permute-start(f32[72,128]{1,0:T(8,128)S(1)} %fusion), channel_id=1, source_target_pairs={{0,64},{1,65},{2,66},{3,67},{4,68},{5,69},{6,70},{7,71},{8,72},{9,... | collective-permute-start | bytes 110600 | tf_op jit(solution)/shard_map/ppermute | solution.py:660
  50.7 4.9 %collective-permute-start.6 = (f32[72,128]{1,0:T(8,128)S(1)}, f32[72,128]{1,0:T(8,128)S(1)}, u32[]{:S(2)}, u32[]{:S(2)}) collective-permute-start(f32[72,128]{1,0:T(8,128)S(1)} %fusion.1), channel_id=1, source_target_pairs={{0,128},{1,129},{2,130},{3,131},{4,132},{5,133},{6,134},{7,135},{8... | collective-permute-start | bytes 110600 | tf_op jit(solution)/shard_map/ppermute | solution.py:660
  55.7 6.4 %collective-permute-start.7 = (f32[72,128]{1,0:T(8,128)S(1)}, f32[72,128]{1,0:T(8,128)S(1)}, u32[]{:S(2)}, u32[]{:S(2)}) collective-permute-start(f32[72,128]{1,0:T(8,128)S(1)} %add.87), channel_id=1, source_target_pairs={{0,144},{1,145},{2,146},{3,147},{4,148},{5,149},{6,150},{7,151},{8... | collective-permute-start | bytes 110600 | tf_op jit(solution)/shard_map/ppermute | solution.py:660
  75.8 2.0 %collective-permute-start.8 = (f32[1152,128]{1,0:T(8,128)S(1)}, f32[1152,128]{1,0:T(8,128)S(1)}, u32[]{:S(2)}, u32[]{:S(2)}) collective-permute-start(f32[1152,128]{1,0:T(8,128)S(1)} %bitcast.25), channel_id=1, source_target_pairs={{0,32},{32,0},{64,96},{96,64},{128,160},{160,128},{192,224},{224,1... | collective-permute-start | bytes 1769480 | tf_op jit(solution)/shard_map/ppermute | solution.py:650
  75.8 2.0 %copy-start.15 = (f32[7,32,512]{2,1,0:T(8,128)S(1)}, f32[7,32,512]{2,1,0:T(8,128)}, u32[]{:S(2)}) copy-start(f32[7,32,512]{2,1,0:T(8,128)} %copy-done.14) | copy-start | bytes 1376260
  75.8 2.0 %copy-start.17 = (f32[128,512]{1,0:T(8,128)S(1)}, f32[128,512]{1,0:T(8,128)}, u32[]{:S(2)}) copy-start(f32[128,512]{1,0:T(8,128)} %copy-done.16) | copy-start | bytes 786436
  75.8 2.0 %copy-start.19 = (f32[128,512]{1,0:T(8,128)S(1)}, f32[128,512]{1,0:T(8,128)}, u32[]{:S(2)}) copy-start(f32[128,512]{1,0:T(8,128)} %copy-done.18) | copy-start | bytes 786436
  75.9 2.0 %copy-start.21 = (f32[40,512]{1,0:T(8,128)S(1)}, f32[40,512]{1,0:T(8,128)}, u32[]{:S(2)}) copy-start(f32[40,512]{1,0:T(8,128)} %copy-done.20) | copy-start | bytes 245764
  83.0 11.9 %collective-permute-start.9 = (f32[3,3,256]{2,1,0:T(4,128)S(1)}, f32[3,3,256]{2,1,0:T(4,128)S(1)}, u32[]{:S(2)}, u32[]{:S(2)}) collective-permute-start(f32[3,3,256]{2,1,0:T(4,128)S(1)} %get-tuple-element.73), channel_id=1, source_target_pairs={{0,1},{1,0},{2,3},{3,2},{4,5},{5,4},{6,7},{7,6},{8,9},{9,8},{10,11... | collective-permute-start | bytes 27656 | tf_op jit(solution)/shard_map/ppermute | solution.py:650
  83.6 11.8 %collective-permute-start.10 = (f32[3,3,256]{2,1,0:T(4,128)S(1)}, f32[3,3,256]{2,1,0:T(4,128)S(1)}, u32[]{:S(2)}, u32[]{:S(2)}) collective-permute-start(f32[3,3,256]{2,1,0:T(4,128)S(1)} %get-tuple-element.74), channel_id=1, source_target_pairs={{0,31},{1,2},{2,1},{3,4},{4,3},{5,6},{6,5},{7,8},{8,7},{9,10},{10,... | collective-permute-start | bytes 27656 | tf_op jit(solution)/shard_map/ppermute | solution.py:650
  95.4 4.9 %collective-permute-start.12 = (f32[3,256]{1,0:T(4,128)S(1)}, f32[3,256]{1,0:T(4,128)S(1)}, u32[]{:S(2)}, u32[]{:S(2)}) collective-permute-start(f32[3,256]{1,0:T(4,128)S(1)} %get-tuple-element.86), channel_id=1, source_target_pairs={{0,224},{32,64},{64,32},{96,128},{128,96},{160,192},{192,160},{224... | collective-permute-start | bytes 9224 | tf_op jit(solution)/shard_map/ppermute | solution.py:650
  96.3 4.1 %collective-permute-start.11 = (f32[3,256]{1,0:T(4,128)S(1)}, f32[3,256]{1,0:T(4,128)S(1)}, u32[]{:S(2)}, u32[]{:S(2)}) collective-permute-start(f32[3,256]{1,0:T(4,128)S(1)} %get-tuple-element.87), channel_id=1, source_target_pairs={{0,32},{32,0},{64,96},{96,64},{128,160},{160,128},{192,224},{224,1... | collective-permute-start | bytes 9224 | tf_op jit(solution)/shard_map/ppermute | solution.py:650
  (3 other events, 2.0 us)

commit v4 on v3

--- a/solution.py
+++ b/solution.py
@@ -364,14 +364,14 @@
     high, low = qh_ref[...], ql_ref[...]
     core = where_ref[0] & 1
     for out, half in ((send_out, 1 - core), (keep_out, core)):
+        near, rest = (zy_ref[part, pl.ds(pl.multiple_of(256 * half, 256), 256), :] for part in range(2))
+        slabs = mm(high, near, NT) + (mm(low, near, NT) + mm(high, rest, NT))
         for n in range(2):
-            l = 2 * half + n
-            near, rest = (zy_ref[part, pl.ds(pl.multiple_of(128 * l, 128), 128), :] for part in range(2))
-            slab = mm(high, near, NT) + (mm(low, near, NT) + mm(high, rest, NT))
-            unit = unit_ref[l]
+            unit = unit_ref[2 * half + n]
             for k in range(XF):
                 at = SLAB * n + 32 * k
-                out[at : at + 32, :] = slab[32 * k : 32 * k + 32] + local * unit[k : k + 1]
+                value = slabs[32 * k : 32 * k + 32, 128 * n : 128 * n + 128]
+                out[at : at + 32, :] = value + local * unit[k : k + 1]
             out[UNIT_ROW + XROWS * n : UNIT_ROW + XROWS * (n + 1), :] = unit
         out[TOTAL_ROW:HALF, :] = jnp.where(iota((16, 128), 1) < 64, total[0:16], total[16:32])
 

time: 103 us -> 102 us (level)
  transfers between devices with their start and end apart: 13 -> 13, of which waited for: 8 -> 8; matrix products, arithmetic and copies ran while one was open for 0% -> 0% of each run, Pallas kernels for 8% -> 9%
where the time goes in v4:
time: 102 us; the launch traced here: 100 us
  blocking collectives  29.1 us (29%)
  starting transfers between devices  27.6 us (27%)
  Pallas kernels  20.9 us (20%)
  waiting for transfers between devices  18.5 us (18%)
  local copies, waits for them, and re-layouts  2.97 us (3%)
  between operations  1.09 us (1%)
    all_to_all x2, blocking collectives, across_plane(): lax.all_to_all(array, 'gy', 0, 0, tiled=True, axis_index_groups=planes)  29.1 us
    ppermute x10, starting transfers between devices, swapped(): return lax.ppermute(array, axis, pairs)  21.8 us
    ppermute x10, waiting for transfers between devices, swapped(): return lax.ppermute(array, axis, pairs)  10.4 us
    ppermute x3, waiting for transfers between devices, along_z(): return lax.ppermute(array, AXES, pairs)  8.16 us
    pallas_call x1, Pallas kernels, shards(): call(forward_kernel, [((40, atoms), F32), ((128, atoms), F32), ((128, ato...  6.23 us
    ppermute x3, starting transfers between devices, along_z(): return lax.ppermute(array, AXES, pairs)  5.89 us
    pallas_call x1, Pallas kernels, shards(): call(functools.partial(backward_kernel, atoms_all), [((1, atoms), F32), (...  5.15 us
    pallas_call x1, Pallas kernels, shards(): call(functools.partial(ewald_kernel, extents), [((3, atoms), F32)], [pltp...  3.41 us
  transfers between devices with their start and end apart: 13, of which 8 were waited for; matrix products, arithmetic and copies ran while one was open for 0% of the time, Pallas kernels for 9%

profile of v4, /device:TPU:0, one launch (start us, length us, event | category | flops | bytes accessed | tf_op | source)
XLA Modules:
  0.0 100.4 jit_solution(5310434865172375297)
XLA Ops:
  0.7 0.7 copy-done.3
  1.3 0.7 copy-done
  2.2 10.8 %collective-permute-start = (f32[4,256]{1,0:T(4,128)S(1)}, f32[4,256]{1,0:T(4,128)S(1)}, u32[]{:S(2)}, u32[]{:S(2)}) collective-permute-start(f32[4,256]{1,0:T(4,128)S(1)} %shard_map.140), channel_id=1, source_target_pairs={{0,31},{1,2},{2,1},{3,4},{4,3},{5,6},{6,5},{7,8},{8,7},{9,10},{10,... | collective-permute-start | bytes 12296 | tf_op jit(solution)/shard_map/ppermute | solution.py:650
  13.1 0.6 copy-done.11
  13.7 0.8 copy-done.4
  14.6 2.2 %shard_map.141 = (f32[24,512]{1,0:T(8,128)S(1)}, bf16[2,512,512]{2,1,0:T(8,128)(2,1)S(1)}, f32[4,24,128]{2,1,0:T(8,128)S(1)}, f32[2,128,64]{2,1,0:T(8,128)S(1)},...) custom-call(s32[2]{0:T(128)S(1)} %pad_add_fusion.where_ref, f32[3,512]{1,0:T(4,128)S(1)} %copy-done.1, ...), custom_call_target="tpu_custom_call" | custom-call | flops 1000000000 | bytes 2000000 | tf_op jit(solution)/shard_map/pallas_call | solution.py:699
  16.8 0.9 collective-permute-start.3
  17.7 0.3 collective-permute-start.2
  18.0 3.8 %collective-permute-done.3.second_ref = f32[3,4,256]{2,1,0:T(4,128)S(1)} collective-permute-done((f32[3,4,256]{2,1,0:T(4,128)S(1)}, f32[3,4,256]{2,1,0:T(4,128)S(1)}, u32[]{:S(2)}, u32[]{:S(2)}) %collective-permute-start.3) | collective-permute-done | bytes 12320 | tf_op jit(solution)/shard_map/ppermute | solution.py:650
  21.9 6.2 %shard_map.142 = (f32[40,512]{1,0:T(8,128)S(1)}, f32[128,512]{1,0:T(8,128)S(1)}, f32[128,512]{1,0:T(8,128)S(1)}, f32[3,128,512]{2,1,0:T(8,128)S(1)}, f32[7,32,51...) custom-call(s32[2]{0:T(128)S(1)} %pad_add_fusion.where_ref, f32[3,512]{1,0:T(4,128)S(1)} %copy-done.1, ...), custom_call_target="tpu_custom_call" | custom-call | flops 5000000000 | bytes 4000000 | tf_op jit(solution)/shard_map/pallas_call | solution.py:721
  28.1 0.1 collective-permute-start.4
  28.2 2.0 %collective-permute-done.4 = f32[1152,128]{1,0:T(8,128)S(1)} collective-permute-done((f32[1152,128]{1,0:T(8,128)S(1)}, f32[1152,128]{1,0:T(8,128)S(1)}, u32[]{:S(2)}, u32[]{:S(2)}) %collective-permute-start.4) | collective-permute-done | bytes 589856 | tf_op jit(solution)/shard_map/ppermute | solution.py:650
  30.3 15.4 %all_to_all.10 = f32[16,72,128]{2,1,0:T(8,128)S(1)} all-to-all(f32[16,72,128]{2,1,0:T(8,128)S(1)} %bitcast.37), channel_id=1, replica_groups={{0,1,2,3,4,5,6,7,8,9,10,11,12,13,14,15},{16,17,18,19,20,21,22,23,24,25,..., dimensions={0} | all-to-all | bytes 1179648 | tf_op jit(solution)/shard_map/all_to_all | solution.py:665
  45.8 0.1 collective-permute-start.5
  45.9 3.9 %collective-permute-done.5 = f32[72,128]{1,0:T(8,128)S(1)} collective-permute-done((f32[72,128]{1,0:T(8,128)S(1)}, f32[72,128]{1,0:T(8,128)S(1)}, u32[]{:S(2)}, u32[]{:S(2)}) %collective-permute-start.5) | collective-permute-done | bytes 36896 | tf_op jit(solution)/shard_map/ppermute | solution.py:660
  49.8 1.3 %collective-permute-start.6 = (f32[72,128]{1,0:T(8,128)S(1)}, f32[72,128]{1,0:T(8,128)S(1)}, u32[]{:S(2)}, u32[]{:S(2)}) collective-permute-start(f32[72,128]{1,0:T(8,128)S(1)} %fusion.1), channel_id=1, source_target_pairs={{0,128},{1,129},{2,130},{3,131},{4,132},{5,133},{6,134},{7,135},{8... | collective-permute-start | bytes 110600 | tf_op jit(solution)/shard_map/ppermute | solution.py:660
  51.2 1.3 %shard_map.143 = (f32[4,40,128]{2,1,0:T(8,128)S(1)}, f32[128,32]{1,0:T(8,128)S(1)}) custom-call(s32[3,4096]{1,0:T(4,128)S(1)} %copy-done.6, f32[32,128]{1,0:T(8,128)S(1)} %bitcast.35), custom_call_target="tpu_custom_call" | custom-call | flops 1000000000 | bytes 2000000 | tf_op jit(solution)/shard_map/pallas_call | solution.py:768
  52.5 2.3 %collective-permute-done.6 = f32[72,128]{1,0:T(8,128)S(1)} collective-permute-done((f32[72,128]{1,0:T(8,128)S(1)}, f32[72,128]{1,0:T(8,128)S(1)}, u32[]{:S(2)}, u32[]{:S(2)}) %collective-permute-start.6) | collective-permute-done | bytes 36896 | tf_op jit(solution)/shard_map/ppermute | solution.py:660
  54.8 4.5 %collective-permute-start.7 = (f32[72,128]{1,0:T(8,128)S(1)}, f32[72,128]{1,0:T(8,128)S(1)}, u32[]{:S(2)}, u32[]{:S(2)}) collective-permute-start(f32[72,128]{1,0:T(8,128)S(1)} %add.87), channel_id=1, source_target_pairs={{0,144},{1,145},{2,146},{3,147},{4,148},{5,149},{6,150},{7,151},{8... | collective-permute-start | bytes 110600 | tf_op jit(solution)/shard_map/ppermute | solution.py:660
  59.3 1.9 %collective-permute-done.7 = f32[72,128]{1,0:T(8,128)S(1)} collective-permute-done((f32[72,128]{1,0:T(8,128)S(1)}, f32[72,128]{1,0:T(8,128)S(1)}, u32[]{:S(2)}, u32[]{:S(2)}) %collective-permute-start.7) | collective-permute-done | bytes 36896 | tf_op jit(solution)/shard_map/ppermute | solution.py:660
  61.2 13.7 %all_to_all.11 = f32[16,72,128]{2,1,0:T(8,128)S(1)} all-to-all(f32[16,72,128]{2,1,0:T(8,128)S(1)} %broadcast_in_dim.15), channel_id=1, replica_groups={{0,1,2,3,4,5,6,7,8,9,10,11,12,13,14,15},{16,17,18,19,20,21,22,23,24,25,..., dimensions={0} | all-to-all | bytes 1179648 | tf_op jit(solution)/shard_map/all_to_all | solution.py:665
  75.0 1.7 %shard_map.144 = (bf16[544,256]{1,0:T(8,128)(2,1)S(1)}, bf16[544,256]{1,0:T(8,128)(2,1)S(1)}, f32[32,512]{1,0:T(8,128)S(1)}, f32[32,128]{1,0:T(8,128)S(1)}) custom-call(s32[2]{0:T(128)S(1)} %pad_add_fusion.where_ref, f32[1152,128]{1,0:T(8,128)S(1)} %bitcast.26, f32[4,40,128]{2,1,0:T(8,128)S(1)} %get-tuple-element.61.table_ref, ...), custom_call_target="tpu_custom_call" | custom-call | flops 1000000000 | bytes 2000000 | tf_op jit(solution)/shard_map/pallas_call | solution.py:781
  76.6 0.3 collective-permute-done.8.far_ref
  77.0 5.2 %shard_map.145 = (f32[1,512]{1,0:T(1,128)}, f32[32,512]{1,0:T(8,128)S(1)}, bf16[544,256]{1,0:T(8,128)(2,1)S(1)}, bf16[544,256]{1,0:T(8,128)(2,1)S(1)}, f32[3,512...) custom-call(s32[2]{0:T(128)S(1)} %pad_add_fusion.where_ref, ...), custom_call_target="tpu_custom_call" | custom-call | flops 5000000000 | bytes 4000000 | tf_op jit(solution)/shard_map/pallas_call | solution.py:791
  82.1 0.6 collective-permute-start.9
  82.7 7.9 %collective-permute-start.10 = (f32[3,3,256]{2,1,0:T(4,128)S(1)}, f32[3,3,256]{2,1,0:T(4,128)S(1)}, u32[]{:S(2)}, u32[]{:S(2)}) collective-permute-start(f32[3,3,256]{2,1,0:T(4,128)S(1)} %get-tuple-element.74), channel_id=1, source_target_pairs={{0,31},{1,2},{2,1},{3,4},{4,3},{5,6},{6,5},{7,8},{8,7},{9,10},{10,... | collective-permute-start | bytes 27656 | tf_op jit(solution)/shard_map/ppermute | solution.py:650
  90.6 3.4 %shard_map.146.base_ref = f32[3,512]{1,0:T(4,128)S(1)} custom-call(s32[2]{0:T(128)S(1)} %pad_add_fusion.where_ref, f32[3,512]{1,0:T(4,128)S(1)} %copy-done.1, bf16[544,256]{1,0:T(8,128)(2,1)S(1)} %get-tuple-element.75.nh_ref, bf16[544,256]{1,0:T(8,128)(2,1)S(1)} %get-tuple-element.76.nl_ref, bf16[544,256]{1,0:T(8,128)(2,1)S(1)} %get-tuple-element.77.fh_ref, ...), custom_call_target="tpu_custom_call" | custom-call | flops 5000000000 | bytes 4000000 | tf_op jit(solution)/shard_map/pallas_call | solution.py:829
  94.0 0.5 collective-permute-done.10
  94.5 0.9 collective-permute-start.12
  95.4 0.3 collective-permute-start.11
  95.7 3.8 %collective-permute-done.12.second_ref = f32[3,256]{1,0:T(4,128)S(1)} collective-permute-done((f32[3,256]{1,0:T(4,128)S(1)}, f32[3,256]{1,0:T(4,128)S(1)}, u32[]{:S(2)}, u32[]{:S(2)}) %collective-permute-start.12) | collective-permute-done | bytes 3104 | tf_op jit(solution)/shard_map/ppermute | solution.py:650
  99.4 0.9 shard_map.147
  (59 shorter events, 0.5 us)
Async XLA Ops:
  1.3 0.7 copy-start
  2.0 11.0 %copy-start.12 = (f32[8,128]{1,0:T(8,128)S(1)}, f32[8,128]{1,0:T(8,128)}, u32[]{:S(2)}) copy-start(f32[8,128]{1,0:T(8,128)} %embed_ref.1) | copy-start | bytes 12292
  2.1 14.7 %collective-permute-start.1 = (f32[4,256]{1,0:T(4,128)S(1)}, f32[4,256]{1,0:T(4,128)S(1)}, u32[]{:S(2)}, u32[]{:S(2)}) collective-permute-start(f32[4,256]{1,0:T(4,128)S(1)} %shard_map.140), channel_id=1, source_target_pairs={{0,1},{1,0},{2,3},{3,2},{4,5},{5,4},{6,7},{7,6},{8,9},{9,8},{10,11... | collective-permute-start | bytes 12296 | tf_op jit(solution)/shard_map/ppermute | solution.py:650
  2.2 14.6 %collective-permute-start = (f32[4,256]{1,0:T(4,128)S(1)}, f32[4,256]{1,0:T(4,128)S(1)}, u32[]{:S(2)}, u32[]{:S(2)}) collective-permute-start(f32[4,256]{1,0:T(4,128)S(1)} %shard_map.140), channel_id=1, source_target_pairs={{0,31},{1,2},{2,1},{3,4},{4,3},{5,6},{6,5},{7,8},{8,7},{9,10},{10,... | collective-permute-start | bytes 12296 | tf_op jit(solution)/shard_map/ppermute | solution.py:650
  13.0 0.7 copy-start.11
  13.0 0.7 copy-start.1
  13.7 0.8 copy-start.4
  14.6 7.3 %copy-start.7 = (s32[512,32]{0,1:T(8,128)S(1)}, s32[512,32]{0,1:T(8,128)}, u32[]{:S(2)}) copy-start(s32[512,32]{0,1:T(8,128)} %param.15) | copy-start | bytes 196612
  14.6 7.3 %copy-start.8 = (f32[128,128]{1,0:T(8,128)S(1)}, f32[128,128]{1,0:T(8,128)}, u32[]{:S(2)}) copy-start(f32[128,128]{1,0:T(8,128)} %scalar_ref.3) | copy-start | bytes 196612
  14.6 7.3 %copy-start.9 = (f32[128,128]{1,0:T(8,128)S(1)}, f32[128,128]{1,0:T(8,128)}, u32[]{:S(2)}) copy-start(f32[128,128]{1,0:T(8,128)} %vector_ref.3) | copy-start | bytes 196612
  14.6 7.3 %copy-start.10 = (f32[128,32]{0,1:T(8,128)S(1)}, f32[128,32]{0,1:T(8,128)}, u32[]{:S(2)}) copy-start(f32[128,32]{0,1:T(8,128)} %param.25) | copy-start | bytes 49156
  16.8 5.1 %copy-start.5 = (f32[128,128]{1,0:T(8,128)S(1)}, f32[128,128]{1,0:T(8,128)}, u32[]{:S(2)}) copy-start(f32[128,128]{1,0:T(8,128)} %hidden_ref.1) | copy-start | bytes 196612
  16.8 5.0 %collective-permute-start.3 = (f32[3,4,256]{2,1,0:T(4,128)S(1)}, f32[3,4,256]{2,1,0:T(4,128)S(1)}, u32[]{:S(2)}, u32[]{:S(2)}) collective-permute-start(f32[3,4,256]{2,1,0:T(4,128)S(1)} %pad_maximum_fusion.mid_ref), channel_id=1, source_target_pairs={{0,224},{32,64},{64,32},{96,128},{128,96},{160,192},{192,160},{224... | collective-permute-start | bytes 36872 | tf_op jit(solution)/shard_map/ppermute | solution.py:650
  17.7 4.1 %collective-permute-start.2 = (f32[3,4,256]{2,1,0:T(4,128)S(1)}, f32[3,4,256]{2,1,0:T(4,128)S(1)}, u32[]{:S(2)}, u32[]{:S(2)}) collective-permute-start(f32[3,4,256]{2,1,0:T(4,128)S(1)} %pad_maximum_fusion.mid_ref), channel_id=1, source_target_pairs={{0,32},{32,0},{64,96},{96,64},{128,160},{160,128},{192,224},{224,1... | collective-permute-start | bytes 36872 | tf_op jit(solution)/shard_map/ppermute | solution.py:650
  28.1 2.2 %copy-start.14 = (f32[7,32,512]{2,1,0:T(8,128)}, f32[7,32,512]{2,1,0:T(8,128)S(1)}, u32[]{:S(2)}) copy-start(f32[7,32,512]{2,1,0:T(8,128)S(1)} %get-tuple-element.70.geo_ref) | copy-start | bytes 1376260
  28.1 2.2 %copy-start.16 = (f32[128,512]{1,0:T(8,128)}, f32[128,512]{1,0:T(8,128)S(1)}, u32[]{:S(2)}) copy-start(f32[128,512]{1,0:T(8,128)S(1)} %get-tuple-element.67.hbar_ref) | copy-start | bytes 786436
  28.1 2.2 %copy-start.18 = (f32[128,512]{1,0:T(8,128)}, f32[128,512]{1,0:T(8,128)S(1)}, u32[]{:S(2)}) copy-start(f32[128,512]{1,0:T(8,128)S(1)} %get-tuple-element.68.slope_ref) | copy-start | bytes 786436
  28.1 2.2 %copy-start.20 = (f32[40,512]{1,0:T(8,128)}, f32[40,512]{1,0:T(8,128)S(1)}, u32[]{:S(2)}) copy-start(f32[40,512]{1,0:T(8,128)S(1)} %get-tuple-element.66.charge_ref) | copy-start | bytes 245764
  28.1 2.1 %collective-permute-start.4 = (f32[1152,128]{1,0:T(8,128)S(1)}, f32[1152,128]{1,0:T(8,128)S(1)}, u32[]{:S(2)}, u32[]{:S(2)}) collective-permute-start(f32[1152,128]{1,0:T(8,128)S(1)} %get-tuple-element.54), channel_id=1, source_target_pairs={{0,32},{32,0},{64,96},{96,64},{128,160},{160,128},{192,224},{224,1... | collective-permute-start | bytes 1769480 | tf_op jit(solution)/shard_map/ppermute | solution.py:650
  45.7 5.4 %copy-start.6 = (s32[3,4096]{1,0:T(4,128)S(1)}, s32[3,4096]{1,0:T(4,128)}, u32[]{:S(2)}) copy-start(s32[3,4096]{1,0:T(4,128)} %wave_ref) | copy-start | bytes 147460
  45.8 4.0 %collective-permute-start.5 = (f32[72,128]{1,0:T(8,128)S(1)}, f32[72,128]{1,0:T(8,128)S(1)}, u32[]{:S(2)}, u32[]{:S(2)}) collective-permute-start(f32[72,128]{1,0:T(8,128)S(1)} %fusion), channel_id=1, source_target_pairs={{0,64},{1,65},{2,66},{3,67},{4,68},{5,69},{6,70},{7,71},{8,72},{9,... | collective-permute-start | bytes 110600 | tf_op jit(solution)/shard_map/ppermute | solution.py:660
  49.8 4.9 %collective-permute-start.6 = (f32[72,128]{1,0:T(8,128)S(1)}, f32[72,128]{1,0:T(8,128)S(1)}, u32[]{:S(2)}, u32[]{:S(2)}) collective-permute-start(f32[72,128]{1,0:T(8,128)S(1)} %fusion.1), channel_id=1, source_target_pairs={{0,128},{1,129},{2,130},{3,131},{4,132},{5,133},{6,134},{7,135},{8... | collective-permute-start | bytes 110600 | tf_op jit(solution)/shard_map/ppermute | solution.py:660
  54.8 6.4 %collective-permute-start.7 = (f32[72,128]{1,0:T(8,128)S(1)}, f32[72,128]{1,0:T(8,128)S(1)}, u32[]{:S(2)}, u32[]{:S(2)}) collective-permute-start(f32[72,128]{1,0:T(8,128)S(1)} %add.87), channel_id=1, source_target_pairs={{0,144},{1,145},{2,146},{3,147},{4,148},{5,149},{6,150},{7,151},{8... | collective-permute-start | bytes 110600 | tf_op jit(solution)/shard_map/ppermute | solution.py:660
  74.9 2.0 %collective-permute-start.8 = (f32[1152,128]{1,0:T(8,128)S(1)}, f32[1152,128]{1,0:T(8,128)S(1)}, u32[]{:S(2)}, u32[]{:S(2)}) collective-permute-start(f32[1152,128]{1,0:T(8,128)S(1)} %bitcast.25), channel_id=1, source_target_pairs={{0,32},{32,0},{64,96},{96,64},{128,160},{160,128},{192,224},{224,1... | collective-permute-start | bytes 1769480 | tf_op jit(solution)/shard_map/ppermute | solution.py:650
  74.9 2.0 %copy-start.15 = (f32[7,32,512]{2,1,0:T(8,128)S(1)}, f32[7,32,512]{2,1,0:T(8,128)}, u32[]{:S(2)}) copy-start(f32[7,32,512]{2,1,0:T(8,128)} %copy-done.14) | copy-start | bytes 1376260
  74.9 2.0 %copy-start.17 = (f32[128,512]{1,0:T(8,128)S(1)}, f32[128,512]{1,0:T(8,128)}, u32[]{:S(2)}) copy-start(f32[128,512]{1,0:T(8,128)} %copy-done.16) | copy-start | bytes 786436
  74.9 2.0 %copy-start.19 = (f32[128,512]{1,0:T(8,128)S(1)}, f32[128,512]{1,0:T(8,128)}, u32[]{:S(2)}) copy-start(f32[128,512]{1,0:T(8,128)} %copy-done.18) | copy-start | bytes 786436
  75.0 2.0 %copy-start.21 = (f32[40,512]{1,0:T(8,128)S(1)}, f32[40,512]{1,0:T(8,128)}, u32[]{:S(2)}) copy-start(f32[40,512]{1,0:T(8,128)} %copy-done.20) | copy-start | bytes 245764
  82.1 11.9 %collective-permute-start.9 = (f32[3,3,256]{2,1,0:T(4,128)S(1)}, f32[3,3,256]{2,1,0:T(4,128)S(1)}, u32[]{:S(2)}, u32[]{:S(2)}) collective-permute-start(f32[3,3,256]{2,1,0:T(4,128)S(1)} %get-tuple-element.73), channel_id=1, source_target_pairs={{0,1},{1,0},{2,3},{3,2},{4,5},{5,4},{6,7},{7,6},{8,9},{9,8},{10,11... | collective-permute-start | bytes 27656 | tf_op jit(solution)/shard_map/ppermute | solution.py:650
  82.7 11.8 %collective-permute-start.10 = (f32[3,3,256]{2,1,0:T(4,128)S(1)}, f32[3,3,256]{2,1,0:T(4,128)S(1)}, u32[]{:S(2)}, u32[]{:S(2)}) collective-permute-start(f32[3,3,256]{2,1,0:T(4,128)S(1)} %get-tuple-element.74), channel_id=1, source_target_pairs={{0,31},{1,2},{2,1},{3,4},{4,3},{5,6},{6,5},{7,8},{8,7},{9,10},{10,... | collective-permute-start | bytes 27656 | tf_op jit(solution)/shard_map/ppermute | solution.py:650
  94.5 4.9 %collective-permute-start.12 = (f32[3,256]{1,0:T(4,128)S(1)}, f32[3,256]{1,0:T(4,128)S(1)}, u32[]{:S(2)}, u32[]{:S(2)}) collective-permute-start(f32[3,256]{1,0:T(4,128)S(1)} %get-tuple-element.86), channel_id=1, source_target_pairs={{0,224},{32,64},{64,32},{96,128},{128,96},{160,192},{192,160},{224... | collective-permute-start | bytes 9224 | tf_op jit(solution)/shard_map/ppermute | solution.py:650
  95.4 4.1 %collective-permute-start.11 = (f32[3,256]{1,0:T(4,128)S(1)}, f32[3,256]{1,0:T(4,128)S(1)}, u32[]{:S(2)}, u32[]{:S(2)}) collective-permute-start(f32[3,256]{1,0:T(4,128)S(1)} %get-tuple-element.87), channel_id=1, source_target_pairs={{0,32},{32,0},{64,96},{96,64},{128,160},{160,128},{192,224},{224,1... | collective-permute-start | bytes 9224 | tf_op jit(solution)/shard_map/ppermute | solution.py:650
  (3 other events, 2.0 us)

commit v5 on v4

--- a/solution.py
+++ b/solution.py
@@ -247,34 +247,24 @@
     slope_out,
     vsum_out,
     geo_out,
-    keep_out,
     send_out,
     tab_ref,
     moment_ref,
     qh_ref,
     ql_ref,
-    halo_ref,
-    sems,
 ):
     atoms = pos_ref.shape[1]
     tiles = atoms // 128
-    copies = [
-        pltpu.make_async_copy(ref, halo_ref.at[n], sems.at[n]) for n, ref in enumerate((mid_ref, first_ref, second_ref))
-    ]
-    for copy in copies:
-        copy.start()
     for c in range(3):
         for j in range(tiles):
             tab_ref[c, j : j + 1, :] = pos_ref[c : c + 1, pl.ds(128 * j, 128)]
     for j in range(tiles):
         tab_ref[3, j : j + 1, :] = species_ref[:, pl.ds(128 * j, 128)].astype(F32)
-    for copy in copies:
-        copy.wait()
     even = (where_ref[0] & 1) == 0
     for j in range(3):
-        first, second = halo_ref[1, j], halo_ref[2, j]
+        first, second = first_ref[j], second_ref[j]
         prev, after = jnp.where(even, second, first), jnp.where(even, first, second)
-        for i, block in enumerate((prev, halo_ref[0, j], after)):
+        for i, block in enumerate((prev, mid_ref[j], after)):
             shifts = (i - 1.0, j - 1.0, 0.0, 0.0)
             for c in range(4):
                 for h in range(2):
@@ -354,26 +344,32 @@
     charge_out[0:32, :] = charges
     charge_out[33:40, :] = jnp.zeros((7, atoms), F32)
 
+    half_sums(1 - (where_ref[0] & 1), charges, x_ref, zy_ref, unit_ref, send_out, qh_ref, ql_ref)
+
+
+def half_sums(half, charges, x_ref, zy_ref, unit_ref, out, qh_ref, ql_ref):
     total = jnp.sum(charges, axis=1, keepdims=True)
-    local = total * (1.0 / atoms)
+    local = total * (1.0 / charges.shape[1])
     centred = charges - local
     for k in range(XF):
         high, low = parts(centred * x_ref[k : k + 1, :])
         qh_ref[32 * k : 32 * k + 32, :] = high
         ql_ref[32 * k : 32 * k + 32, :] = low
     high, low = qh_ref[...], ql_ref[...]
-    core = where_ref[0] & 1
-    for out, half in ((send_out, 1 - core), (keep_out, core)):
-        near, rest = (zy_ref[part, pl.ds(pl.multiple_of(256 * half, 256), 256), :] for part in range(2))
-        slabs = mm(high, near, NT) + (mm(low, near, NT) + mm(high, rest, NT))
-        for n in range(2):
-            unit = unit_ref[2 * half + n]
-            for k in range(XF):
-                at = SLAB * n + 32 * k
-                value = slabs[32 * k : 32 * k + 32, 128 * n : 128 * n + 128]
-                out[at : at + 32, :] = value + local * unit[k : k + 1]
-            out[UNIT_ROW + XROWS * n : UNIT_ROW + XROWS * (n + 1), :] = unit
-        out[TOTAL_ROW:HALF, :] = jnp.where(iota((16, 128), 1) < 64, total[0:16], total[16:32])
+    near, rest = (zy_ref[part, pl.ds(pl.multiple_of(256 * half, 256), 256), :] for part in range(2))
+    slabs = mm(high, near, NT) + (mm(low, near, NT) + mm(high, rest, NT))
+    for n in range(2):
+        unit = unit_ref[2 * half + n]
+        for k in range(XF):
+            at = SLAB * n + 32 * k
+            value = slabs[32 * k : 32 * k + 32, 128 * n : 128 * n + 128]
+            out[at : at + 32, :] = value + local * unit[k : k + 1]
+        out[UNIT_ROW + XROWS * n : UNIT_ROW + XROWS * (n + 1), :] = unit
+    out[TOTAL_ROW:HALF, :] = jnp.where(iota((16, 128), 1) < 64, total[0:16], total[16:32])
+
+
+def keep_kernel(where_ref, charge_ref, x_ref, zy_ref, unit_ref, keep_out, qh_ref, ql_ref):
+    half_sums(where_ref[0] & 1, charge_ref[0:32, :], x_ref, zy_ref, unit_ref, keep_out, qh_ref, ql_ref)
 
 
 def quarters(x, which):
@@ -625,16 +621,9 @@
         total(c, x_ref, high_ref, low_ref)
 
 
-def finish_kernel(base_ref, mid_ref, first_ref, second_ref, ghost_ref, out_ref, back_ref, sems):
+def finish_kernel(base_ref, mid_ref, first_ref, second_ref, ghost_ref, out_ref):
     atoms = base_ref.shape[1]
-    copies = [
-        pltpu.make_async_copy(ref, back_ref.at[n], sems.at[n]) for n, ref in enumerate((mid_ref, first_ref, second_ref))
-    ]
-    for copy in copies:
-        copy.start()
-    for copy in copies:
-        copy.wait()
-    returned = back_ref[0] + back_ref[1] + back_ref[2]
+    returned = mid_ref[...] + first_ref[...] + second_ref[...]
     high = returned.astype(BF16).astype(F32)
     rest = returned - high
     middle = rest.astype(BF16).astype(F32)
@@ -665,9 +654,8 @@
     return lax.all_to_all(array, "gy", 0, 0, tiled=True, axis_index_groups=planes)
 
 
-def reduced(keep, send):
-    keep = keep + swapped(send, "gx", False)
-    got = across_plane(keep.reshape(16, -1, 128))
+def reduced(keep, got):
+    got = across_plane((keep + got).reshape(16, -1, 128))
     return sum((got[k] for k in range(1, 16)), got[0])
 
 
@@ -718,7 +706,7 @@
 
     nbr = neighbours.T
     charge_t = charge_weight.T
-    charge, hbar, slope, vsum, geo, keep, send = call(
+    charge, hbar, slope, vsum, geo, send = call(
         forward_kernel,
         [
             ((40, atoms), F32),
@@ -727,17 +715,14 @@
             ((3, 128, atoms), F32),
             ((7, 32, atoms), F32),
             ((HALF, 128), F32),
-            ((HALF, 128), F32),
         ],
         [
             pltpu.VMEM((4, 24, 128), F32),
             pltpu.VMEM((4, 64, atoms), F32),
             pltpu.VMEM((SLAB, atoms), BF16),
             pltpu.VMEM((SLAB, atoms), BF16),
-            pltpu.VMEM((3, 3, 4, 256), F32),
-            pltpu.SemaphoreType.DMA((3,)),
         ],
-        spaces="svvaaa" + "v" * 11,
+        spaces="s" + "v" * 16,
         vmem=16,
         flops=5 * 10**9,
         nbytes=4 * 10**6,
@@ -761,7 +746,18 @@
         unit,
     )
 
-    keep = reduced(keep, send)
+    got = swapped(send, "gx", False)
+    (keep,) = call(
+        keep_kernel,
+        [((HALF, 128), F32)],
+        [pltpu.VMEM((SLAB, atoms), BF16), pltpu.VMEM((SLAB, atoms), BF16)],
+        spaces="svvvv",
+        vmem=16,
+        flops=10**9,
+        nbytes=2 * 10**6,
+    )(where, charge, fx, zy, unit)
+    got, keep = lax.optimization_barrier((got, keep))
+    keep = reduced(keep, got)
     keep = keep + along_z(keep, 1)
     got = along_z(keep, 2)
     keep, waves_late, charge_late = lax.optimization_barrier((keep, wave_index, charge_t))
@@ -842,8 +838,7 @@
     (forces,) = call(
         finish_kernel,
         [((3, atoms), F32)],
-        [pltpu.VMEM((3, 3, 256), F32), pltpu.SemaphoreType.DMA((3,))],
-        spaces="vaaav",
+        spaces="vvvvv",
         vmem=4,
     )(base, column[1], first, second, ghosts)
     return forces, site[0]

time: 102 us -> 101 us (level)
  waiting for transfers between devices: 18.5 us -> 17.3 us
    ppermute x10, waiting for transfers between devices: 10.4 us -> 9.17 us  [swapped(): return lax.ppermute(array, axis, pairs)]
    pallas_call x1 -> x2, Pallas kernels: 0.85 us -> 2.01 us  [the longest x1 1.2 us: shards(): call(keep_kernel, [((HALF, 128), F32)], [pltpu.VMEM((SLAB, atoms), BF16),...]
    unnamed x44 -> x36, local copies, waits for them, and re-layouts: 2.93 us -> 2.92 us
  transfers between devices with their start and end apart: 13 -> 13, of which waited for: 8 -> 8; matrix products, arithmetic and copies ran while one was open for 0% -> 0% of each run, Pallas kernels for 9% -> 10%
where the time goes in v5:
time: 101 us; the launch traced here: 99.7 us
  blocking collectives  29.1 us (29%)
  starting transfers between devices  27.6 us (27%)
  Pallas kernels  21.5 us (21%)
  waiting for transfers between devices  17.3 us (17%)
  local copies, waits for them, and re-layouts  2.96 us (3%)
    all_to_all x2, blocking collectives, across_plane(): lax.all_to_all(array, 'gy', 0, 0, tiled=True, axis_index_groups=planes)  29.1 us
    ppermute x10, starting transfers between devices, swapped(): return lax.ppermute(array, axis, pairs)  21.8 us
    ppermute x10, waiting for transfers between devices, swapped(): return lax.ppermute(array, axis, pairs)  9.17 us
    ppermute x3, waiting for transfers between devices, along_z(): return lax.ppermute(array, AXES, pairs)  8.17 us
    ppermute x3, starting transfers between devices, along_z(): return lax.ppermute(array, AXES, pairs)  5.88 us
    pallas_call x1, Pallas kernels, shards(): call(forward_kernel, [((40, atoms), F32), ((128, atoms), F32), ((128, ato...  5.72 us
    pallas_call x1, Pallas kernels, shards(): call(functools.partial(backward_kernel, atoms_all), [((1, atoms), F32), (...  5.14 us
    pallas_call x1, Pallas kernels, shards(): call(functools.partial(ewald_kernel, extents), [((3, atoms), F32)], [pltp...  3.41 us
  transfers between devices with their start and end apart: 13, of which 8 were waited for; matrix products, arithmetic and copies ran while one was open for 0% of the time, Pallas kernels for 10%

profile of v5, /device:TPU:0, one launch (start us, length us, event | category | flops | bytes accessed | tf_op | source)
XLA Modules:
  0.0 99.7 jit_solution(466909724851120539)
XLA Ops:
  0.7 0.7 copy-done.3
  1.3 0.7 copy-done
  2.2 10.8 %collective-permute-start = (f32[4,256]{1,0:T(4,128)S(1)}, f32[4,256]{1,0:T(4,128)S(1)}, u32[]{:S(2)}, u32[]{:S(2)}) collective-permute-start(f32[4,256]{1,0:T(4,128)S(1)} %shard_map.140), channel_id=1, source_target_pairs={{0,31},{1,2},{2,1},{3,4},{4,3},{5,6},{6,5},{7,8},{8,7},{9,10},{10,... | collective-permute-start | bytes 12296 | tf_op jit(solution)/shard_map/ppermute | solution.py:639
  13.1 0.6 copy-done.11
  13.7 0.8 copy-done.4
  14.6 2.2 %shard_map.141 = (f32[24,512]{1,0:T(8,128)S(1)}, bf16[2,512,512]{2,1,0:T(8,128)(2,1)S(1)}, f32[4,24,128]{2,1,0:T(8,128)S(1)}, f32[2,128,64]{2,1,0:T(8,128)S(1)},...) custom-call(s32[2]{0:T(128)S(1)} %pad_add_fusion.where_ref, f32[3,512]{1,0:T(4,128)S(1)} %copy-done.1, ...), custom_call_target="tpu_custom_call" | custom-call | flops 1000000000 | bytes 2000000 | tf_op jit(solution)/shard_map/pallas_call | solution.py:687
  16.8 0.9 collective-permute-start.3
  17.7 0.3 collective-permute-start.2
  18.0 3.8 %collective-permute-done.3.second_ref = f32[3,4,256]{2,1,0:T(4,128)S(1)} collective-permute-done((f32[3,4,256]{2,1,0:T(4,128)S(1)}, f32[3,4,256]{2,1,0:T(4,128)S(1)}, u32[]{:S(2)}, u32[]{:S(2)}) %collective-permute-start.3) | collective-permute-done | bytes 12320 | tf_op jit(solution)/shard_map/ppermute | solution.py:639
  21.9 5.7 %shard_map.142 = (f32[40,512]{1,0:T(8,128)S(1)}, f32[128,512]{1,0:T(8,128)S(1)}, f32[128,512]{1,0:T(8,128)S(1)}, f32[3,128,512]{2,1,0:T(8,128)S(1)}, f32[7,32,512]{2,1,0:T(8,128)S(1)}, /*index=5*/f32[1152,128]{1,0:T(8,128)S(1)}) custom-call(s32[2]{0:T(128)S(1)} %pad_add_fusion.where_ref, f32[3,512]{1,0:T(4,128)S(1)} %copy-done.1, s32[1,512]{1,0:T(1,128)S(1)} %bitcast.31, ...), custom_call_target="tpu_custom_call" | custom-call | flops 5000000000 | bytes 4000000 | tf_op jit(solution)/shard_map/pallas_call | solution.py:709
  27.7 1.2 %shard_map.143 = f32[1152,128]{1,0:T(8,128)S(1)} custom-call(s32[2]{0:T(128)S(1)} %pad_add_fusion.where_ref, f32[40,512]{1,0:T(8,128)S(1)} %get-tuple-element.55.charge_ref, f32[24,512]{1,0:T(8,128)S(1)} %get-tuple-element.51.x_ref, bf16[2,512,512]{2,1,0:T(8,128)(2,1)S(1)} %get-tuple-element.52.zy_ref, f32[4,24,128]{2,1,0:T(8,128)S(1)} %get-tuple-element.53.unit_ref), custom_call_target="tpu_custom_call" | custom-call | flops 1000000000 | bytes 2000000 | tf_op jit(solution)/shard_map/pallas_call | solution.py:750
  28.9 0.8 collective-permute-done.4
  29.8 15.4 %all_to_all.10 = f32[16,72,128]{2,1,0:T(8,128)S(1)} all-to-all(f32[16,72,128]{2,1,0:T(8,128)S(1)} %bitcast.37), channel_id=1, replica_groups={{0,1,2,3,4,5,6,7,8,9,10,11,12,13,14,15},{16,17,18,19,20,21,22,23,24,25,..., dimensions={0} | all-to-all | bytes 1179648 | tf_op jit(solution)/shard_map/all_to_all | solution.py:654
  45.2 0.1 collective-permute-start.5
  45.3 3.9 %collective-permute-done.5 = f32[72,128]{1,0:T(8,128)S(1)} collective-permute-done((f32[72,128]{1,0:T(8,128)S(1)}, f32[72,128]{1,0:T(8,128)S(1)}, u32[]{:S(2)}, u32[]{:S(2)}) %collective-permute-start.5) | collective-permute-done | bytes 36896 | tf_op jit(solution)/shard_map/ppermute | solution.py:649
  49.3 1.3 %collective-permute-start.6 = (f32[72,128]{1,0:T(8,128)S(1)}, f32[72,128]{1,0:T(8,128)S(1)}, u32[]{:S(2)}, u32[]{:S(2)}) collective-permute-start(f32[72,128]{1,0:T(8,128)S(1)} %fusion.1), channel_id=1, source_target_pairs={{0,128},{1,129},{2,130},{3,131},{4,132},{5,133},{6,134},{7,135},{8... | collective-permute-start | bytes 110600 | tf_op jit(solution)/shard_map/ppermute | solution.py:649
  50.6 1.3 %shard_map.144 = (f32[4,40,128]{2,1,0:T(8,128)S(1)}, f32[128,32]{1,0:T(8,128)S(1)}) custom-call(s32[3,4096]{1,0:T(4,128)S(1)} %copy-done.6, f32[32,128]{1,0:T(8,128)S(1)} %bitcast.35), custom_call_target="tpu_custom_call" | custom-call | flops 1000000000 | bytes 2000000 | tf_op jit(solution)/shard_map/pallas_call | solution.py:764
  51.9 2.3 %collective-permute-done.6 = f32[72,128]{1,0:T(8,128)S(1)} collective-permute-done((f32[72,128]{1,0:T(8,128)S(1)}, f32[72,128]{1,0:T(8,128)S(1)}, u32[]{:S(2)}, u32[]{:S(2)}) %collective-permute-start.6) | collective-permute-done | bytes 36896 | tf_op jit(solution)/shard_map/ppermute | solution.py:649
  54.2 4.4 %collective-permute-start.7 = (f32[72,128]{1,0:T(8,128)S(1)}, f32[72,128]{1,0:T(8,128)S(1)}, u32[]{:S(2)}, u32[]{:S(2)}) collective-permute-start(f32[72,128]{1,0:T(8,128)S(1)} %add.87), channel_id=1, source_target_pairs={{0,144},{1,145},{2,146},{3,147},{4,148},{5,149},{6,150},{7,151},{8... | collective-permute-start | bytes 110600 | tf_op jit(solution)/shard_map/ppermute | solution.py:649
  58.7 1.9 %collective-permute-done.7 = f32[72,128]{1,0:T(8,128)S(1)} collective-permute-done((f32[72,128]{1,0:T(8,128)S(1)}, f32[72,128]{1,0:T(8,128)S(1)}, u32[]{:S(2)}, u32[]{:S(2)}) %collective-permute-start.7) | collective-permute-done | bytes 36896 | tf_op jit(solution)/shard_map/ppermute | solution.py:649
  60.7 13.7 %all_to_all.11 = f32[16,72,128]{2,1,0:T(8,128)S(1)} all-to-all(f32[16,72,128]{2,1,0:T(8,128)S(1)} %broadcast_in_dim.15), channel_id=1, replica_groups={{0,1,2,3,4,5,6,7,8,9,10,11,12,13,14,15},{16,17,18,19,20,21,22,23,24,25,..., dimensions={0} | all-to-all | bytes 1179648 | tf_op jit(solution)/shard_map/all_to_all | solution.py:654
  74.4 1.7 %shard_map.145 = (bf16[544,256]{1,0:T(8,128)(2,1)S(1)}, bf16[544,256]{1,0:T(8,128)(2,1)S(1)}, f32[32,512]{1,0:T(8,128)S(1)}, f32[32,128]{1,0:T(8,128)S(1)}) custom-call(s32[2]{0:T(128)S(1)} %pad_add_fusion.where_ref, f32[1152,128]{1,0:T(8,128)S(1)} %bitcast.26, f32[4,40,128]{2,1,0:T(8,128)S(1)} %get-tuple-element.64.table_ref, ...), custom_call_target="tpu_custom_call" | custom-call | flops 1000000000 | bytes 2000000 | tf_op jit(solution)/shard_map/pallas_call | solution.py:777
  76.1 0.3 collective-permute-done.8.far_ref
  76.4 5.1 %shard_map.146 = (f32[1,512]{1,0:T(1,128)}, f32[32,512]{1,0:T(8,128)S(1)}, bf16[544,256]{1,0:T(8,128)(2,1)S(1)}, bf16[544,256]{1,0:T(8,128)(2,1)S(1)}, f32[3,512...) custom-call(s32[2]{0:T(128)S(1)} %pad_add_fusion.where_ref, ...), custom_call_target="tpu_custom_call" | custom-call | flops 5000000000 | bytes 4000000 | tf_op jit(solution)/shard_map/pallas_call | solution.py:787
  81.5 0.6 collective-permute-start.9
  82.1 7.9 %collective-permute-start.10 = (f32[3,3,256]{2,1,0:T(4,128)S(1)}, f32[3,3,256]{2,1,0:T(4,128)S(1)}, u32[]{:S(2)}, u32[]{:S(2)}) collective-permute-start(f32[3,3,256]{2,1,0:T(4,128)S(1)} %get-tuple-element.76), channel_id=1, source_target_pairs={{0,31},{1,2},{2,1},{3,4},{4,3},{5,6},{6,5},{7,8},{8,7},{9,10},{10,... | collective-permute-start | bytes 27656 | tf_op jit(solution)/shard_map/ppermute | solution.py:639
  90.0 3.4 %shard_map.147.base_ref = f32[3,512]{1,0:T(4,128)S(1)} custom-call(s32[2]{0:T(128)S(1)} %pad_add_fusion.where_ref, f32[3,512]{1,0:T(4,128)S(1)} %copy-done.1, bf16[544,256]{1,0:T(8,128)(2,1)S(1)} %get-tuple-element.77.nh_ref, bf16[544,256]{1,0:T(8,128)(2,1)S(1)} %get-tuple-element.78.nl_ref, bf16[544,256]{1,0:T(8,128)(2,1)S(1)} %get-tuple-element.79.fh_ref, ...), custom_call_target="tpu_custom_call" | custom-call | flops 5000000000 | bytes 4000000 | tf_op jit(solution)/shard_map/pallas_call | solution.py:825
  93.4 0.5 collective-permute-done.10
  93.9 0.9 collective-permute-start.12
  94.8 0.3 collective-permute-start.11
  95.1 3.8 %collective-permute-done.12.second_ref = f32[3,256]{1,0:T(4,128)S(1)} collective-permute-done((f32[3,256]{1,0:T(4,128)S(1)}, f32[3,256]{1,0:T(4,128)S(1)}, u32[]{:S(2)}, u32[]{:S(2)}) %collective-permute-start.12) | collective-permute-done | bytes 3104 | tf_op jit(solution)/shard_map/ppermute | solution.py:639
  98.9 0.8 shard_map.148
  (52 shorter events, 0.6 us)
Async XLA Ops:
  0.6 0.7 copy-start.3
  0.6 0.7 copy-start.2
  1.3 0.7 copy-start
  2.0 11.0 %copy-start.12 = (f32[8,128]{1,0:T(8,128)S(1)}, f32[8,128]{1,0:T(8,128)}, u32[]{:S(2)}) copy-start(f32[8,128]{1,0:T(8,128)} %embed_ref.1) | copy-start | bytes 12292
  2.1 14.7 %collective-permute-start.1 = (f32[4,256]{1,0:T(4,128)S(1)}, f32[4,256]{1,0:T(4,128)S(1)}, u32[]{:S(2)}, u32[]{:S(2)}) collective-permute-start(f32[4,256]{1,0:T(4,128)S(1)} %shard_map.140), channel_id=1, source_target_pairs={{0,1},{1,0},{2,3},{3,2},{4,5},{5,4},{6,7},{7,6},{8,9},{9,8},{10,11... | collective-permute-start | bytes 12296 | tf_op jit(solution)/shard_map/ppermute | solution.py:639
  2.2 14.6 %collective-permute-start = (f32[4,256]{1,0:T(4,128)S(1)}, f32[4,256]{1,0:T(4,128)S(1)}, u32[]{:S(2)}, u32[]{:S(2)}) collective-permute-start(f32[4,256]{1,0:T(4,128)S(1)} %shard_map.140), channel_id=1, source_target_pairs={{0,31},{1,2},{2,1},{3,4},{4,3},{5,6},{6,5},{7,8},{8,7},{9,10},{10,... | collective-permute-start | bytes 12296 | tf_op jit(solution)/shard_map/ppermute | solution.py:639
  13.0 0.7 copy-start.11
  13.0 0.7 copy-start.1
  13.1 0.7 copy-start.13
  13.7 0.8 copy-start.4
  14.6 7.3 %copy-start.7 = (s32[512,32]{0,1:T(8,128)S(1)}, s32[512,32]{0,1:T(8,128)}, u32[]{:S(2)}) copy-start(s32[512,32]{0,1:T(8,128)} %param.15) | copy-start | bytes 196612
  14.6 7.3 %copy-start.8 = (f32[128,128]{1,0:T(8,128)S(1)}, f32[128,128]{1,0:T(8,128)}, u32[]{:S(2)}) copy-start(f32[128,128]{1,0:T(8,128)} %scalar_ref.3) | copy-start | bytes 196612
  14.6 7.3 %copy-start.9 = (f32[128,128]{1,0:T(8,128)S(1)}, f32[128,128]{1,0:T(8,128)}, u32[]{:S(2)}) copy-start(f32[128,128]{1,0:T(8,128)} %vector_ref.3) | copy-start | bytes 196612
  14.6 7.3 %copy-start.10 = (f32[128,32]{0,1:T(8,128)S(1)}, f32[128,32]{0,1:T(8,128)}, u32[]{:S(2)}) copy-start(f32[128,32]{0,1:T(8,128)} %param.25) | copy-start | bytes 49156
  16.8 5.1 %copy-start.5 = (f32[128,128]{1,0:T(8,128)S(1)}, f32[128,128]{1,0:T(8,128)}, u32[]{:S(2)}) copy-start(f32[128,128]{1,0:T(8,128)} %hidden_ref.1) | copy-start | bytes 196612
  16.8 5.0 %collective-permute-start.3 = (f32[3,4,256]{2,1,0:T(4,128)S(1)}, f32[3,4,256]{2,1,0:T(4,128)S(1)}, u32[]{:S(2)}, u32[]{:S(2)}) collective-permute-start(f32[3,4,256]{2,1,0:T(4,128)S(1)} %pad_maximum_fusion.mid_ref), channel_id=1, source_target_pairs={{0,224},{32,64},{64,32},{96,128},{128,96},{160,192},{192,160},{224... | collective-permute-start | bytes 36872 | tf_op jit(solution)/shard_map/ppermute | solution.py:639
  17.7 4.1 %collective-permute-start.2 = (f32[3,4,256]{2,1,0:T(4,128)S(1)}, f32[3,4,256]{2,1,0:T(4,128)S(1)}, u32[]{:S(2)}, u32[]{:S(2)}) collective-permute-start(f32[3,4,256]{2,1,0:T(4,128)S(1)} %pad_maximum_fusion.mid_ref), channel_id=1, source_target_pairs={{0,32},{32,0},{64,96},{96,64},{128,160},{160,128},{192,224},{224,1... | collective-permute-start | bytes 36872 | tf_op jit(solution)/shard_map/ppermute | solution.py:639
  27.6 1.3 %copy-start.14 = (f32[3,128,512]{2,1,0:T(8,128)}, f32[3,128,512]{2,1,0:T(8,128)S(1)}, u32[]{:S(2)}) copy-start(f32[3,128,512]{2,1,0:T(8,128)S(1)} %get-tuple-element.71.vsum_ref) | copy-start | bytes 2359300
  27.6 1.3 %copy-start.16 = (f32[128,512]{1,0:T(8,128)}, f32[128,512]{1,0:T(8,128)S(1)}, u32[]{:S(2)}) copy-start(f32[128,512]{1,0:T(8,128)S(1)} %get-tuple-element.70.slope_ref) | copy-start | bytes 786436
  27.6 2.1 %collective-permute-start.4 = (f32[1152,128]{1,0:T(8,128)S(1)}, f32[1152,128]{1,0:T(8,128)S(1)}, u32[]{:S(2)}, u32[]{:S(2)}) collective-permute-start(f32[1152,128]{1,0:T(8,128)S(1)} %get-tuple-element.54), channel_id=1, source_target_pairs={{0,32},{32,0},{64,96},{96,64},{128,160},{160,128},{192,224},{224,1... | collective-permute-start | bytes 1769480 | tf_op jit(solution)/shard_map/ppermute | solution.py:639
  45.2 5.4 %copy-start.6 = (s32[3,4096]{1,0:T(4,128)S(1)}, s32[3,4096]{1,0:T(4,128)}, u32[]{:S(2)}) copy-start(s32[3,4096]{1,0:T(4,128)} %wave_ref) | copy-start | bytes 147460
  45.2 4.0 %collective-permute-start.5 = (f32[72,128]{1,0:T(8,128)S(1)}, f32[72,128]{1,0:T(8,128)S(1)}, u32[]{:S(2)}, u32[]{:S(2)}) collective-permute-start(f32[72,128]{1,0:T(8,128)S(1)} %fusion), channel_id=1, source_target_pairs={{0,64},{1,65},{2,66},{3,67},{4,68},{5,69},{6,70},{7,71},{8,72},{9,... | collective-permute-start | bytes 110600 | tf_op jit(solution)/shard_map/ppermute | solution.py:649
  49.3 4.9 %collective-permute-start.6 = (f32[72,128]{1,0:T(8,128)S(1)}, f32[72,128]{1,0:T(8,128)S(1)}, u32[]{:S(2)}, u32[]{:S(2)}) collective-permute-start(f32[72,128]{1,0:T(8,128)S(1)} %fusion.1), channel_id=1, source_target_pairs={{0,128},{1,129},{2,130},{3,131},{4,132},{5,133},{6,134},{7,135},{8... | collective-permute-start | bytes 110600 | tf_op jit(solution)/shard_map/ppermute | solution.py:649
  54.2 6.4 %collective-permute-start.7 = (f32[72,128]{1,0:T(8,128)S(1)}, f32[72,128]{1,0:T(8,128)S(1)}, u32[]{:S(2)}, u32[]{:S(2)}) collective-permute-start(f32[72,128]{1,0:T(8,128)S(1)} %add.87), channel_id=1, source_target_pairs={{0,144},{1,145},{2,146},{3,147},{4,148},{5,149},{6,150},{7,151},{8... | collective-permute-start | bytes 110600 | tf_op jit(solution)/shard_map/ppermute | solution.py:649
  74.4 2.0 %collective-permute-start.8 = (f32[1152,128]{1,0:T(8,128)S(1)}, f32[1152,128]{1,0:T(8,128)S(1)}, u32[]{:S(2)}, u32[]{:S(2)}) collective-permute-start(f32[1152,128]{1,0:T(8,128)S(1)} %bitcast.25), channel_id=1, source_target_pairs={{0,32},{32,0},{64,96},{96,64},{128,160},{160,128},{192,224},{224,1... | collective-permute-start | bytes 1769480 | tf_op jit(solution)/shard_map/ppermute | solution.py:639
  74.4 2.0 %copy-start.15 = (f32[3,128,512]{2,1,0:T(8,128)S(1)}, f32[3,128,512]{2,1,0:T(8,128)}, u32[]{:S(2)}) copy-start(f32[3,128,512]{2,1,0:T(8,128)} %copy-done.14) | copy-start | bytes 2359300
  74.4 2.0 %copy-start.17 = (f32[128,512]{1,0:T(8,128)S(1)}, f32[128,512]{1,0:T(8,128)}, u32[]{:S(2)}) copy-start(f32[128,512]{1,0:T(8,128)} %copy-done.16) | copy-start | bytes 786436
  81.5 11.9 %collective-permute-start.9 = (f32[3,3,256]{2,1,0:T(4,128)S(1)}, f32[3,3,256]{2,1,0:T(4,128)S(1)}, u32[]{:S(2)}, u32[]{:S(2)}) collective-permute-start(f32[3,3,256]{2,1,0:T(4,128)S(1)} %get-tuple-element.75), channel_id=1, source_target_pairs={{0,1},{1,0},{2,3},{3,2},{4,5},{5,4},{6,7},{7,6},{8,9},{9,8},{10,11... | collective-permute-start | bytes 27656 | tf_op jit(solution)/shard_map/ppermute | solution.py:639
  82.1 11.8 %collective-permute-start.10 = (f32[3,3,256]{2,1,0:T(4,128)S(1)}, f32[3,3,256]{2,1,0:T(4,128)S(1)}, u32[]{:S(2)}, u32[]{:S(2)}) collective-permute-start(f32[3,3,256]{2,1,0:T(4,128)S(1)} %get-tuple-element.76), channel_id=1, source_target_pairs={{0,31},{1,2},{2,1},{3,4},{4,3},{5,6},{6,5},{7,8},{8,7},{9,10},{10,... | collective-permute-start | bytes 27656 | tf_op jit(solution)/shard_map/ppermute | solution.py:639
  93.9 4.9 %collective-permute-start.12 = (f32[3,256]{1,0:T(4,128)S(1)}, f32[3,256]{1,0:T(4,128)S(1)}, u32[]{:S(2)}, u32[]{:S(2)}) collective-permute-start(f32[3,256]{1,0:T(4,128)S(1)} %get-tuple-element.88), channel_id=1, source_target_pairs={{0,224},{32,64},{64,32},{96,128},{128,96},{160,192},{192,160},{224... | collective-permute-start | bytes 9224 | tf_op jit(solution)/shard_map/ppermute | solution.py:639
  94.8 4.1 %collective-permute-start.11 = (f32[3,256]{1,0:T(4,128)S(1)}, f32[3,256]{1,0:T(4,128)S(1)}, u32[]{:S(2)}, u32[]{:S(2)}) collective-permute-start(f32[3,256]{1,0:T(4,128)S(1)} %get-tuple-element.89), channel_id=1, source_target_pairs={{0,32},{32,0},{64,96},{96,64},{128,160},{160,128},{192,224},{224,1... | collective-permute-start | bytes 9224 | tf_op jit(solution)/shard_map/ppermute | solution.py:639
